TPU v7x, 32 devices: a whole 2x2x4 slice. The times are simulated.
32 devices in a mesh: dp: 4 (over y, core), expert: 2 (over x), tensor: 4 (over z).
Axes of the slice: x: 2, y: 2, z: 4, core: 2. Of those that a mesh axis runs over, the one named last changes fastest.
Arguments:
- tokens: bfloat16 [1024, 2048], P(('dp', 'expert')), may hold values from -6 to 6
- cotangent: bfloat16 [1024, 2048], P(('dp', 'expert')), may hold values from -6 to 6
- expert_ids: int32 [1024, 1], P(('dp', 'expert')), may hold values from 0 to 31; in each aligned block of 128 rows (0 to 127, 128 to 255, ...) at most 8 rows name the same one
- gate_weight: bfloat16 [32, 2048, 1408], P('expert', 'dp', 'tensor'), may hold values from -0.125 to 0.125
- up_weight: bfloat16 [32, 2048, 1408], P('expert', 'dp', 'tensor'), may hold values from -0.125 to 0.125
- down_weight: bfloat16 [32, 2048, 1408], P('expert', 'dp', 'tensor'), may hold values from -0.15625 to 0.15625
Outputs:
- grad_tokens: bfloat16 [1024, 2048], P(('dp', 'expert'), 'tensor')
- grad_gate: bfloat16 [32, 2048, 1408], P('expert', 'dp', 'tensor')
- grad_up: bfloat16 [32, 2048, 1408], P('expert', 'dp', 'tensor')
Inputs may be any that keep to these rules, and one draw needn't show every extreme that they name: `expert_ids`: among the 128 tokens of one block no expert id occurs more than 8 times, and in every draw some block holds some id exactly 8 times.
All inputs are finite; a program needn't handle non-finite values.
Results may differ from a plain program's by a relative error of at most 0.013.
Values may be sent and summed in bfloat16 or wider, within the bound.
No kernel may reach another device: no remote copies, remote signals or barrier semaphores. Data moves between devices by JAX's collectives and lax.ppermute only.
A program may use at most 192 MiB of HBM per device.

v0:
```python
import functools

import jax
import jax.numpy as jnp
from jax import lax
from jax.experimental import pallas as pl
from jax.experimental.pallas import tpu as pltpu
from jax.sharding import PartitionSpec as P

CAP = 8
META = 16
F32 = jnp.float32
BF16 = jnp.bfloat16
MIB = 1024 * 1024
PLACE_COST = 1 << 34


def swap(value, axis, count, bit):
    return lax.ppermute(value, axis, [(i, i ^ bit) for i in range(count)])


def whole_spec(shape):
    return pl.BlockSpec(shape, lambda *_: (0,) * len(shape))


def params(mib=16):
    return pltpu.CompilerParams(vmem_limit_bytes=mib * MIB)


def placer_of(row, slot_count):
    every = lax.broadcasted_iota(jnp.int32, (slot_count, row.shape[1]), 0)
    return (every == row).astype(F32).astype(BF16)


def place_kernel(first, rows, mine, others, *refs):
    n_dp = len(mine)
    other = []
    for group in others:
        other += [group] if len(group.shape) == 2 else [group.at[i] for i in range(group.shape[0])]
    if first:
        placed, lines = refs[-2:]
    else:
        lines, placed = refs[0], refs[-1]
    local_experts, slot_rows, width = placed.shape
    slots = slot_rows // n_dp
    for rel in range(n_dp):
        if first:
            pair = [b[0 : rows + META, :] for b in (mine[rel], other[rel])]
            metas = [b[rows:, 0:rows].astype(F32) for b in pair]
            ids = jnp.concatenate([m[0:1] for m in metas], axis=1)
            place = jnp.concatenate([m[1:2] for m in metas], axis=1)
            low = (lax.axis_index("expert") * local_experts).astype(F32)
            row = ((ids - low) * slots + place).astype(jnp.int32)
            lines[rel] = jnp.broadcast_to(row, (8, row.shape[1]))
            pair = [b[0:rows] for b in pair]
        else:
            row = lines[rel][0:1]
            pair = [b[...] for b in (mine[rel], other[rel])]
        placer = placer_of(row, local_experts * slots)
        found = jnp.dot(placer, jnp.concatenate(pair, axis=0), preferred_element_type=F32).astype(BF16)
        placed[:, rel * slots : (rel + 1) * slots, :] = found.reshape(local_experts, slots, width)


def place(mine, others, lines, rows, local_experts, after):
    first = lines is None
    n_dp, slots = len(mine), 2 * CAP
    width = mine[0].shape[1]
    placed = jax.ShapeDtypeStruct((local_experts, n_dp * slots, width), BF16)
    line = jax.ShapeDtypeStruct((n_dp, 8, 2 * rows), jnp.int32)
    vmem = pl.BlockSpec(memory_space=pltpu.VMEM)
    operands = [*others] + ([] if first else [lines])

    def kernel(*refs):
        split_at = n_dp + len(others)
        place_kernel(first, rows, refs[:n_dp], refs[n_dp:split_at], *refs[split_at:])

    return pl.pallas_call(
        kernel,
        out_shape=[placed, line] if first else placed,
        in_specs=[vmem] * (n_dp + len(operands))
        + [pl.BlockSpec(memory_space=pl.ANY)] * len(after),
        out_specs=[vmem, vmem] if first else vmem,
        compiler_params=params(),
        cost_estimate=pl.CostEstimate(flops=PLACE_COST, bytes_accessed=4 * rows * width * n_dp, transcendentals=0),
    )(*mine, *operands, *after)


def back_kernel(low, first, last, *refs):
    if first:
        earlier, refs = refs[0], refs[1:]
    if last:
        lines, refs = refs[0], refs[1:]
    h0, h1, gate, up = refs[:4]
    outs, near, sems = refs[4:-2], refs[-2], refs[-1]
    parts = (h0, h1)
    count, slots, _ = h0.shape
    hidden = gate.shape[1]
    per_copy = count // sems.shape[1]

    def copy_of(which, at):
        rows = pl.ds(which * hidden, hidden)
        source = (gate, up)[which].at[pl.ds(first + at * per_copy, per_copy)]
        return pltpu.make_async_copy(source, near.at[pl.ds(at * per_copy, per_copy), rows], sems.at[which, at])

    for at in range(sems.shape[1]):
        for which in range(2):
            copy_of(which, at).start()
    for at in range(sems.shape[1]):
        for which in range(2):
            copy_of(which, at).wait()
        for e in range(at * per_copy, (at + 1) * per_copy):
            grads = jnp.concatenate([h[e] for h in parts], axis=0)
            value = jnp.dot(grads, near[e], preferred_element_type=F32).astype(BF16)
            for i in range(2):
                rows = value[i * slots : (i + 1) * slots]
                if last:
                    outs[-1][i, (first + e) * slots : (first + e + 1) * slots, :] = rows
                else:
                    outs[0][i, e * slots : (e + 1) * slots, :] = rows
    if not last:
        return
    held = outs[-1]
    if first:
        held[:, 0 : first * slots, :] = earlier[...]
    rows = outs[0].shape[0]
    odd = (lax.axis_index("dp") ^ lax.axis_index("tensor")) & 1
    for i in range(2):
        which = odd ^ i
        placer = placer_of(lines[low + which][0:1], held.shape[1])
        token_rows = lax.dot_general(
            placer, held[which], (((0,), (0,)), ((), ())), preferred_element_type=F32
        ).astype(BF16)
        outs[2 * i][...] = token_rows[0:rows]
        outs[2 * i + 1][...] = token_rows[rows:]


def back(low, lines, parts, gate, up, rows, first=0, earlier=None):
    local_experts, hidden, width = gate.shape
    count, slots, _ = parts[0].shape
    last = first + count == local_experts
    vmem = pl.BlockSpec(memory_space=pltpu.VMEM)
    flops = (16 if last else 1) * count * 2 * slots * width * hidden
    operands = ([earlier] if first else []) + ([lines] if last else []) + [*parts]
    near = [
        pltpu.VMEM((count, 2 * hidden, width), BF16),
        pltpu.SemaphoreType.DMA((2, count // 2 if count % 2 == 0 else count)),
    ]
    if last:
        out_shape = [jax.ShapeDtypeStruct((rows, width), BF16)] * 4
        near = [pltpu.VMEM((2, local_experts * slots, width), BF16)] + near
    else:
        out_shape = jax.ShapeDtypeStruct((2, count * slots, width), BF16)
    return pl.pallas_call(
        functools.partial(back_kernel, low, first, last),
        out_shape=out_shape,
        in_specs=[vmem] * len(operands) + [pl.BlockSpec(memory_space=pl.ANY)] * 2,
        out_specs=[vmem] * 4 if last else vmem,
        scratch_shapes=near,
        compiler_params=params(48),
        cost_estimate=pl.CostEstimate(
            flops=flops, bytes_accessed=2 * count * width * hidden * 2 if last else width, transcendentals=0
        ),
    )(*operands, gate, up)


def weight_kernel(placed, h0, h1, h2, h3, gate, up):
    hidden = gate.shape[1]
    for i in range(gate.shape[0]):
        grads = jnp.concatenate([h[i] for h in (h0, h1, h2, h3)], axis=0)
        both = lax.dot_general(
            grads, placed[i], (((0,), (0,)), ((), ())), preferred_element_type=F32
        ).astype(BF16)
        gate[i] = both[0:hidden]
        up[i] = both[hidden:]


def weight_grads(placed, parts, per_step):
    local_experts, slot_rows, width = placed.shape
    _, slots, both = parts[0].shape
    hidden = both // 2
    part_spec = pl.BlockSpec((per_step, slots, both), lambda e: (e, 0, 0))
    out_spec = pl.BlockSpec((per_step, hidden, width), lambda e: (e, 0, 0))
    flops = 2 * local_experts * slot_rows * width * both
    return pl.pallas_call(
        weight_kernel,
        grid=(local_experts // per_step,),
        out_shape=[jax.ShapeDtypeStruct((local_experts, hidden, width), BF16)] * 2,
        in_specs=[pl.BlockSpec((per_step, slot_rows, width), lambda e: (e, 0, 0))] + [part_spec] * len(parts),
        out_specs=[out_spec] * 2,
        compiler_params=params(12),
        cost_estimate=pl.CostEstimate(
            flops=4 * flops, bytes_accessed=local_experts * width * both * 2, transcendentals=0
        ),
    )(placed, *parts)


def plus(first, second):
    return first.astype(F32) + second.astype(F32)


def swiglu_grads(gate_act, up_act, hidden_grad):
    sigmoid_gate = jax.nn.sigmoid(gate_act)
    up_grad = (hidden_grad * gate_act * sigmoid_gate).astype(BF16)
    gate_grad = (
        hidden_grad * up_act * sigmoid_gate * (1.0 + gate_act * (1.0 - sigmoid_gate))
    ).astype(BF16)
    return gate_grad, up_grad


def on_small_slice(tokens, cotangent, expert_ids, gate_weight, up_weight, down_weight):
    n_dp, n_x, n_t = 4, 2, 4
    k, x, t = lax.axis_index("dp"), lax.axis_index("expert"), lax.axis_index("tensor")
    width = gate_weight.shape[1]
    rows = tokens.shape[0]
    ids_row = expert_ids.reshape(1, rows)
    order = jnp.arange(rows, dtype=jnp.int32)
    earlier = (expert_ids == ids_row) & (order[:, None] < order[None, :])
    position = jnp.sum(earlier.astype(jnp.int32), axis=0, keepdims=True) + x * CAP
    meta = jnp.concatenate([ids_row, position], axis=0).astype(BF16)
    meta = jnp.pad(meta, ((0, META - 2), (0, width - rows)))

    def columns(values, rel):
        return lax.dynamic_slice_in_dim(values, (k ^ rel) * width, width, axis=1)

    chunks = [jnp.concatenate([columns(tokens, rel), meta], axis=0) for rel in range(n_dp)]

    def to_owner(value, rel, flip):
        if rel == 0 and flip == 0:
            return value
        pairs = [
            (i * n_x + j, (i ^ rel) * n_x + (j ^ flip)) for i in range(n_dp) for j in range(n_x)
        ]
        return lax.ppermute(value, ("dp", "expert"), pairs)

    own_tokens = [to_owner(c, rel, 0) for rel, c in enumerate(chunks)]
    near_tokens = [to_owner(c, rel, 1) for rel, c in enumerate(chunks[:2])]
    grads = [columns(cotangent, rel) for rel in range(n_dp)]
    far_tokens, grads = lax.optimization_barrier((own_tokens[2:], grads))
    near_tokens, far_tokens = lax.optimization_barrier((near_tokens, far_tokens))
    far_tokens = [swap(c, "expert", n_x, 1) for c in far_tokens]
    own_grads = [to_owner(c, rel, 0) for rel, c in enumerate(grads)]
    leaving_grads = jnp.stack(own_grads)
    far_tokens, leaving_grads = lax.optimization_barrier((far_tokens, leaving_grads))
    other_grads = swap(leaving_grads, "expert", n_x, 1)
    gate_weight, up_weight, down_weight = (
        jnp.swapaxes(weight, 1, 2) for weight in (gate_weight, up_weight, down_weight)
    )
    local_experts = gate_weight.shape[0]

    def project(values, weight):
        act = jnp.einsum("esd,ehd->esh", values, weight, preferred_element_type=F32).astype(BF16)
        return jnp.split(act, n_dp, axis=1)

    def near_and_far(act):
        near, far = swap(act[1], "dp", n_dp, 1), swap(act[3], "dp", n_dp, 1)
        return plus(act[0], near), plus(act[2], far).astype(BF16)

    placed, lines = place(own_tokens, near_tokens + far_tokens, None, rows, local_experts, [leaving_grads])
    gate_near, gate_far = near_and_far(project(placed, gate_weight))
    up_near, up_far = near_and_far(project(placed, up_weight))
    far = jnp.stack([gate_far, up_far])
    there = swap(far, "dp", n_dp, 2)
    placed_grads = place(own_grads, [other_grads], lines, rows, local_experts, [far])
    hidden_act = project(placed_grads, down_weight)
    beside, there = lax.optimization_barrier((swap(hidden_act[3], "dp", n_dp, 1), there))
    hidden_far = plus(hidden_act[2], beside).astype(BF16)
    hidden_near = plus(hidden_act[0], swap(hidden_act[1], "dp", n_dp, 1))
    gate_act, up_act = plus(gate_near, there[0]), plus(up_near, there[1])
    sigmoid_gate = jax.nn.sigmoid(gate_act)
    up_factor = gate_act * sigmoid_gate
    gate_factor = up_act * sigmoid_gate * (1.0 + gate_act * (1.0 - sigmoid_gate))
    hidden_grad = plus(hidden_near, swap(hidden_far, "dp", n_dp, 2))
    part = jnp.concatenate([hidden_grad * gate_factor, hidden_grad * up_factor], axis=2).astype(BF16)
    count = local_experts * 3 // 8
    far = [swap(piece, "dp", n_dp, 2) for piece in jnp.split(part, [count], axis=0)]
    beside = swap(part, "dp", n_dp, 1)
    near_back = back(0, lines, [part, beside], gate_weight, up_weight, rows)
    far[0], _ = lax.optimization_barrier((far[0], near_back[0]))
    far_beside = [swap(far[0], "dp", n_dp, 1)]
    early = back(2, lines, [far[0], far_beside[0]], gate_weight, up_weight, rows)
    far[1], _ = lax.optimization_barrier((far[1], early))
    far_beside.append(swap(far[1], "dp", n_dp, 1))
    far_back = back(2, lines, [far[1], far_beside[1]], gate_weight, up_weight, rows, count, early)
    parts = [part, beside, jnp.concatenate(far, axis=0), jnp.concatenate(far_beside, axis=0)]
    others = swap(jnp.stack(near_back[1::2]), "expert", n_x, 1)
    others, after_back, _ = lax.optimization_barrier((others, placed, far_back[0]))
    weight_grad = weight_grads(after_back, parts, 4)

    def to_keeper(value, low, turn, flip):
        pairs = []
        for i in range(n_dp):
            for j in range(n_x):
                for l in range(n_t):
                    odd = (i ^ l) & 1
                    to = ((i ^ low ^ odd ^ turn) * n_x + (j ^ flip)) * n_t + (l ^ odd)
                    pairs.append(((i * n_x + j) * n_t + l, to))
        return lax.ppermute(value, ("dp", "expert", "tensor"), pairs)

    merged = [plus(own, other).astype(BF16) for own, other in zip(near_back[::2], others)]
    far_terms = [to_keeper(value, 2, at // 2, at % 2) for at, value in enumerate(far_back)]
    merged, _ = lax.optimization_barrier((merged, weight_grad))
    near_terms = [to_keeper(value, 0, turn, 0) for turn, value in enumerate(merged)]
    first, second = (sum(v.astype(F32) for v in terms) for terms in (near_terms, far_terms))
    swapped = ((k ^ t) & 2) == 2
    keep = jnp.where(swapped, second, first)
    leaving = jnp.where(swapped, first, second).astype(BF16)
    grad_tokens = plus(keep, swap(leaving, "tensor", n_t, 2)).astype(BF16)

    grad_gate, grad_up = (jnp.swapaxes(grad, 1, 2) for grad in weight_grad)
    return grad_tokens, grad_gate, grad_up


def bits_of(count):
    bits = []
    bit = 1
    while bit < count:
        bits.append(bit)
        bit *= 2
    return bits


def halving_sum(parts, axis, count):
    parts = dict(parts)
    for bit in bits_of(count):
        leaving = sorted(r for r in parts if r & bit)
        arrived = swap(jnp.stack([parts[r].astype(BF16) for r in leaving]), axis, count, bit)
        for at, r in enumerate(leaving):
            parts[r ^ bit] = plus(parts[r ^ bit], arrived[at])
            del parts[r]
    return parts[0]


def doubling_gather(value, axis, count):
    held = {0: value}
    for bit in reversed(bits_of(count)):
        known = sorted(held)
        arrived = swap(jnp.stack([held[r] for r in known]), axis, count, bit)
        for at, r in enumerate(known):
            held[r ^ bit] = arrived[at]
    return [held[r] for r in range(count)]


def on_any_slice(tokens, cotangent, expert_ids, gate_weight, up_weight, down_weight):
    n_dp, n_x, n_t = lax.axis_size("dp"), lax.axis_size("expert"), lax.axis_size("tensor")
    k, x, t = lax.axis_index("dp"), lax.axis_index("expert"), lax.axis_index("tensor")
    local_experts, width, hidden = gate_weight.shape
    rows = tokens.shape[0]
    slots = n_x * CAP
    ids_row = expert_ids.reshape(1, rows)
    order = jnp.arange(rows, dtype=jnp.int32)
    earlier = (expert_ids == ids_row) & (order[:, None] < order[None, :])
    position = jnp.sum(earlier.astype(jnp.int32), axis=0)
    target = ids_row[0] * CAP + position
    targets = lax.all_gather(target, ("dp", "expert"), axis=0, tiled=False).reshape(n_dp, n_x, rows)
    pair = jnp.stack([tokens, cotangent])
    placers, slot_rows = [], []
    for rel in range(n_dp):
        columns = lax.dynamic_slice_in_dim(pair, (k ^ rel) * width, width, axis=2)
        mine = columns if rel == 0 else swap(columns, "dp", n_dp, rel)
        blocks = lax.all_gather(mine, "expert", axis=1, tiled=True)
        goal = lax.dynamic_index_in_dim(targets, k ^ rel, axis=0, keepdims=False)
        expert = goal // CAP - x * local_experts
        place = jnp.arange(n_x, dtype=jnp.int32)[:, None] * CAP + goal % CAP
        row = jnp.where((expert >= 0) & (expert < local_experts), expert * slots + place, -1)
        row = row.reshape(1, n_x * rows)
        every = jnp.arange(local_experts * slots, dtype=jnp.int32)[:, None]
        placer = (every == row).astype(BF16)
        placers.append(placer)
        slot_rows.append(
            jnp.einsum("sn,and->asd", placer, blocks, preferred_element_type=F32)
            .astype(BF16)
            .reshape(2, local_experts, slots, width)
        )
    slot_rows = jnp.concatenate(slot_rows, axis=2)
    inputs, grads_in = slot_rows[0], slot_rows[1]

    def act(values, weight):
        return jnp.einsum("esd,edf->esf", values, weight, preferred_element_type=F32).astype(BF16)

    acts = jnp.stack([act(inputs, gate_weight), act(inputs, up_weight), act(grads_in, down_weight)])
    acts = acts.reshape(3, local_experts, n_dp, slots, hidden)
    acts = halving_sum({r: acts[:, :, r] for r in range(n_dp)}, "dp", n_dp)
    grads = doubling_gather(jnp.stack(swiglu_grads(acts[0], acts[1], acts[2])), "dp", n_dp)
    grads = jnp.concatenate(grads, axis=2)
    gate_grad, up_grad = grads[0], grads[1]
    partial_value = jnp.einsum("esf,edf->esd", gate_grad, gate_weight, preferred_element_type=F32)
    partial_value = partial_value + jnp.einsum("esf,edf->esd", up_grad, up_weight, preferred_element_type=F32)
    partial_value = partial_value.astype(BF16).reshape(local_experts, n_dp, slots, width)
    per_token = []
    for rel in range(n_dp):
        flat = partial_value[:, rel].reshape(local_experts * slots, width)
        spread = lax.dot_general(placers[rel], flat, (((0,), (0,)), ((), ())), preferred_element_type=F32)
        spread = spread.astype(BF16).reshape(n_x, rows, width)
        per_token.append(lax.psum_scatter(spread, "expert", scatter_dimension=0, tiled=False))
    per_token = jnp.stack(per_token)
    terms = {r: lax.dynamic_index_in_dim(per_token, k ^ t ^ r, axis=0, keepdims=False) for r in range(n_t)}
    summed = halving_sum(terms, "tensor", n_t).astype(BF16)
    summed = lax.ppermute(
        summed, ("dp", "tensor"), [(i * n_t + j, j * n_t + i) for i in range(n_dp) for j in range(n_t)]
    )
    grad_gate = jnp.einsum("esd,esf->edf", inputs, gate_grad, preferred_element_type=F32).astype(BF16)
    grad_up = jnp.einsum("esd,esf->edf", inputs, up_grad, preferred_element_type=F32).astype(BF16)
    return summed, grad_gate, grad_up


def solution(mesh):
    placed = (
        P(("dp", "expert"), None),
        P(("dp", "expert"), None),
        P(("dp", "expert"), None),
        P("expert", "dp", "tensor"),
        P("expert", "dp", "tensor"),
        P("expert", "dp", "tensor"),
    )
    sizes = tuple(mesh.shape[name] for name in ("dp", "expert", "tensor"))
    return jax.shard_map(
        on_small_slice if sizes == (4, 2, 4) else on_any_slice,
        mesh=mesh,
        in_specs=placed,
        out_specs=(
            P(("dp", "expert"), "tensor"),
            P("expert", "dp", "tensor"),
            P("expert", "dp", "tensor"),
        ),
        check_vma=False,
    )
```

profile of v0, /device:TPU:0, one launch (start us, length us, event | category | flops | bytes accessed | tf_op | source)
XLA Modules:
  0.0 97.1 jit_solution(11228634640095740305)
XLA Ops:
  3.4 2.5 %collective-permute-start.1 = (bf16[144,512]{1,0:T(8,128)(2,1)S(1)}, bf16[144,512]{1,0:T(8,128)(2,1)S(1)}, u32[]{:S(2)}, u32[]{:S(2)}) collective-permute-start(bf16[144,512]{1,0:T(8,128)(2,1)S(1)} %get-tuple-element.87), channel_id=1, source_target_pairs={{0,24},{4,28},{8,16},{12,20},{16,8},{20,12},{24,0},{28,4},{1,25},{... | collective-permute-start | bytes 442376 | tf_op jit(solution)/shard_map/ppermute | solution.py:233
  10.1 3.3 %collective-permute-done.refs_2_ = bf16[144,512]{1,0:T(8,128)(2,1)S(1)} collective-permute-done((bf16[144,512]{1,0:T(8,128)(2,1)S(1)}, bf16[144,512]{1,0:T(8,128)(2,1)S(1)}, u32[]{:S(2)}, u32[]{:S(2)}) %collective-permute-start) | collective-permute-done | bytes 147488 | tf_op jit(solution)/shard_map/ppermute | solution.py:233
  13.4 2.4 %collective-permute-start.3 = (bf16[128,512]{1,0:T(8,128)(2,1)S(1)}, bf16[128,512]{1,0:T(8,128)(2,1)S(1)}, u32[]{:S(2)}, u32[]{:S(2)}) collective-permute-start(bf16[128,512]{1,0:T(8,128)(2,1)S(1)} %get-tuple-element.38), channel_id=1, source_target_pairs={{0,16},{4,20},{8,24},{12,28},{16,0},{20,4},{24,8},{28,12},{1,17},{... | collective-permute-start | bytes 393224 | tf_op jit(solution)/shard_map/ppermute | solution.py:233
  15.9 1.7 %collective-permute-start.7 = (bf16[144,512]{1,0:T(8,128)(2,1)S(1)}, bf16[144,512]{1,0:T(8,128)(2,1)S(1)}, u32[]{:S(2)}, u32[]{:S(2)}) collective-permute-start(bf16[144,512]{1,0:T(8,128)(2,1)S(1)} %collective-permute-done.refs_2_), channel_id=1, source_target_pairs={{0,4},{4,0},{1,5},{5,1},{2,6},{6,2},{3,7},{7,3},{8,12},{12,8},{9,1... | collective-permute-start | bytes 442376 | tf_op jit(solution)/shard_map/ppermute | solution.py:19
  18.0 2.2 %collective-permute-done.3.refs_2_ = bf16[128,512]{1,0:T(8,128)(2,1)S(1)} collective-permute-done((bf16[128,512]{1,0:T(8,128)(2,1)S(1)}, bf16[128,512]{1,0:T(8,128)(2,1)S(1)}, u32[]{:S(2)}, u32[]{:S(2)}) %collective-permute-start.3) | collective-permute-done | bytes 131104 | tf_op jit(solution)/shard_map/ppermute | solution.py:233
  20.2 2.3 %collective-permute-done.4.refs_3_ = bf16[128,512]{1,0:T(8,128)(2,1)S(1)} collective-permute-done((bf16[128,512]{1,0:T(8,128)(2,1)S(1)}, bf16[128,512]{1,0:T(8,128)(2,1)S(1)}, u32[]{:S(2)}, u32[]{:S(2)}) %collective-permute-start.4) | collective-permute-done | bytes 131104 | tf_op jit(solution)/shard_map/ppermute | solution.py:233
  22.6 2.5 %collective-permute-done.8.refs_7_ = bf16[144,512]{1,0:T(8,128)(2,1)S(1)} collective-permute-done((bf16[144,512]{1,0:T(8,128)(2,1)S(1)}, bf16[144,512]{1,0:T(8,128)(2,1)S(1)}, u32[]{:S(2)}, u32[]{:S(2)}) %collective-permute-start.8) | collective-permute-done | bytes 147488 | tf_op jit(solution)/shard_map/ppermute | solution.py:19
  25.1 1.7 %collective-permute-start.9 = (bf16[4,128,512]{2,1,0:T(8,128)(2,1)S(1)}, bf16[4,128,512]{2,1,0:T(8,128)(2,1)S(1)}, u32[]{:S(2)}, u32[]{:S(2)}) collective-permute-start(bf16[4,128,512]{2,1,0:T(8,128)(2,1)S(1)} %pad_maximum_fusion.refs_8_), channel_id=1, source_target_pairs={{0,4},{4,0},{1,5},{5,1},{2,6},{6,2},{3,7},{7,3},{8,12},{12,8},{9,1... | collective-permute-start | bytes 1572872 | tf_op jit(solution)/shard_map/ppermute | solution.py:19
  27.3 1.7 %convolution_convert_fusion.1 = bf16[16,64,352]{2,1,0:T(8,128)(2,1)S(1)} fusion(bf16[16,64,512]{2,1,0:T(8,128)(2,1)S(1)} %get-tuple-element.64.placed, bf16[16,512,352]{1,2,0:T(8,128)(2,1)S(1)} %bitcast.48), kind=kOutput, calls=%fused_computation.1 | convolution fusion | flops 369459200 | bytes 7536640 | tf_op jit(solution)/shard_map/esd,ehd->esh/dot_general | solution.py:251
  29.1 1.7 %convolution_convert_fusion.2 = bf16[16,64,352]{2,1,0:T(8,128)(2,1)S(1)} fusion(bf16[16,64,512]{2,1,0:T(8,128)(2,1)S(1)} %get-tuple-element.64.placed, bf16[16,512,352]{1,2,0:T(8,128)(2,1)S(1)} %bitcast.53), kind=kOutput, calls=%fused_computation.2 | convolution fusion | flops 369459200 | bytes 7536640 | tf_op jit(solution)/shard_map/esd,ehd->esh/dot_general | solution.py:251
  32.6 1.7 %collective-permute-start.15 = (bf16[2,16,16,352]{3,2,1,0:T(8,128)(2,1)S(1)}, bf16[2,16,16,352]{3,2,1,0:T(8,128)(2,1)S(1)}, u32[]{:S(2)}, u32[]{:S(2)}) collective-permute-start(bf16[2,16,16,352]{3,2,1,0:T(8,128)(2,1)S(1)} %pad_maximum_fusion.2.refs_6_), channel_id=1, source_target_pairs={{0,16},{8,24},{16,0},{24,8},{1,17},{9,25},{17,1},{25,9},{2,18},{10... | collective-permute-start | bytes 1081352 | tf_op jit(solution)/shard_map/ppermute | solution.py:19
  34.2 4.1 %collective-permute-done.9.refs_4_ = bf16[4,128,512]{2,1,0:T(8,128)(2,1)S(1)} collective-permute-done((bf16[4,128,512]{2,1,0:T(8,128)(2,1)S(1)}, bf16[4,128,512]{2,1,0:T(8,128)(2,1)S(1)}, u32[]{:S(2)}, u32[]{:S(2)}) %collective-permute-start.9) | collective-permute-done | bytes 524320 | tf_op jit(solution)/shard_map/ppermute | solution.py:19
  39.8 1.6 %convolution_convert_fusion = bf16[16,64,352]{2,1,0:T(8,128)(2,1)S(1)} fusion(bf16[16,64,512]{2,1,0:T(8,128)(2,1)S(1)} %shard_map.86, bf16[16,512,352]{1,2,0:T(8,128)(2,1)S(1)} %bitcast.55), kind=kOutput, calls=%fused_computation | convolution fusion | flops 369459200 | bytes 7536640 | tf_op jit(solution)/shard_map/esd,ehd->esh/dot_general | solution.py:251
  44.1 1.6 %collective-permute-start.16 = (bf16[16,16,352]{2,1,0:T(8,128)(2,1)S(1)}, bf16[16,16,352]{2,1,0:T(8,128)(2,1)S(1)}, u32[]{:S(2)}, u32[]{:S(2)}) collective-permute-start(bf16[16,16,352]{2,1,0:T(8,128)(2,1)S(1)} %add_convert_fusion), channel_id=1, source_target_pairs={{0,16},{8,24},{16,0},{24,8},{1,17},{9,25},{17,1},{25,9},{2,18},{10... | collective-permute-start | bytes 540680 | tf_op jit(solution)/shard_map/ppermute | solution.py:19
  45.7 4.8 %collective-permute-done.16 = bf16[16,16,352]{2,1,0:T(8,128)(2,1)S(1)} collective-permute-done((bf16[16,16,352]{2,1,0:T(8,128)(2,1)S(1)}, bf16[16,16,352]{2,1,0:T(8,128)(2,1)S(1)}, u32[]{:S(2)}, u32[]{:S(2)}) %collective-permute-start.16) | collective-permute-done | bytes 180256 | tf_op jit(solution)/shard_map/ppermute | solution.py:19
  53.5 5.1 %shard_map.87 = (bf16[128,512]{1,0:T(8,128)(2,1)S(1)}, bf16[128,512]{1,0:T(8,128)(2,1)S(1)}, bf16[128,512]{1,0:T(8,128)(2,1)S(1)}, bf16[128,512]{1,0:T(8,128)(2,1)S(1)}) custom-call(s32[4,8,256]{2,1,0:T(8,128)S(1)} %get-tuple-element.49.refs_5_.refs_0_.refs_1_, bf16[16,16,704]{2,1,0:T(8,128)(2,1)S(1)} %pad_maximum_fusion.1.refs_1_.h0, ...), custom_call_target="tpu_custom_call" | custom-call | flops 1476395008 | bytes 11534336 | tf_op jit(solution)/shard_map/pallas_call | solution.py:153
  60.0 2.6 %shard_map.88.refs_0_ = bf16[2,96,512]{2,1,0:T(8,128)(2,1)S(1)} custom-call(bf16[6,16,704]{2,1,0:T(8,128)(2,1)S(1)} %collective-permute-done.19.refs_0_, bf16[6,16,704]{2,1,0:T(8,128)(2,1)S(1)} %collective-permute-done.21.refs_1_, bf16[16,352,512]{2,1,0:T(8,128)(2,1)} %bitcast.50, bf16[16,352,512]{2,1,0:T(8,128)(2,1)} %bitcast.45), custom_call_target="tpu_custom_call" | custom-call | flops 34603008 | bytes 512 | tf_op jit(solution)/shard_map/pallas_call | solution.py:153
  64.3 3.8 %shard_map.89 = (bf16[128,512]{1,0:T(8,128)(2,1)S(1)}, bf16[128,512]{1,0:T(8,128)(2,1)S(1)}, bf16[128,512]{1,0:T(8,128)(2,1)S(1)}, bf16[128,512]{1,0:T(8,128)(2,1)S(1)}) custom-call(bf16[2,96,512]{2,1,0:T(8,128)(2,1)S(1)} %shard_map.88.refs_0_, s32[4,8,256]{2,1,0:T(8,128)S(1)} %get-tuple-element.49.refs_5_.refs_0_.refs_1_, ...), custom_call_target="tpu_custom_call" | custom-call | flops 922746880 | bytes 7208960 | tf_op jit(solution)/shard_map/pallas_call | solution.py:153
  68.1 2.4 %collective-permute-start.25 = (bf16[128,512]{1,0:T(8,128)(2,1)S(1)}, bf16[128,512]{1,0:T(8,128)(2,1)S(1)}, u32[]{:S(2)}, u32[]{:S(2)}) collective-permute-start(bf16[128,512]{1,0:T(8,128)(2,1)S(1)} %get-tuple-element.57), channel_id=1, source_target_pairs={{0,20},{1,28},{2,22},{3,30},{4,16},{5,24},{6,18},{7,26},{8,21},{9,... | collective-permute-start | bytes 393224 | tf_op jit(solution)/shard_map/ppermute | solution.py:297
  73.5 5.8 %shard_map.90 = (bf16[16,352,512]{2,1,0:T(8,128)(2,1)}, bf16[16,352,512]{2,1,0:T(8,128)(2,1)}) custom-call(bf16[16,64,512]{2,1,0:T(8,128)(2,1)S(1)} %get-tuple-element.64.placed, bf16[16,16,704]{2,1,0:T(8,128)(2,1)S(1)} %pad_maximum_fusion.1.refs_1_.h0, bf16[16,16,704]{2,1,0:T(8,128)(2,1)S(1)} %collective-permute-done.20.refs_2_.h1, ...), custom_call_target="tpu_custom_call" | custom-call | flops 2952790016 | bytes 11534336 | tf_op jit(solution)/shard_map/pallas_call | solution.py:184
  80.0 2.9 %collective-permute-start.30 = (bf16[128,512]{1,0:T(8,128)(2,1)S(1)}, bf16[128,512]{1,0:T(8,128)(2,1)S(1)}, u32[]{:S(2)}, u32[]{:S(2)}) collective-permute-start(bf16[128,512]{1,0:T(8,128)(2,1)S(1)} %get-tuple-element.68), channel_id=1, source_target_pairs={{0,8},{1,0},{2,10},{3,2},{4,12},{5,4},{6,14},{7,6},{8,9},{9,1},{10... | collective-permute-start | bytes 393224 | tf_op jit(solution)/shard_map/ppermute | solution.py:297
  83.9 4.8 %collective-permute-done.30 = bf16[128,512]{1,0:T(8,128)(2,1)S(1)} collective-permute-done((bf16[128,512]{1,0:T(8,128)(2,1)S(1)}, bf16[128,512]{1,0:T(8,128)(2,1)S(1)}, u32[]{:S(2)}, u32[]{:S(2)}) %collective-permute-start.30) | collective-permute-done | bytes 131104 | tf_op jit(solution)/shard_map/ppermute | solution.py:297
  88.8 2.7 %collective-permute-start.31 = (bf16[128,512]{1,0:T(8,128)(2,1)S(1)}, bf16[128,512]{1,0:T(8,128)(2,1)S(1)}, u32[]{:S(2)}, u32[]{:S(2)}) collective-permute-start(bf16[128,512]{1,0:T(8,128)(2,1)S(1)} %select_convert_fusion), channel_id=1, source_target_pairs={{0,2},{1,3},{2,0},{3,1},{4,6},{5,7},{6,4},{7,5},{8,10},{9,11},{10,... | collective-permute-start | bytes 393224 | tf_op jit(solution)/shard_map/ppermute | solution.py:19
  91.4 4.9 %collective-permute-done.31 = bf16[128,512]{1,0:T(8,128)(2,1)S(1)} collective-permute-done((bf16[128,512]{1,0:T(8,128)(2,1)S(1)}, bf16[128,512]{1,0:T(8,128)(2,1)S(1)}, u32[]{:S(2)}, u32[]{:S(2)}) %collective-permute-start.31) | collective-permute-done | bytes 131104 | tf_op jit(solution)/shard_map/ppermute | solution.py:19
  (89 shorter events, 25.5 us)
Async XLA Ops:
  3.4 6.7 %collective-permute-start.1 = (bf16[144,512]{1,0:T(8,128)(2,1)S(1)}, bf16[144,512]{1,0:T(8,128)(2,1)S(1)}, u32[]{:S(2)}, u32[]{:S(2)}) collective-permute-start(bf16[144,512]{1,0:T(8,128)(2,1)S(1)} %get-tuple-element.87), channel_id=1, source_target_pairs={{0,24},{4,28},{8,16},{12,20},{16,8},{20,12},{24,0},{28,4},{1,25},{... | collective-permute-start | bytes 442376 | tf_op jit(solution)/shard_map/ppermute | solution.py:233
  5.9 7.6 %collective-permute-start = (bf16[144,512]{1,0:T(8,128)(2,1)S(1)}, bf16[144,512]{1,0:T(8,128)(2,1)S(1)}, u32[]{:S(2)}, u32[]{:S(2)}) collective-permute-start(bf16[144,512]{1,0:T(8,128)(2,1)S(1)} %get-tuple-element.90), channel_id=1, source_target_pairs={{0,16},{4,20},{8,24},{12,28},{16,0},{20,4},{24,8},{28,12},{1,17},{... | collective-permute-start | bytes 442376 | tf_op jit(solution)/shard_map/ppermute | solution.py:233
  6.5 9.4 %collective-permute-start.5 = (bf16[144,512]{1,0:T(8,128)(2,1)S(1)}, bf16[144,512]{1,0:T(8,128)(2,1)S(1)}, u32[]{:S(2)}, u32[]{:S(2)}) collective-permute-start(bf16[144,512]{1,0:T(8,128)(2,1)S(1)} %get-tuple-element.88.refs_0_), channel_id=1, source_target_pairs={{0,4},{4,0},{8,12},{12,8},{16,20},{20,16},{24,28},{28,24},{1,5},{5... | collective-permute-start | bytes 442376 | tf_op jit(solution)/shard_map/ppermute | solution.py:233
  8.0 7.9 %collective-permute-start.6 = (bf16[144,512]{1,0:T(8,128)(2,1)S(1)}, bf16[144,512]{1,0:T(8,128)(2,1)S(1)}, u32[]{:S(2)}, u32[]{:S(2)}) collective-permute-start(bf16[144,512]{1,0:T(8,128)(2,1)S(1)} %get-tuple-element.89), channel_id=1, source_target_pairs={{0,12},{4,8},{8,4},{12,0},{16,28},{20,24},{24,20},{28,16},{1,13},{... | collective-permute-start | bytes 442376 | tf_op jit(solution)/shard_map/ppermute | solution.py:233
  13.4 4.5 %collective-permute-start.2 = (bf16[128,512]{1,0:T(8,128)(2,1)S(1)}, bf16[128,512]{1,0:T(8,128)(2,1)S(1)}, u32[]{:S(2)}, u32[]{:S(2)}) collective-permute-start(bf16[128,512]{1,0:T(8,128)(2,1)S(1)} %get-tuple-element.37), channel_id=1, source_target_pairs={{0,8},{4,12},{8,0},{12,4},{16,24},{20,28},{24,16},{28,20},{1,9},{5... | collective-permute-start | bytes 393224 | tf_op jit(solution)/shard_map/ppermute | solution.py:233
  13.4 6.7 %collective-permute-start.3 = (bf16[128,512]{1,0:T(8,128)(2,1)S(1)}, bf16[128,512]{1,0:T(8,128)(2,1)S(1)}, u32[]{:S(2)}, u32[]{:S(2)}) collective-permute-start(bf16[128,512]{1,0:T(8,128)(2,1)S(1)} %get-tuple-element.38), channel_id=1, source_target_pairs={{0,16},{4,20},{8,24},{12,28},{16,0},{20,4},{24,8},{28,12},{1,17},{... | collective-permute-start | bytes 393224 | tf_op jit(solution)/shard_map/ppermute | solution.py:233
  15.8 6.6 %collective-permute-start.4 = (bf16[128,512]{1,0:T(8,128)(2,1)S(1)}, bf16[128,512]{1,0:T(8,128)(2,1)S(1)}, u32[]{:S(2)}, u32[]{:S(2)}) collective-permute-start(bf16[128,512]{1,0:T(8,128)(2,1)S(1)} %get-tuple-element.39), channel_id=1, source_target_pairs={{0,24},{4,28},{8,16},{12,20},{16,8},{20,12},{24,0},{28,4},{1,25},{... | collective-permute-start | bytes 393224 | tf_op jit(solution)/shard_map/ppermute | solution.py:233
  15.9 6.7 %collective-permute-start.7 = (bf16[144,512]{1,0:T(8,128)(2,1)S(1)}, bf16[144,512]{1,0:T(8,128)(2,1)S(1)}, u32[]{:S(2)}, u32[]{:S(2)}) collective-permute-start(bf16[144,512]{1,0:T(8,128)(2,1)S(1)} %collective-permute-done.refs_2_), channel_id=1, source_target_pairs={{0,4},{4,0},{1,5},{5,1},{2,6},{6,2},{3,7},{7,3},{8,12},{12,8},{9,1... | collective-permute-start | bytes 442376 | tf_op jit(solution)/shard_map/ppermute | solution.py:19
  17.6 7.5 %collective-permute-start.8 = (bf16[144,512]{1,0:T(8,128)(2,1)S(1)}, bf16[144,512]{1,0:T(8,128)(2,1)S(1)}, u32[]{:S(2)}, u32[]{:S(2)}) collective-permute-start(bf16[144,512]{1,0:T(8,128)(2,1)S(1)} %collective-permute-done.1.refs_3_), channel_id=1, source_target_pairs={{0,4},{4,0},{1,5},{5,1},{2,6},{6,2},{3,7},{7,3},{8,12},{12,8},{9,1... | collective-permute-start | bytes 442376 | tf_op jit(solution)/shard_map/ppermute | solution.py:19
  17.9 8.9 %collective-permute-start.10 = (bf16[144,512]{1,0:T(8,128)(2,1)S(1)}, bf16[144,512]{1,0:T(8,128)(2,1)S(1)}, u32[]{:S(2)}, u32[]{:S(2)}) collective-permute-start(bf16[144,512]{1,0:T(8,128)(2,1)S(1)} %get-tuple-element.89), channel_id=1, source_target_pairs={{0,8},{4,12},{8,0},{12,4},{16,24},{20,28},{24,16},{28,20},{1,9},{5... | collective-permute-start | bytes 442376 | tf_op jit(solution)/shard_map/ppermute | solution.py:233
  25.1 13.3 %collective-permute-start.9 = (bf16[4,128,512]{2,1,0:T(8,128)(2,1)S(1)}, bf16[4,128,512]{2,1,0:T(8,128)(2,1)S(1)}, u32[]{:S(2)}, u32[]{:S(2)}) collective-permute-start(bf16[4,128,512]{2,1,0:T(8,128)(2,1)S(1)} %pad_maximum_fusion.refs_8_), channel_id=1, source_target_pairs={{0,4},{4,0},{1,5},{5,1},{2,6},{6,2},{3,7},{7,3},{8,12},{12,8},{9,1... | collective-permute-start | bytes 1572872 | tf_op jit(solution)/shard_map/ppermute | solution.py:19
  32.6 11.5 %collective-permute-start.15 = (bf16[2,16,16,352]{3,2,1,0:T(8,128)(2,1)S(1)}, bf16[2,16,16,352]{3,2,1,0:T(8,128)(2,1)S(1)}, u32[]{:S(2)}, u32[]{:S(2)}) collective-permute-start(bf16[2,16,16,352]{3,2,1,0:T(8,128)(2,1)S(1)} %pad_maximum_fusion.2.refs_6_), channel_id=1, source_target_pairs={{0,16},{8,24},{16,0},{24,8},{1,17},{9,25},{17,1},{25,9},{2,18},{10... | collective-permute-start | bytes 1081352 | tf_op jit(solution)/shard_map/ppermute | solution.py:19
  41.6 4.2 %collective-permute-start.17 = (bf16[16,16,352]{2,1,0:T(8,128)(2,1)S(1)}, bf16[16,16,352]{2,1,0:T(8,128)(2,1)S(1)}, u32[]{:S(2)}, u32[]{:S(2)}) collective-permute-start(bf16[16,16,352]{2,1,0:T(8,128)(2,1)S(1)} %get-tuple-element.71), channel_id=1, source_target_pairs={{0,8},{8,0},{16,24},{24,16},{1,9},{9,1},{17,25},{25,17},{2,10},{10... | collective-permute-start | bytes 540680 | tf_op jit(solution)/shard_map/ppermute | solution.py:19
  44.1 6.4 %collective-permute-start.16 = (bf16[16,16,352]{2,1,0:T(8,128)(2,1)S(1)}, bf16[16,16,352]{2,1,0:T(8,128)(2,1)S(1)}, u32[]{:S(2)}, u32[]{:S(2)}) collective-permute-start(bf16[16,16,352]{2,1,0:T(8,128)(2,1)S(1)} %add_convert_fusion), channel_id=1, source_target_pairs={{0,16},{8,24},{16,0},{24,8},{1,17},{9,25},{17,1},{25,9},{2,18},{10... | collective-permute-start | bytes 540680 | tf_op jit(solution)/shard_map/ppermute | solution.py:19
  51.2 7.3 %collective-permute-start.19 = (bf16[6,16,704]{2,1,0:T(8,128)(2,1)S(1)}, bf16[6,16,704]{2,1,0:T(8,128)(2,1)S(1)}, u32[]{:S(2)}, u32[]{:S(2)}) collective-permute-start(bf16[6,16,704]{2,1,0:T(8,128)(2,1)S(1)} %fusion.9), channel_id=1, source_target_pairs={{0,16},{8,24},{16,0},{24,8},{1,17},{9,25},{17,1},{25,9},{2,18},{10... | collective-permute-start | bytes 405512 | tf_op jit(solution)/shard_map/ppermute | solution.py:19
  53.0 9.8 %collective-permute-start.22 = (bf16[10,16,704]{2,1,0:T(8,128)(2,1)S(1)}, bf16[10,16,704]{2,1,0:T(8,128)(2,1)S(1)}, u32[]{:S(2)}, u32[]{:S(2)}) collective-permute-start(bf16[10,16,704]{2,1,0:T(8,128)(2,1)S(1)} %fusion.6), channel_id=1, source_target_pairs={{0,16},{8,24},{16,0},{24,8},{1,17},{9,25},{17,1},{25,9},{2,18},{10... | collective-permute-start | bytes 675848 | tf_op jit(solution)/shard_map/ppermute | solution.py:19
  62.9 10.6 %collective-permute-start.28 = (bf16[2,128,512]{2,1,0:T(8,128)(2,1)S(1)}, bf16[2,128,512]{2,1,0:T(8,128)(2,1)S(1)}, u32[]{:S(2)}, u32[]{:S(2)}) collective-permute-start(bf16[2,128,512]{2,1,0:T(8,128)(2,1)S(1)} %pad_maximum_fusion.9), channel_id=1, source_target_pairs={{0,4},{4,0},{1,5},{5,1},{2,6},{6,2},{3,7},{7,3},{8,12},{12,8},{9,1... | collective-permute-start | bytes 786440 | tf_op jit(solution)/shard_map/ppermute | solution.py:19
  68.1 11.9 %collective-permute-start.25 = (bf16[128,512]{1,0:T(8,128)(2,1)S(1)}, bf16[128,512]{1,0:T(8,128)(2,1)S(1)}, u32[]{:S(2)}, u32[]{:S(2)}) collective-permute-start(bf16[128,512]{1,0:T(8,128)(2,1)S(1)} %get-tuple-element.57), channel_id=1, source_target_pairs={{0,20},{1,28},{2,22},{3,30},{4,16},{5,24},{6,18},{7,26},{8,21},{9,... | collective-permute-start | bytes 393224 | tf_op jit(solution)/shard_map/ppermute | solution.py:297
  70.5 12.4 %collective-permute-start.26 = (bf16[128,512]{1,0:T(8,128)(2,1)S(1)}, bf16[128,512]{1,0:T(8,128)(2,1)S(1)}, u32[]{:S(2)}, u32[]{:S(2)}) collective-permute-start(bf16[128,512]{1,0:T(8,128)(2,1)S(1)} %get-tuple-element.58), channel_id=1, source_target_pairs={{0,24},{1,16},{2,26},{3,18},{4,28},{5,20},{6,30},{7,22},{8,25},{9,... | collective-permute-start | bytes 393224 | tf_op jit(solution)/shard_map/ppermute | solution.py:297
  71.7 11.2 %collective-permute-start.27 = (bf16[128,512]{1,0:T(8,128)(2,1)S(1)}, bf16[128,512]{1,0:T(8,128)(2,1)S(1)}, u32[]{:S(2)}, u32[]{:S(2)}) collective-permute-start(bf16[128,512]{1,0:T(8,128)(2,1)S(1)} %get-tuple-element.59), channel_id=1, source_target_pairs={{0,28},{1,20},{2,30},{3,22},{4,24},{5,16},{6,26},{7,18},{8,29},{9,... | collective-permute-start | bytes 393224 | tf_op jit(solution)/shard_map/ppermute | solution.py:297
  73.0 10.9 %collective-permute-start.24 = (bf16[128,512]{1,0:T(8,128)(2,1)S(1)}, bf16[128,512]{1,0:T(8,128)(2,1)S(1)}, u32[]{:S(2)}, u32[]{:S(2)}) collective-permute-start(bf16[128,512]{1,0:T(8,128)(2,1)S(1)} %get-tuple-element.56), channel_id=1, source_target_pairs={{0,16},{1,24},{2,18},{3,26},{4,20},{5,28},{6,22},{7,30},{8,17},{9,... | collective-permute-start | bytes 393224 | tf_op jit(solution)/shard_map/ppermute | solution.py:297
  79.3 4.5 %collective-permute-start.29 = (bf16[128,512]{1,0:T(8,128)(2,1)S(1)}, bf16[128,512]{1,0:T(8,128)(2,1)S(1)}, u32[]{:S(2)}, u32[]{:S(2)}) collective-permute-start(bf16[128,512]{1,0:T(8,128)(2,1)S(1)} %get-tuple-element.67), channel_id=1, source_target_pairs={{0,0},{1,8},{2,2},{3,10},{4,4},{5,12},{6,6},{7,14},{8,1},{9,9},{10... | collective-permute-start | bytes 393224 | tf_op jit(solution)/shard_map/ppermute | solution.py:297
  80.0 8.6 %collective-permute-start.30 = (bf16[128,512]{1,0:T(8,128)(2,1)S(1)}, bf16[128,512]{1,0:T(8,128)(2,1)S(1)}, u32[]{:S(2)}, u32[]{:S(2)}) collective-permute-start(bf16[128,512]{1,0:T(8,128)(2,1)S(1)} %get-tuple-element.68), channel_id=1, source_target_pairs={{0,8},{1,0},{2,10},{3,2},{4,12},{5,4},{6,14},{7,6},{8,9},{9,1},{10... | collective-permute-start | bytes 393224 | tf_op jit(solution)/shard_map/ppermute | solution.py:297
  88.8 7.6 %collective-permute-start.31 = (bf16[128,512]{1,0:T(8,128)(2,1)S(1)}, bf16[128,512]{1,0:T(8,128)(2,1)S(1)}, u32[]{:S(2)}, u32[]{:S(2)}) collective-permute-start(bf16[128,512]{1,0:T(8,128)(2,1)S(1)} %select_convert_fusion), channel_id=1, source_target_pairs={{0,2},{1,3},{2,0},{3,1},{4,6},{5,7},{6,4},{7,5},{8,10},{9,11},{10,... | collective-permute-start | bytes 393224 | tf_op jit(solution)/shard_map/ppermute | solution.py:19
  (14 other events, 50.8 us)
where the time goes:
time: 97.4 us; the launch traced here: 97.1 us
  waiting for transfers between devices  34.9 us (36%)
  starting transfers between devices  31.1 us (32%)
  Pallas kernels  18.1 us (19%)
  matrix products  4.96 us (5%)
  other arithmetic  3.66 us (4%)
  local copies, waits for them, and re-layouts  3.39 us (3%)
  between operations  1 us (1%)
    ppermute x18, waiting for transfers between devices, swap(): return lax.ppermute(value, axis, [(i, i ^ bit) for i in range(count)])  20.4 us
    ppermute x18, starting transfers between devices, swap(): return lax.ppermute(value, axis, [(i, i ^ bit) for i in range(count)])  15.1 us
    pallas_call x3, Pallas kernels, back(): pl.pallas_call(functools.partial(back_kernel, low, first, last), out_shap...  11.4 us
    ppermute x6, starting transfers between devices, to_keeper(): return lax.ppermute(value, ('dp', 'expert', 'tensor'), pairs)  8.91 us
    ppermute x8, waiting for transfers between devices, to_owner(): return lax.ppermute(value, ('dp', 'expert'), pairs)  8.78 us
    ppermute x8, starting transfers between devices, to_owner(): return lax.ppermute(value, ('dp', 'expert'), pairs)  7.08 us
    pallas_call x1, Pallas kernels, weight_grads(): pl.pallas_call(weight_kernel, grid=(local_experts // per_step,), out_shap...  5.77 us
    ppermute x6, waiting for transfers between devices, to_keeper(): return lax.ppermute(value, ('dp', 'expert', 'tensor'), pairs)  5.73 us
  transfers between devices with their start and end apart: 32, of which 15 were waited for; matrix products, arithmetic and copies ran while one was open for 7% of the time, Pallas kernels for 19%

commit v1 on v0

--- a/solution.py
+++ b/solution.py
@@ -125,7 +125,7 @@
     rows = outs[0].shape[0]
     odd = (lax.axis_index("dp") ^ lax.axis_index("tensor")) & 1
     for i in range(2):
-        which = odd ^ i
+        which = odd ^ i if low else i
         placer = placer_of(lines[low + which][0:1], held.shape[1])
         token_rows = lax.dot_general(
             placer, held[which], (((0,), (0,)), ((), ())), preferred_element_type=F32
@@ -282,8 +282,11 @@
     far_beside.append(swap(far[1], "dp", n_dp, 1))
     far_back = back(2, lines, [far[1], far_beside[1]], gate_weight, up_weight, rows, count, early)
     parts = [part, beside, jnp.concatenate(far, axis=0), jnp.concatenate(far_beside, axis=0)]
-    others = swap(jnp.stack(near_back[1::2]), "expert", n_x, 1)
-    others, after_back, _ = lax.optimization_barrier((others, placed, far_back[0]))
+    own, other, own_beside, other_beside = near_back
+    own_beside, other_beside = swap(own_beside, "dp", n_dp, 1), swap(other_beside, "dp", n_dp, 1)
+    own_beside, other_beside = lax.optimization_barrier((own_beside, other_beside))
+    arrived = swap(jnp.stack([other, other_beside]), "expert", n_x, 1)
+    arrived, after_back, _ = lax.optimization_barrier((arrived, placed, far_back[0]))
     weight_grad = weight_grads(after_back, parts, 4)
 
     def to_keeper(value, low, turn, flip):
@@ -296,11 +299,13 @@
                     pairs.append(((i * n_x + j) * n_t + l, to))
         return lax.ppermute(value, ("dp", "expert", "tensor"), pairs)
 
-    merged = [plus(own, other).astype(BF16) for own, other in zip(near_back[::2], others)]
+    merged = [plus(own, arrived[0]).astype(BF16), plus(own_beside, arrived[1]).astype(BF16)]
+    odd = ((k ^ t) & 1) == 1
+    keep, leaving = jnp.where(odd, merged[1], merged[0]), jnp.where(odd, merged[0], merged[1])
+    first = plus(keep, swap(leaving, "tensor", n_t, 1))
     far_terms = [to_keeper(value, 2, at // 2, at % 2) for at, value in enumerate(far_back)]
-    merged, _ = lax.optimization_barrier((merged, weight_grad))
-    near_terms = [to_keeper(value, 0, turn, 0) for turn, value in enumerate(merged)]
-    first, second = (sum(v.astype(F32) for v in terms) for terms in (near_terms, far_terms))
+    far_terms, _ = lax.optimization_barrier((far_terms, weight_grad))
+    second = sum(value.astype(F32) for value in far_terms)
     swapped = ((k ^ t) & 2) == 2
     keep = jnp.where(swapped, second, first)
     leaving = jnp.where(swapped, first, second).astype(BF16)

time: 97.4 us -> 97.2 us (level)
    ppermute x18 -> x21, waiting for transfers between devices: 20.4 us -> 27.3 us  [swap(): return lax.ppermute(value, axis, [(i, i ^ bit) for i in range(count)])]
    ppermute x6 -> x4, waiting for transfers between devices: 5.73 us -> 1.17 us  [to_keeper(): return lax.ppermute(value, ('dp', 'expert', 'tensor'), pairs)]
    ppermute x6 -> x4, starting transfers between devices: 8.91 us -> 5.04 us  [to_keeper(): return lax.ppermute(value, ('dp', 'expert', 'tensor'), pairs)]
    ppermute x18 -> x21, starting transfers between devices: 15.1 us -> 17.9 us  [swap(): return lax.ppermute(value, axis, [(i, i ^ bit) for i in range(count)])]
    ppermute x8, waiting for transfers between devices: 8.78 us -> 7.09 us  [to_owner(): return lax.ppermute(value, ('dp', 'expert'), pairs)]
  transfers between devices with their start and end apart: 32 -> 33, of which waited for: 15 -> 16; matrix products, arithmetic and copies ran while one was open for 7% -> 7% of each run, Pallas kernels for 19% -> 19%
where the time goes in v1:
time: 97.2 us; the launch traced here: 97 us
  waiting for transfers between devices  35.6 us (37%)
  starting transfers between devices  30.3 us (31%)
  Pallas kernels  18.1 us (19%)
  matrix products  4.95 us (5%)
  other arithmetic  3.75 us (4%)
  local copies, waits for them, and re-layouts  3.39 us (3%)
  between operations  1 us (1%)
    ppermute x21, waiting for transfers between devices, swap(): return lax.ppermute(value, axis, [(i, i ^ bit) for i in range(count)])  27.3 us
    ppermute x21, starting transfers between devices, swap(): return lax.ppermute(value, axis, [(i, i ^ bit) for i in range(count)])  17.9 us
    pallas_call x3, Pallas kernels, back(): pl.pallas_call(functools.partial(back_kernel, low, first, last), out_shap...  11.4 us
    ppermute x8, starting transfers between devices, to_owner(): return lax.ppermute(value, ('dp', 'expert'), pairs)  7.38 us
    ppermute x8, waiting for transfers between devices, to_owner(): return lax.ppermute(value, ('dp', 'expert'), pairs)  7.09 us
    pallas_call x1, Pallas kernels, weight_grads(): pl.pallas_call(weight_kernel, grid=(local_experts // per_step,), out_shap...  5.75 us
    ppermute x4, starting transfers between devices, to_keeper(): return lax.ppermute(value, ('dp', 'expert', 'tensor'), pairs)  5.04 us
    dot_general x3, matrix products, project(): jnp.einsum('esd,ehd->esh', values, weight, preferred_element_type=F32)  4.95 us
  transfers between devices with their start and end apart: 33, of which 16 were waited for; matrix products, arithmetic and copies ran while one was open for 7% of the time, Pallas kernels for 19%

profile of v1, /device:TPU:0, one launch (start us, length us, event | category | flops | bytes accessed | tf_op | source)
XLA Modules:
  0.0 97.0 jit_solution(9757644151940230324)
XLA Ops:
  3.4 3.0 %collective-permute-start = (bf16[144,512]{1,0:T(8,128)(2,1)S(1)}, bf16[144,512]{1,0:T(8,128)(2,1)S(1)}, u32[]{:S(2)}, u32[]{:S(2)}) collective-permute-start(bf16[144,512]{1,0:T(8,128)(2,1)S(1)} %get-tuple-element.96), channel_id=1, source_target_pairs={{0,16},{4,20},{8,24},{12,28},{16,0},{20,4},{24,8},{28,12},{1,17},{... | collective-permute-start | bytes 442376 | tf_op jit(solution)/shard_map/ppermute | solution.py:233
  9.3 1.8 %collective-permute-done.refs_2_ = bf16[144,512]{1,0:T(8,128)(2,1)S(1)} collective-permute-done((bf16[144,512]{1,0:T(8,128)(2,1)S(1)}, bf16[144,512]{1,0:T(8,128)(2,1)S(1)}, u32[]{:S(2)}, u32[]{:S(2)}) %collective-permute-start) | collective-permute-done | bytes 147488 | tf_op jit(solution)/shard_map/ppermute | solution.py:233
  13.5 1.7 %collective-permute-start.3 = (bf16[128,512]{1,0:T(8,128)(2,1)S(1)}, bf16[128,512]{1,0:T(8,128)(2,1)S(1)}, u32[]{:S(2)}, u32[]{:S(2)}) collective-permute-start(bf16[128,512]{1,0:T(8,128)(2,1)S(1)} %get-tuple-element.42), channel_id=1, source_target_pairs={{0,16},{4,20},{8,24},{12,28},{16,0},{20,4},{24,8},{28,12},{1,17},{... | collective-permute-start | bytes 393224 | tf_op jit(solution)/shard_map/ppermute | solution.py:233
  15.3 1.9 %collective-permute-start.7 = (bf16[144,512]{1,0:T(8,128)(2,1)S(1)}, bf16[144,512]{1,0:T(8,128)(2,1)S(1)}, u32[]{:S(2)}, u32[]{:S(2)}) collective-permute-start(bf16[144,512]{1,0:T(8,128)(2,1)S(1)} %collective-permute-done.refs_2_), channel_id=1, source_target_pairs={{0,4},{4,0},{1,5},{5,1},{2,6},{6,2},{3,7},{7,3},{8,12},{12,8},{9,1... | collective-permute-start | bytes 442376 | tf_op jit(solution)/shard_map/ppermute | solution.py:19
  17.4 2.2 %collective-permute-done.3.refs_2_ = bf16[128,512]{1,0:T(8,128)(2,1)S(1)} collective-permute-done((bf16[128,512]{1,0:T(8,128)(2,1)S(1)}, bf16[128,512]{1,0:T(8,128)(2,1)S(1)}, u32[]{:S(2)}, u32[]{:S(2)}) %collective-permute-start.3) | collective-permute-done | bytes 131104 | tf_op jit(solution)/shard_map/ppermute | solution.py:233
  22.0 2.6 %collective-permute-done.8.refs_7_ = bf16[144,512]{1,0:T(8,128)(2,1)S(1)} collective-permute-done((bf16[144,512]{1,0:T(8,128)(2,1)S(1)}, bf16[144,512]{1,0:T(8,128)(2,1)S(1)}, u32[]{:S(2)}, u32[]{:S(2)}) %collective-permute-start.8) | collective-permute-done | bytes 147488 | tf_op jit(solution)/shard_map/ppermute | solution.py:19
  24.6 1.7 %collective-permute-start.9 = (bf16[4,128,512]{2,1,0:T(8,128)(2,1)S(1)}, bf16[4,128,512]{2,1,0:T(8,128)(2,1)S(1)}, u32[]{:S(2)}, u32[]{:S(2)}) collective-permute-start(bf16[4,128,512]{2,1,0:T(8,128)(2,1)S(1)} %pad_maximum_fusion.refs_8_), channel_id=1, source_target_pairs={{0,4},{4,0},{1,5},{5,1},{2,6},{6,2},{3,7},{7,3},{8,12},{12,8},{9,1... | collective-permute-start | bytes 1572872 | tf_op jit(solution)/shard_map/ppermute | solution.py:19
  26.8 1.7 %convolution_convert_fusion.2 = bf16[16,64,352]{2,1,0:T(8,128)(2,1)S(1)} fusion(bf16[16,64,512]{2,1,0:T(8,128)(2,1)S(1)} %get-tuple-element.68.placed, bf16[16,512,352]{1,2,0:T(8,128)(2,1)S(1)} %bitcast.64), kind=kOutput, calls=%fused_computation.2 | convolution fusion | flops 369459200 | bytes 7536640 | tf_op jit(solution)/shard_map/esd,ehd->esh/dot_general | solution.py:251
  28.6 1.7 %convolution_convert_fusion.1 = bf16[16,64,352]{2,1,0:T(8,128)(2,1)S(1)} fusion(bf16[16,64,512]{2,1,0:T(8,128)(2,1)S(1)} %get-tuple-element.68.placed, bf16[16,512,352]{1,2,0:T(8,128)(2,1)S(1)} %bitcast.59), kind=kOutput, calls=%fused_computation.1 | convolution fusion | flops 369459200 | bytes 7536640 | tf_op jit(solution)/shard_map/esd,ehd->esh/dot_general | solution.py:251
  32.1 1.8 %collective-permute-start.15 = (bf16[2,16,16,352]{3,2,1,0:T(8,128)(2,1)S(1)}, bf16[2,16,16,352]{3,2,1,0:T(8,128)(2,1)S(1)}, u32[]{:S(2)}, u32[]{:S(2)}) collective-permute-start(bf16[2,16,16,352]{3,2,1,0:T(8,128)(2,1)S(1)} %pad_maximum_fusion.2.refs_6_), channel_id=1, source_target_pairs={{0,16},{8,24},{16,0},{24,8},{1,17},{9,25},{17,1},{25,9},{2,18},{10... | collective-permute-start | bytes 1081352 | tf_op jit(solution)/shard_map/ppermute | solution.py:19
  33.8 4.1 %collective-permute-done.9.refs_4_ = bf16[4,128,512]{2,1,0:T(8,128)(2,1)S(1)} collective-permute-done((bf16[4,128,512]{2,1,0:T(8,128)(2,1)S(1)}, bf16[4,128,512]{2,1,0:T(8,128)(2,1)S(1)}, u32[]{:S(2)}, u32[]{:S(2)}) %collective-permute-start.9) | collective-permute-done | bytes 524320 | tf_op jit(solution)/shard_map/ppermute | solution.py:19
  43.6 1.8 %collective-permute-start.16 = (bf16[16,16,352]{2,1,0:T(8,128)(2,1)S(1)}, bf16[16,16,352]{2,1,0:T(8,128)(2,1)S(1)}, u32[]{:S(2)}, u32[]{:S(2)}) collective-permute-start(bf16[16,16,352]{2,1,0:T(8,128)(2,1)S(1)} %add_convert_fusion), channel_id=1, source_target_pairs={{0,16},{8,24},{16,0},{24,8},{1,17},{9,25},{17,1},{25,9},{2,18},{10... | collective-permute-start | bytes 540680 | tf_op jit(solution)/shard_map/ppermute | solution.py:19
  45.4 4.7 %collective-permute-done.16 = bf16[16,16,352]{2,1,0:T(8,128)(2,1)S(1)} collective-permute-done((bf16[16,16,352]{2,1,0:T(8,128)(2,1)S(1)}, bf16[16,16,352]{2,1,0:T(8,128)(2,1)S(1)}, u32[]{:S(2)}, u32[]{:S(2)}) %collective-permute-start.16) | collective-permute-done | bytes 180256 | tf_op jit(solution)/shard_map/ppermute | solution.py:19
  50.7 1.8 %collective-permute-start.22 = (bf16[10,16,704]{2,1,0:T(8,128)(2,1)S(1)}, bf16[10,16,704]{2,1,0:T(8,128)(2,1)S(1)}, u32[]{:S(2)}, u32[]{:S(2)}) collective-permute-start(bf16[10,16,704]{2,1,0:T(8,128)(2,1)S(1)} %fusion.6), channel_id=1, source_target_pairs={{0,16},{8,24},{16,0},{24,8},{1,17},{9,25},{17,1},{25,9},{2,18},{10... | collective-permute-start | bytes 675848 | tf_op jit(solution)/shard_map/ppermute | solution.py:19
  53.0 5.0 %shard_map.87 = (bf16[128,512]{1,0:T(8,128)(2,1)S(1)}, bf16[128,512]{1,0:T(8,128)(2,1)S(1)}, bf16[128,512]{1,0:T(8,128)(2,1)S(1)}, bf16[128,512]{1,0:T(8,128)(2,1)S(1)}) custom-call(s32[4,8,256]{2,1,0:T(8,128)S(1)} %get-tuple-element.53.refs_5_.refs_0_.refs_1_, bf16[16,16,704]{2,1,0:T(8,128)(2,1)S(1)} %pad_maximum_fusion.1.refs_1_.h0, ...), custom_call_target="tpu_custom_call" | custom-call | flops 1476395008 | bytes 11534336 | tf_op jit(solution)/shard_map/pallas_call | solution.py:153
  58.1 4.3 %collective-permute-done.19.refs_0_ = bf16[6,16,704]{2,1,0:T(8,128)(2,1)S(1)} collective-permute-done((bf16[6,16,704]{2,1,0:T(8,128)(2,1)S(1)}, bf16[6,16,704]{2,1,0:T(8,128)(2,1)S(1)}, u32[]{:S(2)}, u32[]{:S(2)}) %collective-permute-start.19) | collective-permute-done | bytes 135200 | tf_op jit(solution)/shard_map/ppermute | solution.py:19
  64.2 2.6 %shard_map.88.refs_0_ = bf16[2,96,512]{2,1,0:T(8,128)(2,1)S(1)} custom-call(bf16[6,16,704]{2,1,0:T(8,128)(2,1)S(1)} %collective-permute-done.19.refs_0_, bf16[6,16,704]{2,1,0:T(8,128)(2,1)S(1)} %collective-permute-done.21.refs_1_, bf16[16,352,512]{2,1,0:T(8,128)(2,1)} %bitcast.61, bf16[16,352,512]{2,1,0:T(8,128)(2,1)} %bitcast.56), custom_call_target="tpu_custom_call" | custom-call | flops 34603008 | bytes 512 | tf_op jit(solution)/shard_map/pallas_call | solution.py:153
  68.4 3.8 %shard_map.89 = (bf16[128,512]{1,0:T(8,128)(2,1)S(1)}, bf16[128,512]{1,0:T(8,128)(2,1)S(1)}, bf16[128,512]{1,0:T(8,128)(2,1)S(1)}, bf16[128,512]{1,0:T(8,128)(2,1)S(1)}) custom-call(bf16[2,96,512]{2,1,0:T(8,128)(2,1)S(1)} %shard_map.88.refs_0_, s32[4,8,256]{2,1,0:T(8,128)S(1)} %get-tuple-element.53.refs_5_.refs_0_.refs_1_, ...), custom_call_target="tpu_custom_call" | custom-call | flops 922746880 | bytes 7208960 | tf_op jit(solution)/shard_map/pallas_call | solution.py:153
  72.2 1.7 %collective-permute-start.24 = (bf16[128,512]{1,0:T(8,128)(2,1)S(1)}, bf16[128,512]{1,0:T(8,128)(2,1)S(1)}, u32[]{:S(2)}, u32[]{:S(2)}) collective-permute-start(bf16[128,512]{1,0:T(8,128)(2,1)S(1)} %get-tuple-element.60), channel_id=1, source_target_pairs={{0,16},{1,24},{2,18},{3,26},{4,20},{5,28},{6,22},{7,30},{8,17},{9,... | collective-permute-start | bytes 393224 | tf_op jit(solution)/shard_map/ppermute | solution.py:300
  74.9 2.0 %collective-permute-start.26 = (bf16[128,512]{1,0:T(8,128)(2,1)S(1)}, bf16[128,512]{1,0:T(8,128)(2,1)S(1)}, u32[]{:S(2)}, u32[]{:S(2)}) collective-permute-start(bf16[128,512]{1,0:T(8,128)(2,1)S(1)} %get-tuple-element.62), channel_id=1, source_target_pairs={{0,24},{1,16},{2,26},{3,18},{4,28},{5,20},{6,30},{7,22},{8,25},{9,... | collective-permute-start | bytes 393224 | tf_op jit(solution)/shard_map/ppermute | solution.py:300
  77.4 1.9 %collective-permute-start.31 = (bf16[128,512]{1,0:T(8,128)(2,1)S(1)}, bf16[128,512]{1,0:T(8,128)(2,1)S(1)}, u32[]{:S(2)}, u32[]{:S(2)}) collective-permute-start(bf16[128,512]{1,0:T(8,128)(2,1)S(1)} %broadcast_select_fusion), channel_id=1, source_target_pairs={{0,1},{1,0},{2,3},{3,2},{4,5},{5,4},{6,7},{7,6},{8,9},{9,8},{10,11... | collective-permute-start | bytes 393224 | tf_op jit(solution)/shard_map/ppermute | solution.py:19
  79.3 5.7 %shard_map.90 = (bf16[16,352,512]{2,1,0:T(8,128)(2,1)}, bf16[16,352,512]{2,1,0:T(8,128)(2,1)}) custom-call(bf16[16,64,512]{2,1,0:T(8,128)(2,1)S(1)} %get-tuple-element.68.placed, bf16[16,16,704]{2,1,0:T(8,128)(2,1)S(1)} %pad_maximum_fusion.1.refs_1_.h0, bf16[16,16,704]{2,1,0:T(8,128)(2,1)S(1)} %collective-permute-done.20.refs_2_.h1, ...), custom_call_target="tpu_custom_call" | custom-call | flops 2952790016 | bytes 11534336 | tf_op jit(solution)/shard_map/pallas_call | solution.py:184
  86.5 2.7 %collective-permute-start.32 = (bf16[128,512]{1,0:T(8,128)(2,1)S(1)}, bf16[128,512]{1,0:T(8,128)(2,1)S(1)}, u32[]{:S(2)}, u32[]{:S(2)}) collective-permute-start(bf16[128,512]{1,0:T(8,128)(2,1)S(1)} %select_convert_fusion), channel_id=1, source_target_pairs={{0,2},{1,3},{2,0},{3,1},{4,6},{5,7},{6,4},{7,5},{8,10},{9,11},{10,... | collective-permute-start | bytes 393224 | tf_op jit(solution)/shard_map/ppermute | solution.py:19
  89.2 7.0 %collective-permute-done.32 = bf16[128,512]{1,0:T(8,128)(2,1)S(1)} collective-permute-done((bf16[128,512]{1,0:T(8,128)(2,1)S(1)}, bf16[128,512]{1,0:T(8,128)(2,1)S(1)}, u32[]{:S(2)}, u32[]{:S(2)}) %collective-permute-start.32) | collective-permute-done | bytes 131104 | tf_op jit(solution)/shard_map/ppermute | solution.py:19
  (91 shorter events, 27.0 us)
Async XLA Ops:
  3.4 7.7 %collective-permute-start = (bf16[144,512]{1,0:T(8,128)(2,1)S(1)}, bf16[144,512]{1,0:T(8,128)(2,1)S(1)}, u32[]{:S(2)}, u32[]{:S(2)}) collective-permute-start(bf16[144,512]{1,0:T(8,128)(2,1)S(1)} %get-tuple-element.96), channel_id=1, source_target_pairs={{0,16},{4,20},{8,24},{12,28},{16,0},{20,4},{24,8},{28,12},{1,17},{... | collective-permute-start | bytes 442376 | tf_op jit(solution)/shard_map/ppermute | solution.py:233
  6.4 6.3 %collective-permute-start.1 = (bf16[144,512]{1,0:T(8,128)(2,1)S(1)}, bf16[144,512]{1,0:T(8,128)(2,1)S(1)}, u32[]{:S(2)}, u32[]{:S(2)}) collective-permute-start(bf16[144,512]{1,0:T(8,128)(2,1)S(1)} %get-tuple-element.93), channel_id=1, source_target_pairs={{0,24},{4,28},{8,16},{12,20},{16,8},{20,12},{24,0},{28,4},{1,25},{... | collective-permute-start | bytes 442376 | tf_op jit(solution)/shard_map/ppermute | solution.py:233
  6.4 8.9 %collective-permute-start.5 = (bf16[144,512]{1,0:T(8,128)(2,1)S(1)}, bf16[144,512]{1,0:T(8,128)(2,1)S(1)}, u32[]{:S(2)}, u32[]{:S(2)}) collective-permute-start(bf16[144,512]{1,0:T(8,128)(2,1)S(1)} %get-tuple-element.94.refs_0_), channel_id=1, source_target_pairs={{0,4},{4,0},{8,12},{12,8},{16,20},{20,16},{24,28},{28,24},{1,5},{5... | collective-permute-start | bytes 442376 | tf_op jit(solution)/shard_map/ppermute | solution.py:233
  7.9 7.4 %collective-permute-start.6 = (bf16[144,512]{1,0:T(8,128)(2,1)S(1)}, bf16[144,512]{1,0:T(8,128)(2,1)S(1)}, u32[]{:S(2)}, u32[]{:S(2)}) collective-permute-start(bf16[144,512]{1,0:T(8,128)(2,1)S(1)} %get-tuple-element.95), channel_id=1, source_target_pairs={{0,12},{4,8},{8,4},{12,0},{16,28},{20,24},{24,20},{28,16},{1,13},{... | collective-permute-start | bytes 442376 | tf_op jit(solution)/shard_map/ppermute | solution.py:233
  12.7 4.7 %collective-permute-start.2 = (bf16[128,512]{1,0:T(8,128)(2,1)S(1)}, bf16[128,512]{1,0:T(8,128)(2,1)S(1)}, u32[]{:S(2)}, u32[]{:S(2)}) collective-permute-start(bf16[128,512]{1,0:T(8,128)(2,1)S(1)} %get-tuple-element.41), channel_id=1, source_target_pairs={{0,8},{4,12},{8,0},{12,4},{16,24},{20,28},{24,16},{28,20},{1,9},{5... | collective-permute-start | bytes 393224 | tf_op jit(solution)/shard_map/ppermute | solution.py:233
  13.5 6.1 %collective-permute-start.3 = (bf16[128,512]{1,0:T(8,128)(2,1)S(1)}, bf16[128,512]{1,0:T(8,128)(2,1)S(1)}, u32[]{:S(2)}, u32[]{:S(2)}) collective-permute-start(bf16[128,512]{1,0:T(8,128)(2,1)S(1)} %get-tuple-element.42), channel_id=1, source_target_pairs={{0,16},{4,20},{8,24},{12,28},{16,0},{20,4},{24,8},{28,12},{1,17},{... | collective-permute-start | bytes 393224 | tf_op jit(solution)/shard_map/ppermute | solution.py:233
  15.3 5.8 %collective-permute-start.4 = (bf16[128,512]{1,0:T(8,128)(2,1)S(1)}, bf16[128,512]{1,0:T(8,128)(2,1)S(1)}, u32[]{:S(2)}, u32[]{:S(2)}) collective-permute-start(bf16[128,512]{1,0:T(8,128)(2,1)S(1)} %get-tuple-element.43), channel_id=1, source_target_pairs={{0,24},{4,28},{8,16},{12,20},{16,8},{20,12},{24,0},{28,4},{1,25},{... | collective-permute-start | bytes 393224 | tf_op jit(solution)/shard_map/ppermute | solution.py:233
  15.3 6.7 %collective-permute-start.7 = (bf16[144,512]{1,0:T(8,128)(2,1)S(1)}, bf16[144,512]{1,0:T(8,128)(2,1)S(1)}, u32[]{:S(2)}, u32[]{:S(2)}) collective-permute-start(bf16[144,512]{1,0:T(8,128)(2,1)S(1)} %collective-permute-done.refs_2_), channel_id=1, source_target_pairs={{0,4},{4,0},{1,5},{5,1},{2,6},{6,2},{3,7},{7,3},{8,12},{12,8},{9,1... | collective-permute-start | bytes 442376 | tf_op jit(solution)/shard_map/ppermute | solution.py:19
  17.2 7.4 %collective-permute-start.8 = (bf16[144,512]{1,0:T(8,128)(2,1)S(1)}, bf16[144,512]{1,0:T(8,128)(2,1)S(1)}, u32[]{:S(2)}, u32[]{:S(2)}) collective-permute-start(bf16[144,512]{1,0:T(8,128)(2,1)S(1)} %collective-permute-done.1.refs_3_), channel_id=1, source_target_pairs={{0,4},{4,0},{1,5},{5,1},{2,6},{6,2},{3,7},{7,3},{8,12},{12,8},{9,1... | collective-permute-start | bytes 442376 | tf_op jit(solution)/shard_map/ppermute | solution.py:19
  17.4 8.9 %collective-permute-start.10 = (bf16[144,512]{1,0:T(8,128)(2,1)S(1)}, bf16[144,512]{1,0:T(8,128)(2,1)S(1)}, u32[]{:S(2)}, u32[]{:S(2)}) collective-permute-start(bf16[144,512]{1,0:T(8,128)(2,1)S(1)} %get-tuple-element.95), channel_id=1, source_target_pairs={{0,8},{4,12},{8,0},{12,4},{16,24},{20,28},{24,16},{28,20},{1,9},{5... | collective-permute-start | bytes 442376 | tf_op jit(solution)/shard_map/ppermute | solution.py:233
  24.6 13.4 %collective-permute-start.9 = (bf16[4,128,512]{2,1,0:T(8,128)(2,1)S(1)}, bf16[4,128,512]{2,1,0:T(8,128)(2,1)S(1)}, u32[]{:S(2)}, u32[]{:S(2)}) collective-permute-start(bf16[4,128,512]{2,1,0:T(8,128)(2,1)S(1)} %pad_maximum_fusion.refs_8_), channel_id=1, source_target_pairs={{0,4},{4,0},{1,5},{5,1},{2,6},{6,2},{3,7},{7,3},{8,12},{12,8},{9,1... | collective-permute-start | bytes 1572872 | tf_op jit(solution)/shard_map/ppermute | solution.py:19
  32.1 11.5 %collective-permute-start.15 = (bf16[2,16,16,352]{3,2,1,0:T(8,128)(2,1)S(1)}, bf16[2,16,16,352]{3,2,1,0:T(8,128)(2,1)S(1)}, u32[]{:S(2)}, u32[]{:S(2)}) collective-permute-start(bf16[2,16,16,352]{3,2,1,0:T(8,128)(2,1)S(1)} %pad_maximum_fusion.2.refs_6_), channel_id=1, source_target_pairs={{0,16},{8,24},{16,0},{24,8},{1,17},{9,25},{17,1},{25,9},{2,18},{10... | collective-permute-start | bytes 1081352 | tf_op jit(solution)/shard_map/ppermute | solution.py:19
  41.2 4.2 %collective-permute-start.17 = (bf16[16,16,352]{2,1,0:T(8,128)(2,1)S(1)}, bf16[16,16,352]{2,1,0:T(8,128)(2,1)S(1)}, u32[]{:S(2)}, u32[]{:S(2)}) collective-permute-start(bf16[16,16,352]{2,1,0:T(8,128)(2,1)S(1)} %get-tuple-element.79), channel_id=1, source_target_pairs={{0,8},{8,0},{16,24},{24,16},{1,9},{9,1},{17,25},{25,17},{2,10},{10... | collective-permute-start | bytes 540680 | tf_op jit(solution)/shard_map/ppermute | solution.py:19
  41.7 3.7 %collective-permute-start.18 = (bf16[16,16,352]{2,1,0:T(8,128)(2,1)S(1)}, bf16[16,16,352]{2,1,0:T(8,128)(2,1)S(1)}, u32[]{:S(2)}, u32[]{:S(2)}) collective-permute-start(bf16[16,16,352]{2,1,0:T(8,128)(2,1)S(1)} %get-tuple-element.81), channel_id=1, source_target_pairs={{0,8},{8,0},{16,24},{24,16},{1,9},{9,1},{17,25},{25,17},{2,10},{10... | collective-permute-start | bytes 540680 | tf_op jit(solution)/shard_map/ppermute | solution.py:19
  43.6 6.4 %collective-permute-start.16 = (bf16[16,16,352]{2,1,0:T(8,128)(2,1)S(1)}, bf16[16,16,352]{2,1,0:T(8,128)(2,1)S(1)}, u32[]{:S(2)}, u32[]{:S(2)}) collective-permute-start(bf16[16,16,352]{2,1,0:T(8,128)(2,1)S(1)} %add_convert_fusion), channel_id=1, source_target_pairs={{0,16},{8,24},{16,0},{24,8},{1,17},{9,25},{17,1},{25,9},{2,18},{10... | collective-permute-start | bytes 540680 | tf_op jit(solution)/shard_map/ppermute | solution.py:19
  50.7 16.1 %collective-permute-start.22 = (bf16[10,16,704]{2,1,0:T(8,128)(2,1)S(1)}, bf16[10,16,704]{2,1,0:T(8,128)(2,1)S(1)}, u32[]{:S(2)}, u32[]{:S(2)}) collective-permute-start(bf16[10,16,704]{2,1,0:T(8,128)(2,1)S(1)} %fusion.6), channel_id=1, source_target_pairs={{0,16},{8,24},{16,0},{24,8},{1,17},{9,25},{17,1},{25,9},{2,18},{10... | collective-permute-start | bytes 675848 | tf_op jit(solution)/shard_map/ppermute | solution.py:19
  52.6 9.7 %collective-permute-start.19 = (bf16[6,16,704]{2,1,0:T(8,128)(2,1)S(1)}, bf16[6,16,704]{2,1,0:T(8,128)(2,1)S(1)}, u32[]{:S(2)}, u32[]{:S(2)}) collective-permute-start(bf16[6,16,704]{2,1,0:T(8,128)(2,1)S(1)} %fusion.9), channel_id=1, source_target_pairs={{0,16},{8,24},{16,0},{24,8},{1,17},{9,25},{17,1},{25,9},{2,18},{10... | collective-permute-start | bytes 405512 | tf_op jit(solution)/shard_map/ppermute | solution.py:19
  67.1 10.2 %collective-permute-start.30 = (bf16[2,128,512]{2,1,0:T(8,128)(2,1)S(1)}, bf16[2,128,512]{2,1,0:T(8,128)(2,1)S(1)}, u32[]{:S(2)}, u32[]{:S(2)}) collective-permute-start(bf16[2,128,512]{2,1,0:T(8,128)(2,1)S(1)} %pad_maximum_fusion.9), channel_id=1, source_target_pairs={{0,4},{4,0},{1,5},{5,1},{2,6},{6,2},{3,7},{7,3},{8,12},{12,8},{9,1... | collective-permute-start | bytes 786440 | tf_op jit(solution)/shard_map/ppermute | solution.py:19
  72.2 12.8 %collective-permute-start.24 = (bf16[128,512]{1,0:T(8,128)(2,1)S(1)}, bf16[128,512]{1,0:T(8,128)(2,1)S(1)}, u32[]{:S(2)}, u32[]{:S(2)}) collective-permute-start(bf16[128,512]{1,0:T(8,128)(2,1)S(1)} %get-tuple-element.60), channel_id=1, source_target_pairs={{0,16},{1,24},{2,18},{3,26},{4,20},{5,28},{6,22},{7,30},{8,17},{9,... | collective-permute-start | bytes 393224 | tf_op jit(solution)/shard_map/ppermute | solution.py:300
  73.9 11.2 %collective-permute-start.25 = (bf16[128,512]{1,0:T(8,128)(2,1)S(1)}, bf16[128,512]{1,0:T(8,128)(2,1)S(1)}, u32[]{:S(2)}, u32[]{:S(2)}) collective-permute-start(bf16[128,512]{1,0:T(8,128)(2,1)S(1)} %get-tuple-element.61), channel_id=1, source_target_pairs={{0,20},{1,28},{2,22},{3,30},{4,16},{5,24},{6,18},{7,26},{8,21},{9,... | collective-permute-start | bytes 393224 | tf_op jit(solution)/shard_map/ppermute | solution.py:300
  74.9 11.3 %collective-permute-start.26 = (bf16[128,512]{1,0:T(8,128)(2,1)S(1)}, bf16[128,512]{1,0:T(8,128)(2,1)S(1)}, u32[]{:S(2)}, u32[]{:S(2)}) collective-permute-start(bf16[128,512]{1,0:T(8,128)(2,1)S(1)} %get-tuple-element.62), channel_id=1, source_target_pairs={{0,24},{1,16},{2,26},{3,18},{4,28},{5,20},{6,30},{7,22},{8,25},{9,... | collective-permute-start | bytes 393224 | tf_op jit(solution)/shard_map/ppermute | solution.py:300
  76.9 9.3 %collective-permute-start.27 = (bf16[128,512]{1,0:T(8,128)(2,1)S(1)}, bf16[128,512]{1,0:T(8,128)(2,1)S(1)}, u32[]{:S(2)}, u32[]{:S(2)}) collective-permute-start(bf16[128,512]{1,0:T(8,128)(2,1)S(1)} %get-tuple-element.63), channel_id=1, source_target_pairs={{0,28},{1,20},{2,30},{3,22},{4,24},{5,16},{6,26},{7,18},{8,29},{9,... | collective-permute-start | bytes 393224 | tf_op jit(solution)/shard_map/ppermute | solution.py:300
  77.4 8.9 %collective-permute-start.31 = (bf16[128,512]{1,0:T(8,128)(2,1)S(1)}, bf16[128,512]{1,0:T(8,128)(2,1)S(1)}, u32[]{:S(2)}, u32[]{:S(2)}) collective-permute-start(bf16[128,512]{1,0:T(8,128)(2,1)S(1)} %broadcast_select_fusion), channel_id=1, source_target_pairs={{0,1},{1,0},{2,3},{3,2},{4,5},{5,4},{6,7},{7,6},{8,9},{9,8},{10,11... | collective-permute-start | bytes 393224 | tf_op jit(solution)/shard_map/ppermute | solution.py:19
  86.5 9.7 %collective-permute-start.32 = (bf16[128,512]{1,0:T(8,128)(2,1)S(1)}, bf16[128,512]{1,0:T(8,128)(2,1)S(1)}, u32[]{:S(2)}, u32[]{:S(2)}) collective-permute-start(bf16[128,512]{1,0:T(8,128)(2,1)S(1)} %select_convert_fusion), channel_id=1, source_target_pairs={{0,2},{1,3},{2,0},{3,1},{4,6},{5,7},{6,4},{7,5},{8,10},{9,11},{10,... | collective-permute-start | bytes 393224 | tf_op jit(solution)/shard_map/ppermute | solution.py:19
  (15 other events, 54.0 us)

commit v2 on v1

--- a/solution.py
+++ b/solution.py
@@ -271,7 +271,7 @@
     gate_factor = up_act * sigmoid_gate * (1.0 + gate_act * (1.0 - sigmoid_gate))
     hidden_grad = plus(hidden_near, swap(hidden_far, "dp", n_dp, 2))
     part = jnp.concatenate([hidden_grad * gate_factor, hidden_grad * up_factor], axis=2).astype(BF16)
-    count = local_experts * 3 // 8
+    count = local_experts * 7 // 16
     far = [swap(piece, "dp", n_dp, 2) for piece in jnp.split(part, [count], axis=0)]
     beside = swap(part, "dp", n_dp, 1)
     near_back = back(0, lines, [part, beside], gate_weight, up_weight, rows)

time: 97.2 us -> 93.1 us (0.958)
  waiting for transfers between devices: 35.6 us -> 31.2 us
    ppermute x21, waiting for transfers between devices: 27.3 us -> 23 us  [swap(): return lax.ppermute(value, axis, [(i, i ^ bit) for i in range(count)])]
  transfers between devices with their start and end apart: 33 -> 33, of which waited for: 16 -> 16; matrix products, arithmetic and copies ran while one was open for 7% -> 7% of each run, Pallas kernels for 19% -> 20%
where the time goes in v2:
time: 93.1 us; the launch traced here: 92.9 us
  waiting for transfers between devices  31.2 us (34%)
  starting transfers between devices  30.4 us (33%)
  Pallas kernels  18.2 us (20%)
  matrix products  4.95 us (5%)
  other arithmetic  3.76 us (4%)
  local copies, waits for them, and re-layouts  3.39 us (4%)
  between operations  1.01 us (1%)
    ppermute x21, waiting for transfers between devices, swap(): return lax.ppermute(value, axis, [(i, i ^ bit) for i in range(count)])  23 us
    ppermute x21, starting transfers between devices, swap(): return lax.ppermute(value, axis, [(i, i ^ bit) for i in range(count)])  18 us
    pallas_call x3, Pallas kernels, back(): pl.pallas_call(functools.partial(back_kernel, low, first, last), out_shap...  11.6 us
    ppermute x8, starting transfers between devices, to_owner(): return lax.ppermute(value, ('dp', 'expert'), pairs)  7.38 us
    ppermute x8, waiting for transfers between devices, to_owner(): return lax.ppermute(value, ('dp', 'expert'), pairs)  7.09 us
    pallas_call x1, Pallas kernels, weight_grads(): pl.pallas_call(weight_kernel, grid=(local_experts // per_step,), out_shap...  5.75 us
    ppermute x4, starting transfers between devices, to_keeper(): return lax.ppermute(value, ('dp', 'expert', 'tensor'), pairs)  5.01 us
    dot_general x3, matrix products, project(): jnp.einsum('esd,ehd->esh', values, weight, preferred_element_type=F32)  4.95 us
  transfers between devices with their start and end apart: 33, of which 16 were waited for; matrix products, arithmetic and copies ran while one was open for 7% of the time, Pallas kernels for 20%

profile of v2, /device:TPU:0, one launch (start us, length us, event | category | flops | bytes accessed | tf_op | source)
XLA Modules:
  0.0 92.9 jit_solution(8897153796075760050)
XLA Ops:
  3.4 3.0 %collective-permute-start = (bf16[144,512]{1,0:T(8,128)(2,1)S(1)}, bf16[144,512]{1,0:T(8,128)(2,1)S(1)}, u32[]{:S(2)}, u32[]{:S(2)}) collective-permute-start(bf16[144,512]{1,0:T(8,128)(2,1)S(1)} %get-tuple-element.96), channel_id=1, source_target_pairs={{0,16},{4,20},{8,24},{12,28},{16,0},{20,4},{24,8},{28,12},{1,17},{... | collective-permute-start | bytes 442376 | tf_op jit(solution)/shard_map/ppermute | solution.py:233
  9.3 1.8 %collective-permute-done.refs_2_ = bf16[144,512]{1,0:T(8,128)(2,1)S(1)} collective-permute-done((bf16[144,512]{1,0:T(8,128)(2,1)S(1)}, bf16[144,512]{1,0:T(8,128)(2,1)S(1)}, u32[]{:S(2)}, u32[]{:S(2)}) %collective-permute-start) | collective-permute-done | bytes 147488 | tf_op jit(solution)/shard_map/ppermute | solution.py:233
  13.5 1.7 %collective-permute-start.3 = (bf16[128,512]{1,0:T(8,128)(2,1)S(1)}, bf16[128,512]{1,0:T(8,128)(2,1)S(1)}, u32[]{:S(2)}, u32[]{:S(2)}) collective-permute-start(bf16[128,512]{1,0:T(8,128)(2,1)S(1)} %get-tuple-element.42), channel_id=1, source_target_pairs={{0,16},{4,20},{8,24},{12,28},{16,0},{20,4},{24,8},{28,12},{1,17},{... | collective-permute-start | bytes 393224 | tf_op jit(solution)/shard_map/ppermute | solution.py:233
  15.3 1.9 %collective-permute-start.7 = (bf16[144,512]{1,0:T(8,128)(2,1)S(1)}, bf16[144,512]{1,0:T(8,128)(2,1)S(1)}, u32[]{:S(2)}, u32[]{:S(2)}) collective-permute-start(bf16[144,512]{1,0:T(8,128)(2,1)S(1)} %collective-permute-done.refs_2_), channel_id=1, source_target_pairs={{0,4},{4,0},{1,5},{5,1},{2,6},{6,2},{3,7},{7,3},{8,12},{12,8},{9,1... | collective-permute-start | bytes 442376 | tf_op jit(solution)/shard_map/ppermute | solution.py:19
  17.4 2.2 %collective-permute-done.3.refs_2_ = bf16[128,512]{1,0:T(8,128)(2,1)S(1)} collective-permute-done((bf16[128,512]{1,0:T(8,128)(2,1)S(1)}, bf16[128,512]{1,0:T(8,128)(2,1)S(1)}, u32[]{:S(2)}, u32[]{:S(2)}) %collective-permute-start.3) | collective-permute-done | bytes 131104 | tf_op jit(solution)/shard_map/ppermute | solution.py:233
  22.0 2.6 %collective-permute-done.8.refs_7_ = bf16[144,512]{1,0:T(8,128)(2,1)S(1)} collective-permute-done((bf16[144,512]{1,0:T(8,128)(2,1)S(1)}, bf16[144,512]{1,0:T(8,128)(2,1)S(1)}, u32[]{:S(2)}, u32[]{:S(2)}) %collective-permute-start.8) | collective-permute-done | bytes 147488 | tf_op jit(solution)/shard_map/ppermute | solution.py:19
  24.6 1.7 %collective-permute-start.9 = (bf16[4,128,512]{2,1,0:T(8,128)(2,1)S(1)}, bf16[4,128,512]{2,1,0:T(8,128)(2,1)S(1)}, u32[]{:S(2)}, u32[]{:S(2)}) collective-permute-start(bf16[4,128,512]{2,1,0:T(8,128)(2,1)S(1)} %pad_maximum_fusion.refs_8_), channel_id=1, source_target_pairs={{0,4},{4,0},{1,5},{5,1},{2,6},{6,2},{3,7},{7,3},{8,12},{12,8},{9,1... | collective-permute-start | bytes 1572872 | tf_op jit(solution)/shard_map/ppermute | solution.py:19
  26.8 1.7 %convolution_convert_fusion.2 = bf16[16,64,352]{2,1,0:T(8,128)(2,1)S(1)} fusion(bf16[16,64,512]{2,1,0:T(8,128)(2,1)S(1)} %get-tuple-element.68.placed, bf16[16,512,352]{1,2,0:T(8,128)(2,1)S(1)} %bitcast.64), kind=kOutput, calls=%fused_computation.2 | convolution fusion | flops 369459200 | bytes 7536640 | tf_op jit(solution)/shard_map/esd,ehd->esh/dot_general | solution.py:251
  28.6 1.7 %convolution_convert_fusion.1 = bf16[16,64,352]{2,1,0:T(8,128)(2,1)S(1)} fusion(bf16[16,64,512]{2,1,0:T(8,128)(2,1)S(1)} %get-tuple-element.68.placed, bf16[16,512,352]{1,2,0:T(8,128)(2,1)S(1)} %bitcast.59), kind=kOutput, calls=%fused_computation.1 | convolution fusion | flops 369459200 | bytes 7536640 | tf_op jit(solution)/shard_map/esd,ehd->esh/dot_general | solution.py:251
  32.1 1.8 %collective-permute-start.15 = (bf16[2,16,16,352]{3,2,1,0:T(8,128)(2,1)S(1)}, bf16[2,16,16,352]{3,2,1,0:T(8,128)(2,1)S(1)}, u32[]{:S(2)}, u32[]{:S(2)}) collective-permute-start(bf16[2,16,16,352]{3,2,1,0:T(8,128)(2,1)S(1)} %pad_maximum_fusion.2.refs_6_), channel_id=1, source_target_pairs={{0,16},{8,24},{16,0},{24,8},{1,17},{9,25},{17,1},{25,9},{2,18},{10... | collective-permute-start | bytes 1081352 | tf_op jit(solution)/shard_map/ppermute | solution.py:19
  33.8 4.1 %collective-permute-done.9.refs_4_ = bf16[4,128,512]{2,1,0:T(8,128)(2,1)S(1)} collective-permute-done((bf16[4,128,512]{2,1,0:T(8,128)(2,1)S(1)}, bf16[4,128,512]{2,1,0:T(8,128)(2,1)S(1)}, u32[]{:S(2)}, u32[]{:S(2)}) %collective-permute-start.9) | collective-permute-done | bytes 524320 | tf_op jit(solution)/shard_map/ppermute | solution.py:19
  39.4 1.6 %convolution_convert_fusion = bf16[16,64,352]{2,1,0:T(8,128)(2,1)S(1)} fusion(bf16[16,64,512]{2,1,0:T(8,128)(2,1)S(1)} %shard_map.86, bf16[16,512,352]{1,2,0:T(8,128)(2,1)S(1)} %bitcast.66), kind=kOutput, calls=%fused_computation | convolution fusion | flops 369459200 | bytes 7536640 | tf_op jit(solution)/shard_map/esd,ehd->esh/dot_general | solution.py:251
  43.6 1.8 %collective-permute-start.16 = (bf16[16,16,352]{2,1,0:T(8,128)(2,1)S(1)}, bf16[16,16,352]{2,1,0:T(8,128)(2,1)S(1)}, u32[]{:S(2)}, u32[]{:S(2)}) collective-permute-start(bf16[16,16,352]{2,1,0:T(8,128)(2,1)S(1)} %add_convert_fusion), channel_id=1, source_target_pairs={{0,16},{8,24},{16,0},{24,8},{1,17},{9,25},{17,1},{25,9},{2,18},{10... | collective-permute-start | bytes 540680 | tf_op jit(solution)/shard_map/ppermute | solution.py:19
  45.4 4.7 %collective-permute-done.16 = bf16[16,16,352]{2,1,0:T(8,128)(2,1)S(1)} collective-permute-done((bf16[16,16,352]{2,1,0:T(8,128)(2,1)S(1)}, bf16[16,16,352]{2,1,0:T(8,128)(2,1)S(1)}, u32[]{:S(2)}, u32[]{:S(2)}) %collective-permute-start.16) | collective-permute-done | bytes 180256 | tf_op jit(solution)/shard_map/ppermute | solution.py:19
  50.7 1.8 %collective-permute-start.19 = (bf16[7,16,704]{2,1,0:T(8,128)(2,1)S(1)}, bf16[7,16,704]{2,1,0:T(8,128)(2,1)S(1)}, u32[]{:S(2)}, u32[]{:S(2)}) collective-permute-start(bf16[7,16,704]{2,1,0:T(8,128)(2,1)S(1)} %fusion.9), channel_id=1, source_target_pairs={{0,16},{8,24},{16,0},{24,8},{1,17},{9,25},{17,1},{25,9},{2,18},{10... | collective-permute-start | bytes 473096 | tf_op jit(solution)/shard_map/ppermute | solution.py:19
  53.0 5.0 %shard_map.87 = (bf16[128,512]{1,0:T(8,128)(2,1)S(1)}, bf16[128,512]{1,0:T(8,128)(2,1)S(1)}, bf16[128,512]{1,0:T(8,128)(2,1)S(1)}, bf16[128,512]{1,0:T(8,128)(2,1)S(1)}) custom-call(s32[4,8,256]{2,1,0:T(8,128)S(1)} %get-tuple-element.53.refs_5_.refs_0_.refs_1_, bf16[16,16,704]{2,1,0:T(8,128)(2,1)S(1)} %pad_maximum_fusion.1.refs_1_.h0, ...), custom_call_target="tpu_custom_call" | custom-call | flops 1476395008 | bytes 11534336 | tf_op jit(solution)/shard_map/pallas_call | solution.py:153
  60.0 2.9 %shard_map.88.refs_0_ = bf16[2,112,512]{2,1,0:T(8,128)(2,1)S(1)} custom-call(bf16[7,16,704]{2,1,0:T(8,128)(2,1)S(1)} %collective-permute-done.19.refs_0_, bf16[7,16,704]{2,1,0:T(8,128)(2,1)S(1)} %collective-permute-done.21.refs_1_, bf16[16,352,512]{2,1,0:T(8,128)(2,1)} %bitcast.61, bf16[16,352,512]{2,1,0:T(8,128)(2,1)} %bitcast.56), custom_call_target="tpu_custom_call" | custom-call | flops 40370176 | bytes 512 | tf_op jit(solution)/shard_map/pallas_call | solution.py:153
  64.5 3.7 %shard_map.89 = (bf16[128,512]{1,0:T(8,128)(2,1)S(1)}, bf16[128,512]{1,0:T(8,128)(2,1)S(1)}, bf16[128,512]{1,0:T(8,128)(2,1)S(1)}, bf16[128,512]{1,0:T(8,128)(2,1)S(1)}) custom-call(bf16[2,112,512]{2,1,0:T(8,128)(2,1)S(1)} %shard_map.88.refs_0_, s32[4,8,256]{2,1,0:T(8,128)S(1)} %get-tuple-element.53.refs_5_.refs_0_.refs_1_, ...), custom_call_target="tpu_custom_call" | custom-call | flops 830472192 | bytes 6488064 | tf_op jit(solution)/shard_map/pallas_call | solution.py:153
  68.2 1.7 %collective-permute-start.24 = (bf16[128,512]{1,0:T(8,128)(2,1)S(1)}, bf16[128,512]{1,0:T(8,128)(2,1)S(1)}, u32[]{:S(2)}, u32[]{:S(2)}) collective-permute-start(bf16[128,512]{1,0:T(8,128)(2,1)S(1)} %get-tuple-element.60), channel_id=1, source_target_pairs={{0,16},{1,24},{2,18},{3,26},{4,20},{5,28},{6,22},{7,30},{8,17},{9,... | collective-permute-start | bytes 393224 | tf_op jit(solution)/shard_map/ppermute | solution.py:300
  70.9 2.0 %collective-permute-start.26 = (bf16[128,512]{1,0:T(8,128)(2,1)S(1)}, bf16[128,512]{1,0:T(8,128)(2,1)S(1)}, u32[]{:S(2)}, u32[]{:S(2)}) collective-permute-start(bf16[128,512]{1,0:T(8,128)(2,1)S(1)} %get-tuple-element.62), channel_id=1, source_target_pairs={{0,24},{1,16},{2,26},{3,18},{4,28},{5,20},{6,30},{7,22},{8,25},{9,... | collective-permute-start | bytes 393224 | tf_op jit(solution)/shard_map/ppermute | solution.py:300
  73.3 1.9 %collective-permute-start.31 = (bf16[128,512]{1,0:T(8,128)(2,1)S(1)}, bf16[128,512]{1,0:T(8,128)(2,1)S(1)}, u32[]{:S(2)}, u32[]{:S(2)}) collective-permute-start(bf16[128,512]{1,0:T(8,128)(2,1)S(1)} %broadcast_select_fusion), channel_id=1, source_target_pairs={{0,1},{1,0},{2,3},{3,2},{4,5},{5,4},{6,7},{7,6},{8,9},{9,8},{10,11... | collective-permute-start | bytes 393224 | tf_op jit(solution)/shard_map/ppermute | solution.py:19
  75.3 5.8 %shard_map.90 = (bf16[16,352,512]{2,1,0:T(8,128)(2,1)}, bf16[16,352,512]{2,1,0:T(8,128)(2,1)}) custom-call(bf16[16,64,512]{2,1,0:T(8,128)(2,1)S(1)} %get-tuple-element.68.placed, bf16[16,16,704]{2,1,0:T(8,128)(2,1)S(1)} %pad_maximum_fusion.1.refs_1_.h0, bf16[16,16,704]{2,1,0:T(8,128)(2,1)S(1)} %collective-permute-done.20.refs_2_.h1, ...), custom_call_target="tpu_custom_call" | custom-call | flops 2952790016 | bytes 11534336 | tf_op jit(solution)/shard_map/pallas_call | solution.py:184
  82.4 2.6 %collective-permute-start.32 = (bf16[128,512]{1,0:T(8,128)(2,1)S(1)}, bf16[128,512]{1,0:T(8,128)(2,1)S(1)}, u32[]{:S(2)}, u32[]{:S(2)}) collective-permute-start(bf16[128,512]{1,0:T(8,128)(2,1)S(1)} %select_convert_fusion), channel_id=1, source_target_pairs={{0,2},{1,3},{2,0},{3,1},{4,6},{5,7},{6,4},{7,5},{8,10},{9,11},{10,... | collective-permute-start | bytes 393224 | tf_op jit(solution)/shard_map/ppermute | solution.py:19
  85.1 7.0 %collective-permute-done.32 = bf16[128,512]{1,0:T(8,128)(2,1)S(1)} collective-permute-done((bf16[128,512]{1,0:T(8,128)(2,1)S(1)}, bf16[128,512]{1,0:T(8,128)(2,1)S(1)}, u32[]{:S(2)}, u32[]{:S(2)}) %collective-permute-start.32) | collective-permute-done | bytes 131104 | tf_op jit(solution)/shard_map/ppermute | solution.py:19
  (91 shorter events, 25.4 us)
Async XLA Ops:
  3.4 7.7 %collective-permute-start = (bf16[144,512]{1,0:T(8,128)(2,1)S(1)}, bf16[144,512]{1,0:T(8,128)(2,1)S(1)}, u32[]{:S(2)}, u32[]{:S(2)}) collective-permute-start(bf16[144,512]{1,0:T(8,128)(2,1)S(1)} %get-tuple-element.96), channel_id=1, source_target_pairs={{0,16},{4,20},{8,24},{12,28},{16,0},{20,4},{24,8},{28,12},{1,17},{... | collective-permute-start | bytes 442376 | tf_op jit(solution)/shard_map/ppermute | solution.py:233
  6.4 6.3 %collective-permute-start.1 = (bf16[144,512]{1,0:T(8,128)(2,1)S(1)}, bf16[144,512]{1,0:T(8,128)(2,1)S(1)}, u32[]{:S(2)}, u32[]{:S(2)}) collective-permute-start(bf16[144,512]{1,0:T(8,128)(2,1)S(1)} %get-tuple-element.93), channel_id=1, source_target_pairs={{0,24},{4,28},{8,16},{12,20},{16,8},{20,12},{24,0},{28,4},{1,25},{... | collective-permute-start | bytes 442376 | tf_op jit(solution)/shard_map/ppermute | solution.py:233
  6.4 8.9 %collective-permute-start.5 = (bf16[144,512]{1,0:T(8,128)(2,1)S(1)}, bf16[144,512]{1,0:T(8,128)(2,1)S(1)}, u32[]{:S(2)}, u32[]{:S(2)}) collective-permute-start(bf16[144,512]{1,0:T(8,128)(2,1)S(1)} %get-tuple-element.94.refs_0_), channel_id=1, source_target_pairs={{0,4},{4,0},{8,12},{12,8},{16,20},{20,16},{24,28},{28,24},{1,5},{5... | collective-permute-start | bytes 442376 | tf_op jit(solution)/shard_map/ppermute | solution.py:233
  7.9 7.4 %collective-permute-start.6 = (bf16[144,512]{1,0:T(8,128)(2,1)S(1)}, bf16[144,512]{1,0:T(8,128)(2,1)S(1)}, u32[]{:S(2)}, u32[]{:S(2)}) collective-permute-start(bf16[144,512]{1,0:T(8,128)(2,1)S(1)} %get-tuple-element.95), channel_id=1, source_target_pairs={{0,12},{4,8},{8,4},{12,0},{16,28},{20,24},{24,20},{28,16},{1,13},{... | collective-permute-start | bytes 442376 | tf_op jit(solution)/shard_map/ppermute | solution.py:233
  12.7 4.7 %collective-permute-start.2 = (bf16[128,512]{1,0:T(8,128)(2,1)S(1)}, bf16[128,512]{1,0:T(8,128)(2,1)S(1)}, u32[]{:S(2)}, u32[]{:S(2)}) collective-permute-start(bf16[128,512]{1,0:T(8,128)(2,1)S(1)} %get-tuple-element.41), channel_id=1, source_target_pairs={{0,8},{4,12},{8,0},{12,4},{16,24},{20,28},{24,16},{28,20},{1,9},{5... | collective-permute-start | bytes 393224 | tf_op jit(solution)/shard_map/ppermute | solution.py:233
  13.5 6.1 %collective-permute-start.3 = (bf16[128,512]{1,0:T(8,128)(2,1)S(1)}, bf16[128,512]{1,0:T(8,128)(2,1)S(1)}, u32[]{:S(2)}, u32[]{:S(2)}) collective-permute-start(bf16[128,512]{1,0:T(8,128)(2,1)S(1)} %get-tuple-element.42), channel_id=1, source_target_pairs={{0,16},{4,20},{8,24},{12,28},{16,0},{20,4},{24,8},{28,12},{1,17},{... | collective-permute-start | bytes 393224 | tf_op jit(solution)/shard_map/ppermute | solution.py:233
  15.3 5.8 %collective-permute-start.4 = (bf16[128,512]{1,0:T(8,128)(2,1)S(1)}, bf16[128,512]{1,0:T(8,128)(2,1)S(1)}, u32[]{:S(2)}, u32[]{:S(2)}) collective-permute-start(bf16[128,512]{1,0:T(8,128)(2,1)S(1)} %get-tuple-element.43), channel_id=1, source_target_pairs={{0,24},{4,28},{8,16},{12,20},{16,8},{20,12},{24,0},{28,4},{1,25},{... | collective-permute-start | bytes 393224 | tf_op jit(solution)/shard_map/ppermute | solution.py:233
  15.3 6.7 %collective-permute-start.7 = (bf16[144,512]{1,0:T(8,128)(2,1)S(1)}, bf16[144,512]{1,0:T(8,128)(2,1)S(1)}, u32[]{:S(2)}, u32[]{:S(2)}) collective-permute-start(bf16[144,512]{1,0:T(8,128)(2,1)S(1)} %collective-permute-done.refs_2_), channel_id=1, source_target_pairs={{0,4},{4,0},{1,5},{5,1},{2,6},{6,2},{3,7},{7,3},{8,12},{12,8},{9,1... | collective-permute-start | bytes 442376 | tf_op jit(solution)/shard_map/ppermute | solution.py:19
  17.2 7.4 %collective-permute-start.8 = (bf16[144,512]{1,0:T(8,128)(2,1)S(1)}, bf16[144,512]{1,0:T(8,128)(2,1)S(1)}, u32[]{:S(2)}, u32[]{:S(2)}) collective-permute-start(bf16[144,512]{1,0:T(8,128)(2,1)S(1)} %collective-permute-done.1.refs_3_), channel_id=1, source_target_pairs={{0,4},{4,0},{1,5},{5,1},{2,6},{6,2},{3,7},{7,3},{8,12},{12,8},{9,1... | collective-permute-start | bytes 442376 | tf_op jit(solution)/shard_map/ppermute | solution.py:19
  17.4 8.9 %collective-permute-start.10 = (bf16[144,512]{1,0:T(8,128)(2,1)S(1)}, bf16[144,512]{1,0:T(8,128)(2,1)S(1)}, u32[]{:S(2)}, u32[]{:S(2)}) collective-permute-start(bf16[144,512]{1,0:T(8,128)(2,1)S(1)} %get-tuple-element.95), channel_id=1, source_target_pairs={{0,8},{4,12},{8,0},{12,4},{16,24},{20,28},{24,16},{28,20},{1,9},{5... | collective-permute-start | bytes 442376 | tf_op jit(solution)/shard_map/ppermute | solution.py:233
  24.6 13.4 %collective-permute-start.9 = (bf16[4,128,512]{2,1,0:T(8,128)(2,1)S(1)}, bf16[4,128,512]{2,1,0:T(8,128)(2,1)S(1)}, u32[]{:S(2)}, u32[]{:S(2)}) collective-permute-start(bf16[4,128,512]{2,1,0:T(8,128)(2,1)S(1)} %pad_maximum_fusion.refs_8_), channel_id=1, source_target_pairs={{0,4},{4,0},{1,5},{5,1},{2,6},{6,2},{3,7},{7,3},{8,12},{12,8},{9,1... | collective-permute-start | bytes 1572872 | tf_op jit(solution)/shard_map/ppermute | solution.py:19
  32.1 11.5 %collective-permute-start.15 = (bf16[2,16,16,352]{3,2,1,0:T(8,128)(2,1)S(1)}, bf16[2,16,16,352]{3,2,1,0:T(8,128)(2,1)S(1)}, u32[]{:S(2)}, u32[]{:S(2)}) collective-permute-start(bf16[2,16,16,352]{3,2,1,0:T(8,128)(2,1)S(1)} %pad_maximum_fusion.2.refs_6_), channel_id=1, source_target_pairs={{0,16},{8,24},{16,0},{24,8},{1,17},{9,25},{17,1},{25,9},{2,18},{10... | collective-permute-start | bytes 1081352 | tf_op jit(solution)/shard_map/ppermute | solution.py:19
  41.2 4.2 %collective-permute-start.17 = (bf16[16,16,352]{2,1,0:T(8,128)(2,1)S(1)}, bf16[16,16,352]{2,1,0:T(8,128)(2,1)S(1)}, u32[]{:S(2)}, u32[]{:S(2)}) collective-permute-start(bf16[16,16,352]{2,1,0:T(8,128)(2,1)S(1)} %get-tuple-element.79), channel_id=1, source_target_pairs={{0,8},{8,0},{16,24},{24,16},{1,9},{9,1},{17,25},{25,17},{2,10},{10... | collective-permute-start | bytes 540680 | tf_op jit(solution)/shard_map/ppermute | solution.py:19
  41.7 3.7 %collective-permute-start.18 = (bf16[16,16,352]{2,1,0:T(8,128)(2,1)S(1)}, bf16[16,16,352]{2,1,0:T(8,128)(2,1)S(1)}, u32[]{:S(2)}, u32[]{:S(2)}) collective-permute-start(bf16[16,16,352]{2,1,0:T(8,128)(2,1)S(1)} %get-tuple-element.81), channel_id=1, source_target_pairs={{0,8},{8,0},{16,24},{24,16},{1,9},{9,1},{17,25},{25,17},{2,10},{10... | collective-permute-start | bytes 540680 | tf_op jit(solution)/shard_map/ppermute | solution.py:19
  43.6 6.4 %collective-permute-start.16 = (bf16[16,16,352]{2,1,0:T(8,128)(2,1)S(1)}, bf16[16,16,352]{2,1,0:T(8,128)(2,1)S(1)}, u32[]{:S(2)}, u32[]{:S(2)}) collective-permute-start(bf16[16,16,352]{2,1,0:T(8,128)(2,1)S(1)} %add_convert_fusion), channel_id=1, source_target_pairs={{0,16},{8,24},{16,0},{24,8},{1,17},{9,25},{17,1},{25,9},{2,18},{10... | collective-permute-start | bytes 540680 | tf_op jit(solution)/shard_map/ppermute | solution.py:19
  50.7 7.3 %collective-permute-start.19 = (bf16[7,16,704]{2,1,0:T(8,128)(2,1)S(1)}, bf16[7,16,704]{2,1,0:T(8,128)(2,1)S(1)}, u32[]{:S(2)}, u32[]{:S(2)}) collective-permute-start(bf16[7,16,704]{2,1,0:T(8,128)(2,1)S(1)} %fusion.9), channel_id=1, source_target_pairs={{0,16},{8,24},{16,0},{24,8},{1,17},{9,25},{17,1},{25,9},{2,18},{10... | collective-permute-start | bytes 473096 | tf_op jit(solution)/shard_map/ppermute | solution.py:19
  52.6 10.3 %collective-permute-start.22 = (bf16[9,16,704]{2,1,0:T(8,128)(2,1)S(1)}, bf16[9,16,704]{2,1,0:T(8,128)(2,1)S(1)}, u32[]{:S(2)}, u32[]{:S(2)}) collective-permute-start(bf16[9,16,704]{2,1,0:T(8,128)(2,1)S(1)} %fusion.6), channel_id=1, source_target_pairs={{0,16},{8,24},{16,0},{24,8},{1,17},{9,25},{17,1},{25,9},{2,18},{10... | collective-permute-start | bytes 608264 | tf_op jit(solution)/shard_map/ppermute | solution.py:19
  63.2 10.1 %collective-permute-start.30 = (bf16[2,128,512]{2,1,0:T(8,128)(2,1)S(1)}, bf16[2,128,512]{2,1,0:T(8,128)(2,1)S(1)}, u32[]{:S(2)}, u32[]{:S(2)}) collective-permute-start(bf16[2,128,512]{2,1,0:T(8,128)(2,1)S(1)} %pad_maximum_fusion.9), channel_id=1, source_target_pairs={{0,4},{4,0},{1,5},{5,1},{2,6},{6,2},{3,7},{7,3},{8,12},{12,8},{9,1... | collective-permute-start | bytes 786440 | tf_op jit(solution)/shard_map/ppermute | solution.py:19
  68.2 13.1 %collective-permute-start.24 = (bf16[128,512]{1,0:T(8,128)(2,1)S(1)}, bf16[128,512]{1,0:T(8,128)(2,1)S(1)}, u32[]{:S(2)}, u32[]{:S(2)}) collective-permute-start(bf16[128,512]{1,0:T(8,128)(2,1)S(1)} %get-tuple-element.60), channel_id=1, source_target_pairs={{0,16},{1,24},{2,18},{3,26},{4,20},{5,28},{6,22},{7,30},{8,17},{9,... | collective-permute-start | bytes 393224 | tf_op jit(solution)/shard_map/ppermute | solution.py:300
  69.9 11.4 %collective-permute-start.25 = (bf16[128,512]{1,0:T(8,128)(2,1)S(1)}, bf16[128,512]{1,0:T(8,128)(2,1)S(1)}, u32[]{:S(2)}, u32[]{:S(2)}) collective-permute-start(bf16[128,512]{1,0:T(8,128)(2,1)S(1)} %get-tuple-element.61), channel_id=1, source_target_pairs={{0,20},{1,28},{2,22},{3,30},{4,16},{5,24},{6,18},{7,26},{8,21},{9,... | collective-permute-start | bytes 393224 | tf_op jit(solution)/shard_map/ppermute | solution.py:300
  70.9 11.3 %collective-permute-start.26 = (bf16[128,512]{1,0:T(8,128)(2,1)S(1)}, bf16[128,512]{1,0:T(8,128)(2,1)S(1)}, u32[]{:S(2)}, u32[]{:S(2)}) collective-permute-start(bf16[128,512]{1,0:T(8,128)(2,1)S(1)} %get-tuple-element.62), channel_id=1, source_target_pairs={{0,24},{1,16},{2,26},{3,18},{4,28},{5,20},{6,30},{7,22},{8,25},{9,... | collective-permute-start | bytes 393224 | tf_op jit(solution)/shard_map/ppermute | solution.py:300
  72.8 9.4 %collective-permute-start.27 = (bf16[128,512]{1,0:T(8,128)(2,1)S(1)}, bf16[128,512]{1,0:T(8,128)(2,1)S(1)}, u32[]{:S(2)}, u32[]{:S(2)}) collective-permute-start(bf16[128,512]{1,0:T(8,128)(2,1)S(1)} %get-tuple-element.63), channel_id=1, source_target_pairs={{0,28},{1,20},{2,30},{3,22},{4,24},{5,16},{6,26},{7,18},{8,29},{9,... | collective-permute-start | bytes 393224 | tf_op jit(solution)/shard_map/ppermute | solution.py:300
  73.3 8.9 %collective-permute-start.31 = (bf16[128,512]{1,0:T(8,128)(2,1)S(1)}, bf16[128,512]{1,0:T(8,128)(2,1)S(1)}, u32[]{:S(2)}, u32[]{:S(2)}) collective-permute-start(bf16[128,512]{1,0:T(8,128)(2,1)S(1)} %broadcast_select_fusion), channel_id=1, source_target_pairs={{0,1},{1,0},{2,3},{3,2},{4,5},{5,4},{6,7},{7,6},{8,9},{9,8},{10,11... | collective-permute-start | bytes 393224 | tf_op jit(solution)/shard_map/ppermute | solution.py:19
  82.4 9.7 %collective-permute-start.32 = (bf16[128,512]{1,0:T(8,128)(2,1)S(1)}, bf16[128,512]{1,0:T(8,128)(2,1)S(1)}, u32[]{:S(2)}, u32[]{:S(2)}) collective-permute-start(bf16[128,512]{1,0:T(8,128)(2,1)S(1)} %select_convert_fusion), channel_id=1, source_target_pairs={{0,2},{1,3},{2,0},{3,1},{4,6},{5,7},{6,4},{7,5},{8,10},{9,11},{10,... | collective-permute-start | bytes 393224 | tf_op jit(solution)/shard_map/ppermute | solution.py:19
  (15 other events, 54.1 us)

commit v3 on v2

--- a/solution.py
+++ b/solution.py
@@ -46,11 +46,15 @@
     for rel in range(n_dp):
         if first:
             pair = [b[0 : rows + META, :] for b in (mine[rel], other[rel])]
-            metas = [b[rows:, 0:rows].astype(F32) for b in pair]
-            ids = jnp.concatenate([m[0:1] for m in metas], axis=1)
-            place = jnp.concatenate([m[1:2] for m in metas], axis=1)
-            low = (lax.axis_index("expert") * local_experts).astype(F32)
-            row = ((ids - low) * slots + place).astype(jnp.int32)
+            here = lax.axis_index("expert")
+            goals = [b[rows:, 0:rows][0:1].astype(F32).astype(jnp.int32) for b in pair]
+            row = jnp.concatenate(
+                [
+                    (goal // CAP - here * local_experts) * slots + source * CAP + goal % CAP
+                    for goal, source in zip(goals, (here, 1 - here))
+                ],
+                axis=1,
+            )
             lines[rel] = jnp.broadcast_to(row, (8, row.shape[1]))
             pair = [b[0:rows] for b in pair]
         else:
@@ -91,32 +95,20 @@
     if last:
         lines, refs = refs[0], refs[1:]
     h0, h1, gate, up = refs[:4]
-    outs, near, sems = refs[4:-2], refs[-2], refs[-1]
-    parts = (h0, h1)
+    outs = refs[4:]
     count, slots, _ = h0.shape
     hidden = gate.shape[1]
-    per_copy = count // sems.shape[1]
-
-    def copy_of(which, at):
-        rows = pl.ds(which * hidden, hidden)
-        source = (gate, up)[which].at[pl.ds(first + at * per_copy, per_copy)]
-        return pltpu.make_async_copy(source, near.at[pl.ds(at * per_copy, per_copy), rows], sems.at[which, at])
-
-    for at in range(sems.shape[1]):
-        for which in range(2):
-            copy_of(which, at).start()
-    for at in range(sems.shape[1]):
-        for which in range(2):
-            copy_of(which, at).wait()
-        for e in range(at * per_copy, (at + 1) * per_copy):
-            grads = jnp.concatenate([h[e] for h in parts], axis=0)
-            value = jnp.dot(grads, near[e], preferred_element_type=F32).astype(BF16)
-            for i in range(2):
-                rows = value[i * slots : (i + 1) * slots]
-                if last:
-                    outs[-1][i, (first + e) * slots : (first + e + 1) * slots, :] = rows
-                else:
-                    outs[0][i, e * slots : (e + 1) * slots, :] = rows
+    for e in range(count):
+        grads = jnp.concatenate([h0[e], h1[e]], axis=0)
+        value = jnp.dot(grads[:, 0:hidden], gate[first + e], preferred_element_type=F32)
+        value = value + jnp.dot(grads[:, hidden:], up[first + e], preferred_element_type=F32)
+        value = value.astype(BF16)
+        for i in range(2):
+            rows = value[i * slots : (i + 1) * slots]
+            if last:
+                outs[-1][i, (first + e) * slots : (first + e + 1) * slots, :] = rows
+            else:
+                outs[0][i, e * slots : (e + 1) * slots, :] = rows
     if not last:
         return
     held = outs[-1]
@@ -141,10 +133,7 @@
     vmem = pl.BlockSpec(memory_space=pltpu.VMEM)
     flops = (16 if last else 1) * count * 2 * slots * width * hidden
     operands = ([earlier] if first else []) + ([lines] if last else []) + [*parts]
-    near = [
-        pltpu.VMEM((count, 2 * hidden, width), BF16),
-        pltpu.SemaphoreType.DMA((2, count // 2 if count % 2 == 0 else count)),
-    ]
+    near = []
     if last:
         out_shape = [jax.ShapeDtypeStruct((rows, width), BF16)] * 4
         near = [pltpu.VMEM((2, local_experts * slots, width), BF16)] + near
@@ -153,10 +142,10 @@
     return pl.pallas_call(
         functools.partial(back_kernel, low, first, last),
         out_shape=out_shape,
-        in_specs=[vmem] * len(operands) + [pl.BlockSpec(memory_space=pl.ANY)] * 2,
+        in_specs=[vmem] * (len(operands) + 2),
         out_specs=[vmem] * 4 if last else vmem,
         scratch_shapes=near,
-        compiler_params=params(48),
+        compiler_params=params(24),
         cost_estimate=pl.CostEstimate(
             flops=flops, bytes_accessed=2 * count * width * hidden * 2 if last else width, transcendentals=0
         ),
@@ -215,9 +204,8 @@
     ids_row = expert_ids.reshape(1, rows)
     order = jnp.arange(rows, dtype=jnp.int32)
     earlier = (expert_ids == ids_row) & (order[:, None] < order[None, :])
-    position = jnp.sum(earlier.astype(jnp.int32), axis=0, keepdims=True) + x * CAP
-    meta = jnp.concatenate([ids_row, position], axis=0).astype(BF16)
-    meta = jnp.pad(meta, ((0, META - 2), (0, width - rows)))
+    goal = ids_row * CAP + jnp.sum(earlier.astype(jnp.int32), axis=0, keepdims=True)
+    meta = jnp.pad(goal.astype(BF16), ((0, META - 1), (0, width - rows)))
 
     def columns(values, rel):
         return lax.dynamic_slice_in_dim(values, (k ^ rel) * width, width, axis=1)
@@ -418,8 +406,14 @@
         P("expert", "dp", "tensor"),
     )
     sizes = tuple(mesh.shape[name] for name in ("dp", "expert", "tensor"))
+
+    def on_device(tokens, cotangent, expert_ids, *weights):
+        experts = weights[0].shape[0] * sizes[1]
+        small = sizes == (4, 2, 4) and experts * CAP <= 256
+        return (on_small_slice if small else on_any_slice)(tokens, cotangent, expert_ids, *weights)
+
     return jax.shard_map(
-        on_small_slice if sizes == (4, 2, 4) else on_any_slice,
+        on_device,
         mesh=mesh,
         in_specs=placed,
         out_specs=(

time: 93.1 us -> 99.5 us (1.069)
  local copies, waits for them, and re-layouts: 3.39 us -> 13.9 us
  Pallas kernels: 18.2 us -> 11.4 us
  waiting for transfers between devices: 31.2 us -> 33.9 us
    unnamed x12 -> x20, local copies, waits for them, and re-layouts: 0.98 us -> 11.5 us
    pallas_call x3, Pallas kernels: 11.6 us -> 4.76 us  [back(): pl.pallas_call(functools.partial(back_kernel, low, first, last), out_shap...]
    ppermute x21, waiting for transfers between devices: 23 us -> 25.7 us  [swap(): return lax.ppermute(value, axis, [(i, i ^ bit) for i in range(count)])]
  transfers between devices with their start and end apart: 33 -> 33, of which waited for: 16 -> 16; matrix products, arithmetic and copies ran while one was open for 7% -> 7% of each run, Pallas kernels for 20% -> 11%
where the time goes in v3:
time: 99.5 us; the launch traced here: 99.2 us
  waiting for transfers between devices  33.9 us (34%)
  starting transfers between devices  30.3 us (30%)
  local copies, waits for them, and re-layouts  13.9 us (14%)
  Pallas kernels  11.4 us (11%)
  matrix products  4.95 us (5%)
  other arithmetic  3.73 us (4%)
    ppermute x21, waiting for transfers between devices, swap(): return lax.ppermute(value, axis, [(i, i ^ bit) for i in range(count)])  25.7 us
    ppermute x21, starting transfers between devices, swap(): return lax.ppermute(value, axis, [(i, i ^ bit) for i in range(count)])  17.9 us
    unnamed x20, local copies, waits for them, and re-layouts  11.5 us
    ppermute x8, starting transfers between devices, to_owner(): return lax.ppermute(value, ('dp', 'expert'), pairs)  7.38 us
    ppermute x8, waiting for transfers between devices, to_owner(): return lax.ppermute(value, ('dp', 'expert'), pairs)  7.09 us
    pallas_call x1, Pallas kernels, weight_grads(): pl.pallas_call(weight_kernel, grid=(local_experts // per_step,), out_shap...  5.75 us
    ppermute x4, starting transfers between devices, to_keeper(): return lax.ppermute(value, ('dp', 'expert', 'tensor'), pairs)  5.03 us
    dot_general x3, matrix products, project(): jnp.einsum('esd,ehd->esh', values, weight, preferred_element_type=F32)  4.95 us
  transfers between devices with their start and end apart: 33, of which 16 were waited for; matrix products, arithmetic and copies ran while one was open for 7% of the time, Pallas kernels for 11%

profile of v3, /device:TPU:0, one launch (start us, length us, event | category | flops | bytes accessed | tf_op | source)
XLA Modules:
  0.0 99.2 jit_solution(6594155850803305419)
XLA Ops:
  3.3 3.0 %collective-permute-start = (bf16[144,512]{1,0:T(8,128)(2,1)S(1)}, bf16[144,512]{1,0:T(8,128)(2,1)S(1)}, u32[]{:S(2)}, u32[]{:S(2)}) collective-permute-start(bf16[144,512]{1,0:T(8,128)(2,1)S(1)} %get-tuple-element.94), channel_id=1, source_target_pairs={{0,16},{4,20},{8,24},{12,28},{16,0},{20,4},{24,8},{28,12},{1,17},{... | collective-permute-start | bytes 442376 | tf_op jit(solution)/shard_map/ppermute | solution.py:221
  9.2 1.8 %collective-permute-done.refs_2_ = bf16[144,512]{1,0:T(8,128)(2,1)S(1)} collective-permute-done((bf16[144,512]{1,0:T(8,128)(2,1)S(1)}, bf16[144,512]{1,0:T(8,128)(2,1)S(1)}, u32[]{:S(2)}, u32[]{:S(2)}) %collective-permute-start) | collective-permute-done | bytes 147488 | tf_op jit(solution)/shard_map/ppermute | solution.py:221
  13.5 1.7 %collective-permute-start.3 = (bf16[128,512]{1,0:T(8,128)(2,1)S(1)}, bf16[128,512]{1,0:T(8,128)(2,1)S(1)}, u32[]{:S(2)}, u32[]{:S(2)}) collective-permute-start(bf16[128,512]{1,0:T(8,128)(2,1)S(1)} %get-tuple-element.42), channel_id=1, source_target_pairs={{0,16},{4,20},{8,24},{12,28},{16,0},{20,4},{24,8},{28,12},{1,17},{... | collective-permute-start | bytes 393224 | tf_op jit(solution)/shard_map/ppermute | solution.py:221
  15.2 1.9 %collective-permute-start.7 = (bf16[144,512]{1,0:T(8,128)(2,1)S(1)}, bf16[144,512]{1,0:T(8,128)(2,1)S(1)}, u32[]{:S(2)}, u32[]{:S(2)}) collective-permute-start(bf16[144,512]{1,0:T(8,128)(2,1)S(1)} %collective-permute-done.refs_2_), channel_id=1, source_target_pairs={{0,4},{4,0},{1,5},{5,1},{2,6},{6,2},{3,7},{7,3},{8,12},{12,8},{9,1... | collective-permute-start | bytes 442376 | tf_op jit(solution)/shard_map/ppermute | solution.py:19
  17.3 2.2 %collective-permute-done.3.refs_2_ = bf16[128,512]{1,0:T(8,128)(2,1)S(1)} collective-permute-done((bf16[128,512]{1,0:T(8,128)(2,1)S(1)}, bf16[128,512]{1,0:T(8,128)(2,1)S(1)}, u32[]{:S(2)}, u32[]{:S(2)}) %collective-permute-start.3) | collective-permute-done | bytes 131104 | tf_op jit(solution)/shard_map/ppermute | solution.py:221
  22.0 2.6 %collective-permute-done.8.refs_7_ = bf16[144,512]{1,0:T(8,128)(2,1)S(1)} collective-permute-done((bf16[144,512]{1,0:T(8,128)(2,1)S(1)}, bf16[144,512]{1,0:T(8,128)(2,1)S(1)}, u32[]{:S(2)}, u32[]{:S(2)}) %collective-permute-start.8) | collective-permute-done | bytes 147488 | tf_op jit(solution)/shard_map/ppermute | solution.py:19
  24.5 1.7 %collective-permute-start.9 = (bf16[4,128,512]{2,1,0:T(8,128)(2,1)S(1)}, bf16[4,128,512]{2,1,0:T(8,128)(2,1)S(1)}, u32[]{:S(2)}, u32[]{:S(2)}) collective-permute-start(bf16[4,128,512]{2,1,0:T(8,128)(2,1)S(1)} %pad_maximum_fusion.refs_8_), channel_id=1, source_target_pairs={{0,4},{4,0},{1,5},{5,1},{2,6},{6,2},{3,7},{7,3},{8,12},{12,8},{9,1... | collective-permute-start | bytes 1572872 | tf_op jit(solution)/shard_map/ppermute | solution.py:19
  32.0 1.8 %collective-permute-start.15 = (bf16[2,16,16,352]{3,2,1,0:T(8,128)(2,1)S(1)}, bf16[2,16,16,352]{3,2,1,0:T(8,128)(2,1)S(1)}, u32[]{:S(2)}, u32[]{:S(2)}) collective-permute-start(bf16[2,16,16,352]{3,2,1,0:T(8,128)(2,1)S(1)} %pad_maximum_fusion.2.refs_6_), channel_id=1, source_target_pairs={{0,16},{8,24},{16,0},{24,8},{1,17},{9,25},{17,1},{25,9},{2,18},{10... | collective-permute-start | bytes 1081352 | tf_op jit(solution)/shard_map/ppermute | solution.py:19
  33.8 4.1 %collective-permute-done.9.refs_4_ = bf16[4,128,512]{2,1,0:T(8,128)(2,1)S(1)} collective-permute-done((bf16[4,128,512]{2,1,0:T(8,128)(2,1)S(1)}, bf16[4,128,512]{2,1,0:T(8,128)(2,1)S(1)}, u32[]{:S(2)}, u32[]{:S(2)}) %collective-permute-start.9) | collective-permute-done | bytes 524320 | tf_op jit(solution)/shard_map/ppermute | solution.py:19
  43.5 1.8 %collective-permute-start.16 = (bf16[16,16,352]{2,1,0:T(8,128)(2,1)S(1)}, bf16[16,16,352]{2,1,0:T(8,128)(2,1)S(1)}, u32[]{:S(2)}, u32[]{:S(2)}) collective-permute-start(bf16[16,16,352]{2,1,0:T(8,128)(2,1)S(1)} %add_convert_fusion), channel_id=1, source_target_pairs={{0,16},{8,24},{16,0},{24,8},{1,17},{9,25},{17,1},{25,9},{2,18},{10... | collective-permute-start | bytes 540680 | tf_op jit(solution)/shard_map/ppermute | solution.py:19
  45.3 4.7 %collective-permute-done.16 = bf16[16,16,352]{2,1,0:T(8,128)(2,1)S(1)} collective-permute-done((bf16[16,16,352]{2,1,0:T(8,128)(2,1)S(1)}, bf16[16,16,352]{2,1,0:T(8,128)(2,1)S(1)}, u32[]{:S(2)}, u32[]{:S(2)}) %collective-permute-start.16) | collective-permute-done | bytes 180256 | tf_op jit(solution)/shard_map/ppermute | solution.py:19
  50.7 1.8 %collective-permute-start.19 = (bf16[7,16,704]{2,1,0:T(8,128)(2,1)S(1)}, bf16[7,16,704]{2,1,0:T(8,128)(2,1)S(1)}, u32[]{:S(2)}, u32[]{:S(2)}) collective-permute-start(bf16[7,16,704]{2,1,0:T(8,128)(2,1)S(1)} %fusion.10), channel_id=1, source_target_pairs={{0,16},{8,24},{16,0},{24,8},{1,17},{9,25},{17,1},{25,9},{2,18},{10... | collective-permute-start | bytes 473096 | tf_op jit(solution)/shard_map/ppermute | solution.py:19
  53.0 2.3 %shard_map.87 = (bf16[128,512]{1,0:T(8,128)(2,1)S(1)}, bf16[128,512]{1,0:T(8,128)(2,1)S(1)}, bf16[128,512]{1,0:T(8,128)(2,1)S(1)}, bf16[128,512]{1,0:T(8,128)(2,1)S(1)}) custom-call(s32[4,8,256]{2,1,0:T(8,128)S(1)} %get-tuple-element.53.refs_5_.refs_0_.refs_1_, bf16[16,16,704]{2,1,0:T(8,128)(2,1)S(1)} %pad_maximum_fusion.1.refs_1_.h0, ...), custom_call_target="tpu_custom_call" | custom-call | flops 1476395008 | bytes 11534336 | tf_op jit(solution)/shard_map/pallas_call | solution.py:142
  55.3 2.6 %collective-permute-done.19.refs_0_ = bf16[7,16,704]{2,1,0:T(8,128)(2,1)S(1)} collective-permute-done((bf16[7,16,704]{2,1,0:T(8,128)(2,1)S(1)}, bf16[7,16,704]{2,1,0:T(8,128)(2,1)S(1)}, u32[]{:S(2)}, u32[]{:S(2)}) %collective-permute-start.19) | collective-permute-done | bytes 157728 | tf_op jit(solution)/shard_map/ppermute | solution.py:19
  59.8 2.6 %copy-done = bf16[16,512,352]{1,2,0:T(8,128)(2,1)S(1)} copy-done((bf16[16,512,352]{1,2,0:T(8,128)(2,1)S(1)}, bf16[16,512,352]{1,2,0:T(8,128)(2,1)}, u32[]{:S(2)}) %copy-start) | copy-done | bytes 5767192
  62.4 2.6 %copy-done.2 = bf16[16,512,352]{1,2,0:T(8,128)(2,1)S(1)} copy-done((bf16[16,512,352]{1,2,0:T(8,128)(2,1)S(1)}, bf16[16,512,352]{1,2,0:T(8,128)(2,1)}, u32[]{:S(2)}) %copy-start.2) | copy-done | bytes 5767192
  67.7 2.6 %copy-done.1 = bf16[16,512,352]{1,2,0:T(8,128)(2,1)S(1)} copy-done((bf16[16,512,352]{1,2,0:T(8,128)(2,1)S(1)}, bf16[16,512,352]{1,2,0:T(8,128)(2,1)}, u32[]{:S(2)}) %copy-start.1) | copy-done | bytes 5767192
  70.3 2.6 %copy-done.3 = bf16[16,512,352]{1,2,0:T(8,128)(2,1)S(1)} copy-done((bf16[16,512,352]{1,2,0:T(8,128)(2,1)S(1)}, bf16[16,512,352]{1,2,0:T(8,128)(2,1)}, u32[]{:S(2)}) %copy-start.3) | copy-done | bytes 5767192
  74.4 1.7 %collective-permute-start.24 = (bf16[128,512]{1,0:T(8,128)(2,1)S(1)}, bf16[128,512]{1,0:T(8,128)(2,1)S(1)}, u32[]{:S(2)}, u32[]{:S(2)}) collective-permute-start(bf16[128,512]{1,0:T(8,128)(2,1)S(1)} %get-tuple-element.60), channel_id=1, source_target_pairs={{0,16},{1,24},{2,18},{3,26},{4,20},{5,28},{6,22},{7,30},{8,17},{9,... | collective-permute-start | bytes 393224 | tf_op jit(solution)/shard_map/ppermute | solution.py:288
  77.1 2.0 %collective-permute-start.26 = (bf16[128,512]{1,0:T(8,128)(2,1)S(1)}, bf16[128,512]{1,0:T(8,128)(2,1)S(1)}, u32[]{:S(2)}, u32[]{:S(2)}) collective-permute-start(bf16[128,512]{1,0:T(8,128)(2,1)S(1)} %get-tuple-element.62), channel_id=1, source_target_pairs={{0,24},{1,16},{2,26},{3,18},{4,28},{5,20},{6,30},{7,22},{8,25},{9,... | collective-permute-start | bytes 393224 | tf_op jit(solution)/shard_map/ppermute | solution.py:288
  79.6 1.9 %collective-permute-start.31 = (bf16[128,512]{1,0:T(8,128)(2,1)S(1)}, bf16[128,512]{1,0:T(8,128)(2,1)S(1)}, u32[]{:S(2)}, u32[]{:S(2)}) collective-permute-start(bf16[128,512]{1,0:T(8,128)(2,1)S(1)} %broadcast_select_fusion), channel_id=1, source_target_pairs={{0,1},{1,0},{2,3},{3,2},{4,5},{5,4},{6,7},{7,6},{8,9},{9,8},{10,11... | collective-permute-start | bytes 393224 | tf_op jit(solution)/shard_map/ppermute | solution.py:19
  81.5 5.8 %shard_map.90 = (bf16[16,352,512]{2,1,0:T(8,128)(2,1)}, bf16[16,352,512]{2,1,0:T(8,128)(2,1)}) custom-call(bf16[16,64,512]{2,1,0:T(8,128)(2,1)S(1)} %get-tuple-element.68.placed, bf16[16,16,704]{2,1,0:T(8,128)(2,1)S(1)} %pad_maximum_fusion.1.refs_1_.h0, bf16[16,16,704]{2,1,0:T(8,128)(2,1)S(1)} %collective-permute-done.20.refs_2_.h1, ...), custom_call_target="tpu_custom_call" | custom-call | flops 2952790016 | bytes 11534336 | tf_op jit(solution)/shard_map/pallas_call | solution.py:173
  88.7 2.7 %collective-permute-start.32 = (bf16[128,512]{1,0:T(8,128)(2,1)S(1)}, bf16[128,512]{1,0:T(8,128)(2,1)S(1)}, u32[]{:S(2)}, u32[]{:S(2)}) collective-permute-start(bf16[128,512]{1,0:T(8,128)(2,1)S(1)} %select_convert_fusion), channel_id=1, source_target_pairs={{0,2},{1,3},{2,0},{3,1},{4,6},{5,7},{6,4},{7,5},{8,10},{9,11},{10,... | collective-permute-start | bytes 393224 | tf_op jit(solution)/shard_map/ppermute | solution.py:19
  91.3 7.0 %collective-permute-done.32 = bf16[128,512]{1,0:T(8,128)(2,1)S(1)} collective-permute-done((bf16[128,512]{1,0:T(8,128)(2,1)S(1)}, bf16[128,512]{1,0:T(8,128)(2,1)S(1)}, u32[]{:S(2)}, u32[]{:S(2)}) %collective-permute-start.32) | collective-permute-done | bytes 131104 | tf_op jit(solution)/shard_map/ppermute | solution.py:19
  (97 shorter events, 32.7 us)
Async XLA Ops:
  3.3 7.7 %collective-permute-start = (bf16[144,512]{1,0:T(8,128)(2,1)S(1)}, bf16[144,512]{1,0:T(8,128)(2,1)S(1)}, u32[]{:S(2)}, u32[]{:S(2)}) collective-permute-start(bf16[144,512]{1,0:T(8,128)(2,1)S(1)} %get-tuple-element.94), channel_id=1, source_target_pairs={{0,16},{4,20},{8,24},{12,28},{16,0},{20,4},{24,8},{28,12},{1,17},{... | collective-permute-start | bytes 442376 | tf_op jit(solution)/shard_map/ppermute | solution.py:221
  6.4 6.3 %collective-permute-start.1 = (bf16[144,512]{1,0:T(8,128)(2,1)S(1)}, bf16[144,512]{1,0:T(8,128)(2,1)S(1)}, u32[]{:S(2)}, u32[]{:S(2)}) collective-permute-start(bf16[144,512]{1,0:T(8,128)(2,1)S(1)} %get-tuple-element.93), channel_id=1, source_target_pairs={{0,24},{4,28},{8,16},{12,20},{16,8},{20,12},{24,0},{28,4},{1,25},{... | collective-permute-start | bytes 442376 | tf_op jit(solution)/shard_map/ppermute | solution.py:221
  6.4 8.9 %collective-permute-start.5 = (bf16[144,512]{1,0:T(8,128)(2,1)S(1)}, bf16[144,512]{1,0:T(8,128)(2,1)S(1)}, u32[]{:S(2)}, u32[]{:S(2)}) collective-permute-start(bf16[144,512]{1,0:T(8,128)(2,1)S(1)} %get-tuple-element.95.refs_0_), channel_id=1, source_target_pairs={{0,4},{4,0},{8,12},{12,8},{16,20},{20,16},{24,28},{28,24},{1,5},{5... | collective-permute-start | bytes 442376 | tf_op jit(solution)/shard_map/ppermute | solution.py:221
  7.9 7.4 %collective-permute-start.6 = (bf16[144,512]{1,0:T(8,128)(2,1)S(1)}, bf16[144,512]{1,0:T(8,128)(2,1)S(1)}, u32[]{:S(2)}, u32[]{:S(2)}) collective-permute-start(bf16[144,512]{1,0:T(8,128)(2,1)S(1)} %get-tuple-element.96), channel_id=1, source_target_pairs={{0,12},{4,8},{8,4},{12,0},{16,28},{20,24},{24,20},{28,16},{1,13},{... | collective-permute-start | bytes 442376 | tf_op jit(solution)/shard_map/ppermute | solution.py:221
  12.6 4.7 %collective-permute-start.2 = (bf16[128,512]{1,0:T(8,128)(2,1)S(1)}, bf16[128,512]{1,0:T(8,128)(2,1)S(1)}, u32[]{:S(2)}, u32[]{:S(2)}) collective-permute-start(bf16[128,512]{1,0:T(8,128)(2,1)S(1)} %get-tuple-element.41), channel_id=1, source_target_pairs={{0,8},{4,12},{8,0},{12,4},{16,24},{20,28},{24,16},{28,20},{1,9},{5... | collective-permute-start | bytes 393224 | tf_op jit(solution)/shard_map/ppermute | solution.py:221
  13.5 6.1 %collective-permute-start.3 = (bf16[128,512]{1,0:T(8,128)(2,1)S(1)}, bf16[128,512]{1,0:T(8,128)(2,1)S(1)}, u32[]{:S(2)}, u32[]{:S(2)}) collective-permute-start(bf16[128,512]{1,0:T(8,128)(2,1)S(1)} %get-tuple-element.42), channel_id=1, source_target_pairs={{0,16},{4,20},{8,24},{12,28},{16,0},{20,4},{24,8},{28,12},{1,17},{... | collective-permute-start | bytes 393224 | tf_op jit(solution)/shard_map/ppermute | solution.py:221
  15.2 5.8 %collective-permute-start.4 = (bf16[128,512]{1,0:T(8,128)(2,1)S(1)}, bf16[128,512]{1,0:T(8,128)(2,1)S(1)}, u32[]{:S(2)}, u32[]{:S(2)}) collective-permute-start(bf16[128,512]{1,0:T(8,128)(2,1)S(1)} %get-tuple-element.43), channel_id=1, source_target_pairs={{0,24},{4,28},{8,16},{12,20},{16,8},{20,12},{24,0},{28,4},{1,25},{... | collective-permute-start | bytes 393224 | tf_op jit(solution)/shard_map/ppermute | solution.py:221
  15.2 6.7 %collective-permute-start.7 = (bf16[144,512]{1,0:T(8,128)(2,1)S(1)}, bf16[144,512]{1,0:T(8,128)(2,1)S(1)}, u32[]{:S(2)}, u32[]{:S(2)}) collective-permute-start(bf16[144,512]{1,0:T(8,128)(2,1)S(1)} %collective-permute-done.refs_2_), channel_id=1, source_target_pairs={{0,4},{4,0},{1,5},{5,1},{2,6},{6,2},{3,7},{7,3},{8,12},{12,8},{9,1... | collective-permute-start | bytes 442376 | tf_op jit(solution)/shard_map/ppermute | solution.py:19
  17.1 7.4 %collective-permute-start.8 = (bf16[144,512]{1,0:T(8,128)(2,1)S(1)}, bf16[144,512]{1,0:T(8,128)(2,1)S(1)}, u32[]{:S(2)}, u32[]{:S(2)}) collective-permute-start(bf16[144,512]{1,0:T(8,128)(2,1)S(1)} %collective-permute-done.1.refs_3_), channel_id=1, source_target_pairs={{0,4},{4,0},{1,5},{5,1},{2,6},{6,2},{3,7},{7,3},{8,12},{12,8},{9,1... | collective-permute-start | bytes 442376 | tf_op jit(solution)/shard_map/ppermute | solution.py:19
  17.3 8.9 %collective-permute-start.10 = (bf16[144,512]{1,0:T(8,128)(2,1)S(1)}, bf16[144,512]{1,0:T(8,128)(2,1)S(1)}, u32[]{:S(2)}, u32[]{:S(2)}) collective-permute-start(bf16[144,512]{1,0:T(8,128)(2,1)S(1)} %get-tuple-element.96), channel_id=1, source_target_pairs={{0,8},{4,12},{8,0},{12,4},{16,24},{20,28},{24,16},{28,20},{1,9},{5... | collective-permute-start | bytes 442376 | tf_op jit(solution)/shard_map/ppermute | solution.py:221
  24.5 13.4 %collective-permute-start.9 = (bf16[4,128,512]{2,1,0:T(8,128)(2,1)S(1)}, bf16[4,128,512]{2,1,0:T(8,128)(2,1)S(1)}, u32[]{:S(2)}, u32[]{:S(2)}) collective-permute-start(bf16[4,128,512]{2,1,0:T(8,128)(2,1)S(1)} %pad_maximum_fusion.refs_8_), channel_id=1, source_target_pairs={{0,4},{4,0},{1,5},{5,1},{2,6},{6,2},{3,7},{7,3},{8,12},{12,8},{9,1... | collective-permute-start | bytes 1572872 | tf_op jit(solution)/shard_map/ppermute | solution.py:19
  32.0 11.5 %collective-permute-start.15 = (bf16[2,16,16,352]{3,2,1,0:T(8,128)(2,1)S(1)}, bf16[2,16,16,352]{3,2,1,0:T(8,128)(2,1)S(1)}, u32[]{:S(2)}, u32[]{:S(2)}) collective-permute-start(bf16[2,16,16,352]{3,2,1,0:T(8,128)(2,1)S(1)} %pad_maximum_fusion.2.refs_6_), channel_id=1, source_target_pairs={{0,16},{8,24},{16,0},{24,8},{1,17},{9,25},{17,1},{25,9},{2,18},{10... | collective-permute-start | bytes 1081352 | tf_op jit(solution)/shard_map/ppermute | solution.py:19
  41.1 4.2 %collective-permute-start.17 = (bf16[16,16,352]{2,1,0:T(8,128)(2,1)S(1)}, bf16[16,16,352]{2,1,0:T(8,128)(2,1)S(1)}, u32[]{:S(2)}, u32[]{:S(2)}) collective-permute-start(bf16[16,16,352]{2,1,0:T(8,128)(2,1)S(1)} %get-tuple-element.79), channel_id=1, source_target_pairs={{0,8},{8,0},{16,24},{24,16},{1,9},{9,1},{17,25},{25,17},{2,10},{10... | collective-permute-start | bytes 540680 | tf_op jit(solution)/shard_map/ppermute | solution.py:19
  41.6 3.7 %collective-permute-start.18 = (bf16[16,16,352]{2,1,0:T(8,128)(2,1)S(1)}, bf16[16,16,352]{2,1,0:T(8,128)(2,1)S(1)}, u32[]{:S(2)}, u32[]{:S(2)}) collective-permute-start(bf16[16,16,352]{2,1,0:T(8,128)(2,1)S(1)} %get-tuple-element.81), channel_id=1, source_target_pairs={{0,8},{8,0},{16,24},{24,16},{1,9},{9,1},{17,25},{25,17},{2,10},{10... | collective-permute-start | bytes 540680 | tf_op jit(solution)/shard_map/ppermute | solution.py:19
  43.5 6.4 %collective-permute-start.16 = (bf16[16,16,352]{2,1,0:T(8,128)(2,1)S(1)}, bf16[16,16,352]{2,1,0:T(8,128)(2,1)S(1)}, u32[]{:S(2)}, u32[]{:S(2)}) collective-permute-start(bf16[16,16,352]{2,1,0:T(8,128)(2,1)S(1)} %add_convert_fusion), channel_id=1, source_target_pairs={{0,16},{8,24},{16,0},{24,8},{1,17},{9,25},{17,1},{25,9},{2,18},{10... | collective-permute-start | bytes 540680 | tf_op jit(solution)/shard_map/ppermute | solution.py:19
  50.7 7.2 %collective-permute-start.19 = (bf16[7,16,704]{2,1,0:T(8,128)(2,1)S(1)}, bf16[7,16,704]{2,1,0:T(8,128)(2,1)S(1)}, u32[]{:S(2)}, u32[]{:S(2)}) collective-permute-start(bf16[7,16,704]{2,1,0:T(8,128)(2,1)S(1)} %fusion.10), channel_id=1, source_target_pairs={{0,16},{8,24},{16,0},{24,8},{1,17},{9,25},{17,1},{25,9},{2,18},{10... | collective-permute-start | bytes 473096 | tf_op jit(solution)/shard_map/ppermute | solution.py:19
  52.5 13.5 %collective-permute-start.22 = (bf16[9,16,704]{2,1,0:T(8,128)(2,1)S(1)}, bf16[9,16,704]{2,1,0:T(8,128)(2,1)S(1)}, u32[]{:S(2)}, u32[]{:S(2)}) collective-permute-start(bf16[9,16,704]{2,1,0:T(8,128)(2,1)S(1)} %fusion.7), channel_id=1, source_target_pairs={{0,16},{8,24},{16,0},{24,8},{1,17},{9,25},{17,1},{25,9},{2,18},{10... | collective-permute-start | bytes 608264 | tf_op jit(solution)/shard_map/ppermute | solution.py:19
  66.3 13.2 %collective-permute-start.30 = (bf16[2,128,512]{2,1,0:T(8,128)(2,1)S(1)}, bf16[2,128,512]{2,1,0:T(8,128)(2,1)S(1)}, u32[]{:S(2)}, u32[]{:S(2)}) collective-permute-start(bf16[2,128,512]{2,1,0:T(8,128)(2,1)S(1)} %pad_maximum_fusion.5), channel_id=1, source_target_pairs={{0,4},{4,0},{1,5},{5,1},{2,6},{6,2},{3,7},{7,3},{8,12},{12,8},{9,1... | collective-permute-start | bytes 786440 | tf_op jit(solution)/shard_map/ppermute | solution.py:19
  74.4 12.8 %collective-permute-start.24 = (bf16[128,512]{1,0:T(8,128)(2,1)S(1)}, bf16[128,512]{1,0:T(8,128)(2,1)S(1)}, u32[]{:S(2)}, u32[]{:S(2)}) collective-permute-start(bf16[128,512]{1,0:T(8,128)(2,1)S(1)} %get-tuple-element.60), channel_id=1, source_target_pairs={{0,16},{1,24},{2,18},{3,26},{4,20},{5,28},{6,22},{7,30},{8,17},{9,... | collective-permute-start | bytes 393224 | tf_op jit(solution)/shard_map/ppermute | solution.py:288
  76.1 11.2 %collective-permute-start.25 = (bf16[128,512]{1,0:T(8,128)(2,1)S(1)}, bf16[128,512]{1,0:T(8,128)(2,1)S(1)}, u32[]{:S(2)}, u32[]{:S(2)}) collective-permute-start(bf16[128,512]{1,0:T(8,128)(2,1)S(1)} %get-tuple-element.61), channel_id=1, source_target_pairs={{0,20},{1,28},{2,22},{3,30},{4,16},{5,24},{6,18},{7,26},{8,21},{9,... | collective-permute-start | bytes 393224 | tf_op jit(solution)/shard_map/ppermute | solution.py:288
  77.1 11.3 %collective-permute-start.26 = (bf16[128,512]{1,0:T(8,128)(2,1)S(1)}, bf16[128,512]{1,0:T(8,128)(2,1)S(1)}, u32[]{:S(2)}, u32[]{:S(2)}) collective-permute-start(bf16[128,512]{1,0:T(8,128)(2,1)S(1)} %get-tuple-element.62), channel_id=1, source_target_pairs={{0,24},{1,16},{2,26},{3,18},{4,28},{5,20},{6,30},{7,22},{8,25},{9,... | collective-permute-start | bytes 393224 | tf_op jit(solution)/shard_map/ppermute | solution.py:288
  79.1 9.4 %collective-permute-start.27 = (bf16[128,512]{1,0:T(8,128)(2,1)S(1)}, bf16[128,512]{1,0:T(8,128)(2,1)S(1)}, u32[]{:S(2)}, u32[]{:S(2)}) collective-permute-start(bf16[128,512]{1,0:T(8,128)(2,1)S(1)} %get-tuple-element.63), channel_id=1, source_target_pairs={{0,28},{1,20},{2,30},{3,22},{4,24},{5,16},{6,26},{7,18},{8,29},{9,... | collective-permute-start | bytes 393224 | tf_op jit(solution)/shard_map/ppermute | solution.py:288
  79.6 8.9 %collective-permute-start.31 = (bf16[128,512]{1,0:T(8,128)(2,1)S(1)}, bf16[128,512]{1,0:T(8,128)(2,1)S(1)}, u32[]{:S(2)}, u32[]{:S(2)}) collective-permute-start(bf16[128,512]{1,0:T(8,128)(2,1)S(1)} %broadcast_select_fusion), channel_id=1, source_target_pairs={{0,1},{1,0},{2,3},{3,2},{4,5},{5,4},{6,7},{7,6},{8,9},{9,8},{10,11... | collective-permute-start | bytes 393224 | tf_op jit(solution)/shard_map/ppermute | solution.py:19
  88.7 9.7 %collective-permute-start.32 = (bf16[128,512]{1,0:T(8,128)(2,1)S(1)}, bf16[128,512]{1,0:T(8,128)(2,1)S(1)}, u32[]{:S(2)}, u32[]{:S(2)}) collective-permute-start(bf16[128,512]{1,0:T(8,128)(2,1)S(1)} %select_convert_fusion), channel_id=1, source_target_pairs={{0,2},{1,3},{2,0},{3,1},{4,6},{5,7},{6,4},{7,5},{8,10},{9,11},{10,... | collective-permute-start | bytes 393224 | tf_op jit(solution)/shard_map/ppermute | solution.py:19
  (19 other events, 64.6 us)

commit v4 on v3

--- a/solution.py
+++ b/solution.py
@@ -94,15 +94,19 @@
         earlier, refs = refs[0], refs[1:]
     if last:
         lines, refs = refs[0], refs[1:]
-    h0, h1, gate, up = refs[:4]
-    outs = refs[4:]
+    h0, h1, refs = refs[0], refs[1], refs[2:]
     count, slots, _ = h0.shape
-    hidden = gate.shape[1]
+    if low:
+        both, outs = refs[0], refs[1:]
+    else:
+        gate, up, both, outs = refs[0], refs[1], refs[6], refs[2:6] + refs[7:]
+        hidden = gate.shape[1]
     for e in range(count):
         grads = jnp.concatenate([h0[e], h1[e]], axis=0)
-        value = jnp.dot(grads[:, 0:hidden], gate[first + e], preferred_element_type=F32)
-        value = value + jnp.dot(grads[:, hidden:], up[first + e], preferred_element_type=F32)
-        value = value.astype(BF16)
+        if not low:
+            both[e, 0:hidden, :] = gate[e]
+            both[e, hidden:, :] = up[e]
+        value = jnp.dot(grads, both[first + e], preferred_element_type=F32).astype(BF16)
         for i in range(2):
             rows = value[i * slots : (i + 1) * slots]
             if last:
@@ -126,30 +130,32 @@
         outs[2 * i + 1][...] = token_rows[rows:]
 
 
-def back(low, lines, parts, gate, up, rows, first=0, earlier=None):
-    local_experts, hidden, width = gate.shape
-    count, slots, _ = parts[0].shape
+def back(low, lines, parts, weights, rows, first=0, earlier=None):
+    local_experts, _, width = weights[0].shape
+    count, slots, hidden = parts[0].shape
     last = first + count == local_experts
     vmem = pl.BlockSpec(memory_space=pltpu.VMEM)
-    flops = (16 if last else 1) * count * 2 * slots * width * hidden
+    flops = (8 if last else 1) * count * 2 * slots * width * hidden
     operands = ([earlier] if first else []) + ([lines] if last else []) + [*parts]
     near = []
     if last:
         out_shape = [jax.ShapeDtypeStruct((rows, width), BF16)] * 4
+        if not low:
+            out_shape.append(jax.ShapeDtypeStruct((local_experts, hidden, width), BF16))
         near = [pltpu.VMEM((2, local_experts * slots, width), BF16)] + near
     else:
         out_shape = jax.ShapeDtypeStruct((2, count * slots, width), BF16)
     return pl.pallas_call(
         functools.partial(back_kernel, low, first, last),
         out_shape=out_shape,
-        in_specs=[vmem] * (len(operands) + 2),
-        out_specs=[vmem] * 4 if last else vmem,
+        in_specs=[vmem] * (len(operands) + len(weights)),
+        out_specs=[vmem] * len(out_shape) if last else vmem,
         scratch_shapes=near,
-        compiler_params=params(24),
+        compiler_params=params(20 if low else 30),
         cost_estimate=pl.CostEstimate(
-            flops=flops, bytes_accessed=2 * count * width * hidden * 2 if last else width, transcendentals=0
+            flops=flops, bytes_accessed=count * width * hidden * 2 if last else width, transcendentals=0
         ),
-    )(*operands, gate, up)
+    )(*operands, *weights)
 
 
 def weight_kernel(placed, h0, h1, h2, h3, gate, up):
@@ -262,13 +268,13 @@
     count = local_experts * 7 // 16
     far = [swap(piece, "dp", n_dp, 2) for piece in jnp.split(part, [count], axis=0)]
     beside = swap(part, "dp", n_dp, 1)
-    near_back = back(0, lines, [part, beside], gate_weight, up_weight, rows)
+    *near_back, both_weights = back(0, lines, [part, beside], [gate_weight, up_weight], rows)
     far[0], _ = lax.optimization_barrier((far[0], near_back[0]))
     far_beside = [swap(far[0], "dp", n_dp, 1)]
-    early = back(2, lines, [far[0], far_beside[0]], gate_weight, up_weight, rows)
+    early = back(2, lines, [far[0], far_beside[0]], [both_weights], rows)
     far[1], _ = lax.optimization_barrier((far[1], early))
     far_beside.append(swap(far[1], "dp", n_dp, 1))
-    far_back = back(2, lines, [far[1], far_beside[1]], gate_weight, up_weight, rows, count, early)
+    far_back = back(2, lines, [far[1], far_beside[1]], [both_weights], rows, count, early)
     parts = [part, beside, jnp.concatenate(far, axis=0), jnp.concatenate(far_beside, axis=0)]
     own, other, own_beside, other_beside = near_back
     own_beside, other_beside = swap(own_beside, "dp", n_dp, 1), swap(other_beside, "dp", n_dp, 1)

time: 99.5 us -> 96.8 us (0.973)
  waiting for transfers between devices: 33.9 us -> 30.6 us
    ppermute x21, waiting for transfers between devices: 25.7 us -> 22.4 us  [swap(): return lax.ppermute(value, axis, [(i, i ^ bit) for i in range(count)])]
    unnamed x20 -> x18, local copies, waits for them, and re-layouts: 11.5 us -> 11.2 us
  transfers between devices with their start and end apart: 33 -> 33, of which waited for: 16 -> 14; matrix products, arithmetic and copies ran while one was open for 7% -> 7% of each run, Pallas kernels for 11% -> 12%
where the time goes in v4:
time: 96.8 us; the launch traced here: 96.5 us
  starting transfers between devices  31.1 us (32%)
  waiting for transfers between devices  30.6 us (32%)
  local copies, waits for them, and re-layouts  13.6 us (14%)
  Pallas kernels  11.6 us (12%)
  matrix products  4.98 us (5%)
  other arithmetic  3.74 us (4%)
  between operations  0.98 us (1%)
    ppermute x21, waiting for transfers between devices, swap(): return lax.ppermute(value, axis, [(i, i ^ bit) for i in range(count)])  22.4 us
    ppermute x21, starting transfers between devices, swap(): return lax.ppermute(value, axis, [(i, i ^ bit) for i in range(count)])  17.9 us
    unnamed x18, local copies, waits for them, and re-layouts  11.2 us
    ppermute x8, starting transfers between devices, to_owner(): return lax.ppermute(value, ('dp', 'expert'), pairs)  8.11 us
    ppermute x8, waiting for transfers between devices, to_owner(): return lax.ppermute(value, ('dp', 'expert'), pairs)  7.02 us
    pallas_call x1, Pallas kernels, weight_grads(): pl.pallas_call(weight_kernel, grid=(local_experts // per_step,), out_shap...  5.75 us
    ppermute x4, starting transfers between devices, to_keeper(): return lax.ppermute(value, ('dp', 'expert', 'tensor'), pairs)  5.09 us
    dot_general x3, matrix products, project(): jnp.einsum('esd,ehd->esh', values, weight, preferred_element_type=F32)  4.98 us
  transfers between devices with their start and end apart: 33, of which 14 were waited for; matrix products, arithmetic and copies ran while one was open for 7% of the time, Pallas kernels for 12%

profile of v4, /device:TPU:0, one launch (start us, length us, event | category | flops | bytes accessed | tf_op | source)
XLA Modules:
  0.0 96.5 jit_solution(17731183949919784960)
XLA Ops:
  3.3 3.0 %collective-permute-start = (bf16[144,512]{1,0:T(8,128)(2,1)S(1)}, bf16[144,512]{1,0:T(8,128)(2,1)S(1)}, u32[]{:S(2)}, u32[]{:S(2)}) collective-permute-start(bf16[144,512]{1,0:T(8,128)(2,1)S(1)} %get-tuple-element.96), channel_id=1, source_target_pairs={{0,16},{4,20},{8,24},{12,28},{16,0},{20,4},{24,8},{28,12},{1,17},{... | collective-permute-start | bytes 442376 | tf_op jit(solution)/shard_map/ppermute | solution.py:227
  9.2 1.8 %collective-permute-done.refs_2_ = bf16[144,512]{1,0:T(8,128)(2,1)S(1)} collective-permute-done((bf16[144,512]{1,0:T(8,128)(2,1)S(1)}, bf16[144,512]{1,0:T(8,128)(2,1)S(1)}, u32[]{:S(2)}, u32[]{:S(2)}) %collective-permute-start) | collective-permute-done | bytes 147488 | tf_op jit(solution)/shard_map/ppermute | solution.py:227
  12.6 2.2 %collective-permute-start.4 = (bf16[128,512]{1,0:T(8,128)(2,1)S(1)}, bf16[128,512]{1,0:T(8,128)(2,1)S(1)}, u32[]{:S(2)}, u32[]{:S(2)}) collective-permute-start(bf16[128,512]{1,0:T(8,128)(2,1)S(1)} %get-tuple-element.44), channel_id=1, source_target_pairs={{0,24},{4,28},{8,16},{12,20},{16,8},{20,12},{24,0},{28,4},{1,25},{... | collective-permute-start | bytes 393224 | tf_op jit(solution)/shard_map/ppermute | solution.py:227
  15.1 2.0 %collective-permute-start.7 = (bf16[144,512]{1,0:T(8,128)(2,1)S(1)}, bf16[144,512]{1,0:T(8,128)(2,1)S(1)}, u32[]{:S(2)}, u32[]{:S(2)}) collective-permute-start(bf16[144,512]{1,0:T(8,128)(2,1)S(1)} %collective-permute-done.refs_2_), channel_id=1, source_target_pairs={{0,4},{4,0},{1,5},{5,1},{2,6},{6,2},{3,7},{7,3},{8,12},{12,8},{9,1... | collective-permute-start | bytes 442376 | tf_op jit(solution)/shard_map/ppermute | solution.py:19
  19.5 2.2 %collective-permute-done.3.refs_2_ = bf16[128,512]{1,0:T(8,128)(2,1)S(1)} collective-permute-done((bf16[128,512]{1,0:T(8,128)(2,1)S(1)}, bf16[128,512]{1,0:T(8,128)(2,1)S(1)}, u32[]{:S(2)}, u32[]{:S(2)}) %collective-permute-start.3) | collective-permute-done | bytes 131104 | tf_op jit(solution)/shard_map/ppermute | solution.py:227
  21.8 2.7 %collective-permute-done.8.refs_7_ = bf16[144,512]{1,0:T(8,128)(2,1)S(1)} collective-permute-done((bf16[144,512]{1,0:T(8,128)(2,1)S(1)}, bf16[144,512]{1,0:T(8,128)(2,1)S(1)}, u32[]{:S(2)}, u32[]{:S(2)}) %collective-permute-start.8) | collective-permute-done | bytes 147488 | tf_op jit(solution)/shard_map/ppermute | solution.py:19
  24.5 1.7 %collective-permute-start.9 = (bf16[4,128,512]{2,1,0:T(8,128)(2,1)S(1)}, bf16[4,128,512]{2,1,0:T(8,128)(2,1)S(1)}, u32[]{:S(2)}, u32[]{:S(2)}) collective-permute-start(bf16[4,128,512]{2,1,0:T(8,128)(2,1)S(1)} %pad_maximum_fusion.refs_8_), channel_id=1, source_target_pairs={{0,4},{4,0},{1,5},{5,1},{2,6},{6,2},{3,7},{7,3},{8,12},{12,8},{9,1... | collective-permute-start | bytes 1572872 | tf_op jit(solution)/shard_map/ppermute | solution.py:19
  26.7 1.7 %convolution_convert_fusion.1 = bf16[16,64,352]{2,1,0:T(8,128)(2,1)S(1)} fusion(bf16[16,64,512]{2,1,0:T(8,128)(2,1)S(1)} %get-tuple-element.70.placed, bf16[16,512,352]{1,2,0:T(8,128)(2,1)S(1)} %bitcast.53), kind=kOutput, calls=%fused_computation.1 | convolution fusion | flops 369459200 | bytes 7536640 | tf_op jit(solution)/shard_map/esd,ehd->esh/dot_general | solution.py:245
  32.0 1.8 %collective-permute-start.15 = (bf16[2,16,16,352]{3,2,1,0:T(8,128)(2,1)S(1)}, bf16[2,16,16,352]{3,2,1,0:T(8,128)(2,1)S(1)}, u32[]{:S(2)}, u32[]{:S(2)}) collective-permute-start(bf16[2,16,16,352]{3,2,1,0:T(8,128)(2,1)S(1)} %pad_maximum_fusion.2.refs_6_), channel_id=1, source_target_pairs={{0,16},{8,24},{16,0},{24,8},{1,17},{9,25},{17,1},{25,9},{2,18},{10... | collective-permute-start | bytes 1081352 | tf_op jit(solution)/shard_map/ppermute | solution.py:19
  33.8 4.2 %collective-permute-done.9.refs_4_ = bf16[4,128,512]{2,1,0:T(8,128)(2,1)S(1)} collective-permute-done((bf16[4,128,512]{2,1,0:T(8,128)(2,1)S(1)}, bf16[4,128,512]{2,1,0:T(8,128)(2,1)S(1)}, u32[]{:S(2)}, u32[]{:S(2)}) %collective-permute-start.9) | collective-permute-done | bytes 524320 | tf_op jit(solution)/shard_map/ppermute | solution.py:19
  39.4 1.7 %convolution_convert_fusion = bf16[16,64,352]{2,1,0:T(8,128)(2,1)S(1)} fusion(bf16[16,64,512]{2,1,0:T(8,128)(2,1)S(1)} %shard_map.86, bf16[16,512,352]{1,2,0:T(8,128)(2,1)S(1)} %bitcast.64), kind=kOutput, calls=%fused_computation | convolution fusion | flops 369459200 | bytes 7536640 | tf_op jit(solution)/shard_map/esd,ehd->esh/dot_general | solution.py:245
  43.5 1.8 %collective-permute-start.16 = (bf16[16,16,352]{2,1,0:T(8,128)(2,1)S(1)}, bf16[16,16,352]{2,1,0:T(8,128)(2,1)S(1)}, u32[]{:S(2)}, u32[]{:S(2)}) collective-permute-start(bf16[16,16,352]{2,1,0:T(8,128)(2,1)S(1)} %add_convert_fusion), channel_id=1, source_target_pairs={{0,16},{8,24},{16,0},{24,8},{1,17},{9,25},{17,1},{25,9},{2,18},{10... | collective-permute-start | bytes 540680 | tf_op jit(solution)/shard_map/ppermute | solution.py:19
  45.3 4.7 %collective-permute-done.16 = bf16[16,16,352]{2,1,0:T(8,128)(2,1)S(1)} collective-permute-done((bf16[16,16,352]{2,1,0:T(8,128)(2,1)S(1)}, bf16[16,16,352]{2,1,0:T(8,128)(2,1)S(1)}, u32[]{:S(2)}, u32[]{:S(2)}) %collective-permute-start.16) | collective-permute-done | bytes 180256 | tf_op jit(solution)/shard_map/ppermute | solution.py:19
  50.7 1.8 %collective-permute-start.19 = (bf16[7,16,704]{2,1,0:T(8,128)(2,1)S(1)}, bf16[7,16,704]{2,1,0:T(8,128)(2,1)S(1)}, u32[]{:S(2)}, u32[]{:S(2)}) collective-permute-start(bf16[7,16,704]{2,1,0:T(8,128)(2,1)S(1)} %fusion.10), channel_id=1, source_target_pairs={{0,16},{8,24},{16,0},{24,8},{1,17},{9,25},{17,1},{25,9},{2,18},{10... | collective-permute-start | bytes 473096 | tf_op jit(solution)/shard_map/ppermute | solution.py:19
  53.0 2.5 %shard_map.87 = (bf16[128,512]{1,0:T(8,128)(2,1)S(1)}, bf16[128,512]{1,0:T(8,128)(2,1)S(1)}, bf16[128,512]{1,0:T(8,128)(2,1)S(1)}, bf16[128,512]{1,0:T(8,128)(2,1)S(1)}, bf16[16,704,512]{2,1,0:T(8,128)(2,1)S(1)}) custom-call(s32[4,8,256]{2,1,0:T(8,128)S(1)} %get-tuple-element.54.refs_5_.refs_0_.refs_1_, ...), custom_call_target="tpu_custom_call" | custom-call | flops 1476395008 | bytes 11534336 | tf_op jit(solution)/shard_map/pallas_call | solution.py:148
  55.5 4.2 %copy-done = bf16[16,704,512]{2,1,0:T(8,128)(2,1)} copy-done((bf16[16,704,512]{2,1,0:T(8,128)(2,1)}, bf16[16,704,512]{2,1,0:T(8,128)(2,1)S(1)}, u32[]{:S(2)}) %copy-start) | copy-done | bytes 11534360
  61.6 4.3 %copy-done.1 = bf16[16,704,512]{2,1,0:T(8,128)(2,1)S(1)} copy-done((bf16[16,704,512]{2,1,0:T(8,128)(2,1)S(1)}, bf16[16,704,512]{2,1,0:T(8,128)(2,1)}, u32[]{:S(2)}) %copy-start.1) | copy-done | bytes 11534360
  68.5 1.7 %copy-done.2 = bf16[16,704,512]{2,1,0:T(8,128)(2,1)S(1)} copy-done((bf16[16,704,512]{2,1,0:T(8,128)(2,1)S(1)}, bf16[16,704,512]{2,1,0:T(8,128)(2,1)}, u32[]{:S(2)}) %copy-start.2) | copy-done | bytes 11534360
  71.6 1.8 %collective-permute-start.24 = (bf16[128,512]{1,0:T(8,128)(2,1)S(1)}, bf16[128,512]{1,0:T(8,128)(2,1)S(1)}, u32[]{:S(2)}, u32[]{:S(2)}) collective-permute-start(bf16[128,512]{1,0:T(8,128)(2,1)S(1)} %get-tuple-element.62), channel_id=1, source_target_pairs={{0,16},{1,24},{2,18},{3,26},{4,20},{5,28},{6,22},{7,30},{8,17},{9,... | collective-permute-start | bytes 393224 | tf_op jit(solution)/shard_map/ppermute | solution.py:294
  74.4 2.0 %collective-permute-start.26 = (bf16[128,512]{1,0:T(8,128)(2,1)S(1)}, bf16[128,512]{1,0:T(8,128)(2,1)S(1)}, u32[]{:S(2)}, u32[]{:S(2)}) collective-permute-start(bf16[128,512]{1,0:T(8,128)(2,1)S(1)} %get-tuple-element.64), channel_id=1, source_target_pairs={{0,24},{1,16},{2,26},{3,18},{4,28},{5,20},{6,30},{7,22},{8,25},{9,... | collective-permute-start | bytes 393224 | tf_op jit(solution)/shard_map/ppermute | solution.py:294
  76.9 1.9 %collective-permute-start.31 = (bf16[128,512]{1,0:T(8,128)(2,1)S(1)}, bf16[128,512]{1,0:T(8,128)(2,1)S(1)}, u32[]{:S(2)}, u32[]{:S(2)}) collective-permute-start(bf16[128,512]{1,0:T(8,128)(2,1)S(1)} %broadcast_select_fusion), channel_id=1, source_target_pairs={{0,1},{1,0},{2,3},{3,2},{4,5},{5,4},{6,7},{7,6},{8,9},{9,8},{10,11... | collective-permute-start | bytes 393224 | tf_op jit(solution)/shard_map/ppermute | solution.py:19
  78.8 5.7 %shard_map.90 = (bf16[16,352,512]{2,1,0:T(8,128)(2,1)}, bf16[16,352,512]{2,1,0:T(8,128)(2,1)}) custom-call(bf16[16,64,512]{2,1,0:T(8,128)(2,1)S(1)} %get-tuple-element.70.placed, bf16[16,16,704]{2,1,0:T(8,128)(2,1)S(1)} %pad_maximum_fusion.1.refs_1_.h0, bf16[16,16,704]{2,1,0:T(8,128)(2,1)S(1)} %collective-permute-done.20.refs_2_.h1, ...), custom_call_target="tpu_custom_call" | custom-call | flops 2952790016 | bytes 11534336 | tf_op jit(solution)/shard_map/pallas_call | solution.py:179
  86.0 2.6 %collective-permute-start.32 = (bf16[128,512]{1,0:T(8,128)(2,1)S(1)}, bf16[128,512]{1,0:T(8,128)(2,1)S(1)}, u32[]{:S(2)}, u32[]{:S(2)}) collective-permute-start(bf16[128,512]{1,0:T(8,128)(2,1)S(1)} %select_convert_fusion), channel_id=1, source_target_pairs={{0,2},{1,3},{2,0},{3,1},{4,6},{5,7},{6,4},{7,5},{8,10},{9,11},{10,... | collective-permute-start | bytes 393224 | tf_op jit(solution)/shard_map/ppermute | solution.py:19
  88.6 7.1 %collective-permute-done.32 = bf16[128,512]{1,0:T(8,128)(2,1)S(1)} collective-permute-done((bf16[128,512]{1,0:T(8,128)(2,1)S(1)}, bf16[128,512]{1,0:T(8,128)(2,1)S(1)}, u32[]{:S(2)}, u32[]{:S(2)}) %collective-permute-start.32) | collective-permute-done | bytes 131104 | tf_op jit(solution)/shard_map/ppermute | solution.py:19
  (95 shorter events, 28.7 us)
Async XLA Ops:
  3.3 7.7 %collective-permute-start = (bf16[144,512]{1,0:T(8,128)(2,1)S(1)}, bf16[144,512]{1,0:T(8,128)(2,1)S(1)}, u32[]{:S(2)}, u32[]{:S(2)}) collective-permute-start(bf16[144,512]{1,0:T(8,128)(2,1)S(1)} %get-tuple-element.96), channel_id=1, source_target_pairs={{0,16},{4,20},{8,24},{12,28},{16,0},{20,4},{24,8},{28,12},{1,17},{... | collective-permute-start | bytes 442376 | tf_op jit(solution)/shard_map/ppermute | solution.py:227
  6.4 6.3 %collective-permute-start.1 = (bf16[144,512]{1,0:T(8,128)(2,1)S(1)}, bf16[144,512]{1,0:T(8,128)(2,1)S(1)}, u32[]{:S(2)}, u32[]{:S(2)}) collective-permute-start(bf16[144,512]{1,0:T(8,128)(2,1)S(1)} %get-tuple-element.95), channel_id=1, source_target_pairs={{0,24},{4,28},{8,16},{12,20},{16,8},{20,12},{24,0},{28,4},{1,25},{... | collective-permute-start | bytes 442376 | tf_op jit(solution)/shard_map/ppermute | solution.py:227
  6.4 8.8 %collective-permute-start.5 = (bf16[144,512]{1,0:T(8,128)(2,1)S(1)}, bf16[144,512]{1,0:T(8,128)(2,1)S(1)}, u32[]{:S(2)}, u32[]{:S(2)}) collective-permute-start(bf16[144,512]{1,0:T(8,128)(2,1)S(1)} %get-tuple-element.97.refs_0_), channel_id=1, source_target_pairs={{0,4},{4,0},{8,12},{12,8},{16,20},{20,16},{24,28},{28,24},{1,5},{5... | collective-permute-start | bytes 442376 | tf_op jit(solution)/shard_map/ppermute | solution.py:227
  7.9 7.3 %collective-permute-start.6 = (bf16[144,512]{1,0:T(8,128)(2,1)S(1)}, bf16[144,512]{1,0:T(8,128)(2,1)S(1)}, u32[]{:S(2)}, u32[]{:S(2)}) collective-permute-start(bf16[144,512]{1,0:T(8,128)(2,1)S(1)} %get-tuple-element.98), channel_id=1, source_target_pairs={{0,12},{4,8},{8,4},{12,0},{16,28},{20,24},{24,20},{28,16},{1,13},{... | collective-permute-start | bytes 442376 | tf_op jit(solution)/shard_map/ppermute | solution.py:227
  12.6 6.0 %collective-permute-start.4 = (bf16[128,512]{1,0:T(8,128)(2,1)S(1)}, bf16[128,512]{1,0:T(8,128)(2,1)S(1)}, u32[]{:S(2)}, u32[]{:S(2)}) collective-permute-start(bf16[128,512]{1,0:T(8,128)(2,1)S(1)} %get-tuple-element.44), channel_id=1, source_target_pairs={{0,24},{4,28},{8,16},{12,20},{16,8},{20,12},{24,0},{28,4},{1,25},{... | collective-permute-start | bytes 393224 | tf_op jit(solution)/shard_map/ppermute | solution.py:227
  14.8 6.9 %collective-permute-start.3 = (bf16[128,512]{1,0:T(8,128)(2,1)S(1)}, bf16[128,512]{1,0:T(8,128)(2,1)S(1)}, u32[]{:S(2)}, u32[]{:S(2)}) collective-permute-start(bf16[128,512]{1,0:T(8,128)(2,1)S(1)} %get-tuple-element.43), channel_id=1, source_target_pairs={{0,16},{4,20},{8,24},{12,28},{16,0},{20,4},{24,8},{28,12},{1,17},{... | collective-permute-start | bytes 393224 | tf_op jit(solution)/shard_map/ppermute | solution.py:227
  15.1 6.6 %collective-permute-start.2 = (bf16[128,512]{1,0:T(8,128)(2,1)S(1)}, bf16[128,512]{1,0:T(8,128)(2,1)S(1)}, u32[]{:S(2)}, u32[]{:S(2)}) collective-permute-start(bf16[128,512]{1,0:T(8,128)(2,1)S(1)} %get-tuple-element.42), channel_id=1, source_target_pairs={{0,8},{4,12},{8,0},{12,4},{16,24},{20,28},{24,16},{28,20},{1,9},{5... | collective-permute-start | bytes 393224 | tf_op jit(solution)/shard_map/ppermute | solution.py:227
  15.1 6.7 %collective-permute-start.7 = (bf16[144,512]{1,0:T(8,128)(2,1)S(1)}, bf16[144,512]{1,0:T(8,128)(2,1)S(1)}, u32[]{:S(2)}, u32[]{:S(2)}) collective-permute-start(bf16[144,512]{1,0:T(8,128)(2,1)S(1)} %collective-permute-done.refs_2_), channel_id=1, source_target_pairs={{0,4},{4,0},{1,5},{5,1},{2,6},{6,2},{3,7},{7,3},{8,12},{12,8},{9,1... | collective-permute-start | bytes 442376 | tf_op jit(solution)/shard_map/ppermute | solution.py:19
  17.1 7.4 %collective-permute-start.8 = (bf16[144,512]{1,0:T(8,128)(2,1)S(1)}, bf16[144,512]{1,0:T(8,128)(2,1)S(1)}, u32[]{:S(2)}, u32[]{:S(2)}) collective-permute-start(bf16[144,512]{1,0:T(8,128)(2,1)S(1)} %collective-permute-done.1.refs_3_), channel_id=1, source_target_pairs={{0,4},{4,0},{1,5},{5,1},{2,6},{6,2},{3,7},{7,3},{8,12},{12,8},{9,1... | collective-permute-start | bytes 442376 | tf_op jit(solution)/shard_map/ppermute | solution.py:19
  18.7 7.6 %collective-permute-start.10 = (bf16[144,512]{1,0:T(8,128)(2,1)S(1)}, bf16[144,512]{1,0:T(8,128)(2,1)S(1)}, u32[]{:S(2)}, u32[]{:S(2)}) collective-permute-start(bf16[144,512]{1,0:T(8,128)(2,1)S(1)} %get-tuple-element.98), channel_id=1, source_target_pairs={{0,8},{4,12},{8,0},{12,4},{16,24},{20,28},{24,16},{28,20},{1,9},{5... | collective-permute-start | bytes 442376 | tf_op jit(solution)/shard_map/ppermute | solution.py:227
  24.5 13.5 %collective-permute-start.9 = (bf16[4,128,512]{2,1,0:T(8,128)(2,1)S(1)}, bf16[4,128,512]{2,1,0:T(8,128)(2,1)S(1)}, u32[]{:S(2)}, u32[]{:S(2)}) collective-permute-start(bf16[4,128,512]{2,1,0:T(8,128)(2,1)S(1)} %pad_maximum_fusion.refs_8_), channel_id=1, source_target_pairs={{0,4},{4,0},{1,5},{5,1},{2,6},{6,2},{3,7},{7,3},{8,12},{12,8},{9,1... | collective-permute-start | bytes 1572872 | tf_op jit(solution)/shard_map/ppermute | solution.py:19
  32.0 11.5 %collective-permute-start.15 = (bf16[2,16,16,352]{3,2,1,0:T(8,128)(2,1)S(1)}, bf16[2,16,16,352]{3,2,1,0:T(8,128)(2,1)S(1)}, u32[]{:S(2)}, u32[]{:S(2)}) collective-permute-start(bf16[2,16,16,352]{3,2,1,0:T(8,128)(2,1)S(1)} %pad_maximum_fusion.2.refs_6_), channel_id=1, source_target_pairs={{0,16},{8,24},{16,0},{24,8},{1,17},{9,25},{17,1},{25,9},{2,18},{10... | collective-permute-start | bytes 1081352 | tf_op jit(solution)/shard_map/ppermute | solution.py:19
  41.2 4.1 %collective-permute-start.17 = (bf16[16,16,352]{2,1,0:T(8,128)(2,1)S(1)}, bf16[16,16,352]{2,1,0:T(8,128)(2,1)S(1)}, u32[]{:S(2)}, u32[]{:S(2)}) collective-permute-start(bf16[16,16,352]{2,1,0:T(8,128)(2,1)S(1)} %get-tuple-element.81), channel_id=1, source_target_pairs={{0,8},{8,0},{16,24},{24,16},{1,9},{9,1},{17,25},{25,17},{2,10},{10... | collective-permute-start | bytes 540680 | tf_op jit(solution)/shard_map/ppermute | solution.py:19
  41.7 3.6 %collective-permute-start.18 = (bf16[16,16,352]{2,1,0:T(8,128)(2,1)S(1)}, bf16[16,16,352]{2,1,0:T(8,128)(2,1)S(1)}, u32[]{:S(2)}, u32[]{:S(2)}) collective-permute-start(bf16[16,16,352]{2,1,0:T(8,128)(2,1)S(1)} %get-tuple-element.83), channel_id=1, source_target_pairs={{0,8},{8,0},{16,24},{24,16},{1,9},{9,1},{17,25},{25,17},{2,10},{10... | collective-permute-start | bytes 540680 | tf_op jit(solution)/shard_map/ppermute | solution.py:19
  43.5 6.4 %collective-permute-start.16 = (bf16[16,16,352]{2,1,0:T(8,128)(2,1)S(1)}, bf16[16,16,352]{2,1,0:T(8,128)(2,1)S(1)}, u32[]{:S(2)}, u32[]{:S(2)}) collective-permute-start(bf16[16,16,352]{2,1,0:T(8,128)(2,1)S(1)} %add_convert_fusion), channel_id=1, source_target_pairs={{0,16},{8,24},{16,0},{24,8},{1,17},{9,25},{17,1},{25,9},{2,18},{10... | collective-permute-start | bytes 540680 | tf_op jit(solution)/shard_map/ppermute | solution.py:19
  50.7 9.0 %collective-permute-start.19 = (bf16[7,16,704]{2,1,0:T(8,128)(2,1)S(1)}, bf16[7,16,704]{2,1,0:T(8,128)(2,1)S(1)}, u32[]{:S(2)}, u32[]{:S(2)}) collective-permute-start(bf16[7,16,704]{2,1,0:T(8,128)(2,1)S(1)} %fusion.10), channel_id=1, source_target_pairs={{0,16},{8,24},{16,0},{24,8},{1,17},{9,25},{17,1},{25,9},{2,18},{10... | collective-permute-start | bytes 473096 | tf_op jit(solution)/shard_map/ppermute | solution.py:19
  52.6 14.3 %collective-permute-start.22 = (bf16[9,16,704]{2,1,0:T(8,128)(2,1)S(1)}, bf16[9,16,704]{2,1,0:T(8,128)(2,1)S(1)}, u32[]{:S(2)}, u32[]{:S(2)}) collective-permute-start(bf16[9,16,704]{2,1,0:T(8,128)(2,1)S(1)} %fusion.7), channel_id=1, source_target_pairs={{0,16},{8,24},{16,0},{24,8},{1,17},{9,25},{17,1},{25,9},{2,18},{10... | collective-permute-start | bytes 608264 | tf_op jit(solution)/shard_map/ppermute | solution.py:19
  67.1 9.7 %collective-permute-start.30 = (bf16[2,128,512]{2,1,0:T(8,128)(2,1)S(1)}, bf16[2,128,512]{2,1,0:T(8,128)(2,1)S(1)}, u32[]{:S(2)}, u32[]{:S(2)}) collective-permute-start(bf16[2,128,512]{2,1,0:T(8,128)(2,1)S(1)} %pad_maximum_fusion.5), channel_id=1, source_target_pairs={{0,4},{4,0},{1,5},{5,1},{2,6},{6,2},{3,7},{7,3},{8,12},{12,8},{9,1... | collective-permute-start | bytes 786440 | tf_op jit(solution)/shard_map/ppermute | solution.py:19
  71.6 12.9 %collective-permute-start.24 = (bf16[128,512]{1,0:T(8,128)(2,1)S(1)}, bf16[128,512]{1,0:T(8,128)(2,1)S(1)}, u32[]{:S(2)}, u32[]{:S(2)}) collective-permute-start(bf16[128,512]{1,0:T(8,128)(2,1)S(1)} %get-tuple-element.62), channel_id=1, source_target_pairs={{0,16},{1,24},{2,18},{3,26},{4,20},{5,28},{6,22},{7,30},{8,17},{9,... | collective-permute-start | bytes 393224 | tf_op jit(solution)/shard_map/ppermute | solution.py:294
  73.4 11.2 %collective-permute-start.25 = (bf16[128,512]{1,0:T(8,128)(2,1)S(1)}, bf16[128,512]{1,0:T(8,128)(2,1)S(1)}, u32[]{:S(2)}, u32[]{:S(2)}) collective-permute-start(bf16[128,512]{1,0:T(8,128)(2,1)S(1)} %get-tuple-element.63), channel_id=1, source_target_pairs={{0,20},{1,28},{2,22},{3,30},{4,16},{5,24},{6,18},{7,26},{8,21},{9,... | collective-permute-start | bytes 393224 | tf_op jit(solution)/shard_map/ppermute | solution.py:294
  74.4 11.3 %collective-permute-start.26 = (bf16[128,512]{1,0:T(8,128)(2,1)S(1)}, bf16[128,512]{1,0:T(8,128)(2,1)S(1)}, u32[]{:S(2)}, u32[]{:S(2)}) collective-permute-start(bf16[128,512]{1,0:T(8,128)(2,1)S(1)} %get-tuple-element.64), channel_id=1, source_target_pairs={{0,24},{1,16},{2,26},{3,18},{4,28},{5,20},{6,30},{7,22},{8,25},{9,... | collective-permute-start | bytes 393224 | tf_op jit(solution)/shard_map/ppermute | solution.py:294
  76.4 9.4 %collective-permute-start.27 = (bf16[128,512]{1,0:T(8,128)(2,1)S(1)}, bf16[128,512]{1,0:T(8,128)(2,1)S(1)}, u32[]{:S(2)}, u32[]{:S(2)}) collective-permute-start(bf16[128,512]{1,0:T(8,128)(2,1)S(1)} %get-tuple-element.65), channel_id=1, source_target_pairs={{0,28},{1,20},{2,30},{3,22},{4,24},{5,16},{6,26},{7,18},{8,29},{9,... | collective-permute-start | bytes 393224 | tf_op jit(solution)/shard_map/ppermute | solution.py:294
  76.9 8.9 %collective-permute-start.31 = (bf16[128,512]{1,0:T(8,128)(2,1)S(1)}, bf16[128,512]{1,0:T(8,128)(2,1)S(1)}, u32[]{:S(2)}, u32[]{:S(2)}) collective-permute-start(bf16[128,512]{1,0:T(8,128)(2,1)S(1)} %broadcast_select_fusion), channel_id=1, source_target_pairs={{0,1},{1,0},{2,3},{3,2},{4,5},{5,4},{6,7},{7,6},{8,9},{9,8},{10,11... | collective-permute-start | bytes 393224 | tf_op jit(solution)/shard_map/ppermute | solution.py:19
  86.0 9.7 %collective-permute-start.32 = (bf16[128,512]{1,0:T(8,128)(2,1)S(1)}, bf16[128,512]{1,0:T(8,128)(2,1)S(1)}, u32[]{:S(2)}, u32[]{:S(2)}) collective-permute-start(bf16[128,512]{1,0:T(8,128)(2,1)S(1)} %select_convert_fusion), channel_id=1, source_target_pairs={{0,2},{1,3},{2,0},{3,1},{4,6},{5,7},{6,4},{7,5},{8,10},{9,11},{10,... | collective-permute-start | bytes 393224 | tf_op jit(solution)/shard_map/ppermute | solution.py:19
  (18 other events, 64.1 us)

commit v5 on v4

--- a/solution.py
+++ b/solution.py
@@ -207,6 +207,8 @@
     k, x, t = lax.axis_index("dp"), lax.axis_index("expert"), lax.axis_index("tensor")
     width = gate_weight.shape[1]
     rows = tokens.shape[0]
+    odd, swapped = ((k ^ t) & 1) == 1, ((k ^ t) & 2) == 2
+    expert_ids, odd, swapped = lax.optimization_barrier((expert_ids, odd, swapped))
     ids_row = expert_ids.reshape(1, rows)
     order = jnp.arange(rows, dtype=jnp.int32)
     earlier = (expert_ids == ids_row) & (order[:, None] < order[None, :])
@@ -294,13 +296,11 @@
         return lax.ppermute(value, ("dp", "expert", "tensor"), pairs)
 
     merged = [plus(own, arrived[0]).astype(BF16), plus(own_beside, arrived[1]).astype(BF16)]
-    odd = ((k ^ t) & 1) == 1
     keep, leaving = jnp.where(odd, merged[1], merged[0]), jnp.where(odd, merged[0], merged[1])
     first = plus(keep, swap(leaving, "tensor", n_t, 1))
     far_terms = [to_keeper(value, 2, at // 2, at % 2) for at, value in enumerate(far_back)]
     far_terms, _ = lax.optimization_barrier((far_terms, weight_grad))
     second = sum(value.astype(F32) for value in far_terms)
-    swapped = ((k ^ t) & 2) == 2
     keep = jnp.where(swapped, second, first)
     leaving = jnp.where(swapped, first, second).astype(BF16)
     grad_tokens = plus(keep, swap(leaving, "tensor", n_t, 2)).astype(BF16)

time: 96.8 us -> 90.1 us (0.931)
  local copies, waits for them, and re-layouts: 13.6 us -> 3.37 us
  waiting for transfers between devices: 30.6 us -> 34.5 us
    unnamed x18 -> x12, local copies, waits for them, and re-layouts: 11.2 us -> 0.98 us
    ppermute x21, waiting for transfers between devices: 22.4 us -> 27.1 us  [swap(): return lax.ppermute(value, axis, [(i, i ^ bit) for i in range(count)])]
  transfers between devices with their start and end apart: 33 -> 33, of which waited for: 14 -> 17; matrix products, arithmetic and copies ran while one was open for 7% -> 8% of each run, Pallas kernels for 12% -> 13%
where the time goes in v5:
time: 90.1 us; the launch traced here: 89.9 us
  waiting for transfers between devices  34.5 us (38%)
  starting transfers between devices  30.9 us (34%)
  Pallas kernels  11.6 us (13%)
  matrix products  4.98 us (6%)
  other arithmetic  3.75 us (4%)
  local copies, waits for them, and re-layouts  3.37 us (4%)
  between operations  0.94 us (1%)
    ppermute x21, waiting for transfers between devices, swap(): return lax.ppermute(value, axis, [(i, i ^ bit) for i in range(count)])  27.1 us
    ppermute x21, starting transfers between devices, swap(): return lax.ppermute(value, axis, [(i, i ^ bit) for i in range(count)])  17.7 us
    ppermute x8, starting transfers between devices, to_owner(): return lax.ppermute(value, ('dp', 'expert'), pairs)  8.11 us
    ppermute x8, waiting for transfers between devices, to_owner(): return lax.ppermute(value, ('dp', 'expert'), pairs)  7.02 us
    pallas_call x1, Pallas kernels, weight_grads(): pl.pallas_call(weight_kernel, grid=(local_experts // per_step,), out_shap...  5.75 us
    ppermute x4, starting transfers between devices, to_keeper(): return lax.ppermute(value, ('dp', 'expert', 'tensor'), pairs)  5.03 us
    dot_general x3, matrix products, project(): jnp.einsum('esd,ehd->esh', values, weight, preferred_element_type=F32)  4.98 us
    pallas_call x3, Pallas kernels, back(): pl.pallas_call(functools.partial(back_kernel, low, first, last), out_shap...  4.93 us
  transfers between devices with their start and end apart: 33, of which 17 were waited for; matrix products, arithmetic and copies ran while one was open for 8% of the time, Pallas kernels for 13%

profile of v5, /device:TPU:0, one launch (start us, length us, event | category | flops | bytes accessed | tf_op | source)
XLA Modules:
  0.0 89.9 jit_solution(7859733254711658803)
XLA Ops:
  3.3 3.0 %collective-permute-start = (bf16[144,512]{1,0:T(8,128)(2,1)S(1)}, bf16[144,512]{1,0:T(8,128)(2,1)S(1)}, u32[]{:S(2)}, u32[]{:S(2)}) collective-permute-start(bf16[144,512]{1,0:T(8,128)(2,1)S(1)} %get-tuple-element.102), channel_id=1, source_target_pairs={{0,16},{4,20},{8,24},{12,28},{16,0},{20,4},{24,8},{28,12},{1,17},{... | collective-permute-start | bytes 442376 | tf_op jit(solution)/shard_map/ppermute | solution.py:229
  9.2 1.8 %collective-permute-done.refs_2_ = bf16[144,512]{1,0:T(8,128)(2,1)S(1)} collective-permute-done((bf16[144,512]{1,0:T(8,128)(2,1)S(1)}, bf16[144,512]{1,0:T(8,128)(2,1)S(1)}, u32[]{:S(2)}, u32[]{:S(2)}) %collective-permute-start) | collective-permute-done | bytes 147488 | tf_op jit(solution)/shard_map/ppermute | solution.py:229
  11.0 1.6 %collective-permute-done.1.refs_3_ = bf16[144,512]{1,0:T(8,128)(2,1)S(1)} collective-permute-done((bf16[144,512]{1,0:T(8,128)(2,1)S(1)}, bf16[144,512]{1,0:T(8,128)(2,1)S(1)}, u32[]{:S(2)}, u32[]{:S(2)}) %collective-permute-start.1) | collective-permute-done | bytes 147488 | tf_op jit(solution)/shard_map/ppermute | solution.py:229
  12.6 2.2 %collective-permute-start.4 = (bf16[128,512]{1,0:T(8,128)(2,1)S(1)}, bf16[128,512]{1,0:T(8,128)(2,1)S(1)}, u32[]{:S(2)}, u32[]{:S(2)}) collective-permute-start(bf16[128,512]{1,0:T(8,128)(2,1)S(1)} %get-tuple-element.49), channel_id=1, source_target_pairs={{0,24},{4,28},{8,16},{12,20},{16,8},{20,12},{24,0},{28,4},{1,25},{... | collective-permute-start | bytes 393224 | tf_op jit(solution)/shard_map/ppermute | solution.py:229
  15.1 2.0 %collective-permute-start.7 = (bf16[144,512]{1,0:T(8,128)(2,1)S(1)}, bf16[144,512]{1,0:T(8,128)(2,1)S(1)}, u32[]{:S(2)}, u32[]{:S(2)}) collective-permute-start(bf16[144,512]{1,0:T(8,128)(2,1)S(1)} %collective-permute-done.refs_2_), channel_id=1, source_target_pairs={{0,4},{4,0},{1,5},{5,1},{2,6},{6,2},{3,7},{7,3},{8,12},{12,8},{9,1... | collective-permute-start | bytes 442376 | tf_op jit(solution)/shard_map/ppermute | solution.py:19
  19.5 2.2 %collective-permute-done.3.refs_2_ = bf16[128,512]{1,0:T(8,128)(2,1)S(1)} collective-permute-done((bf16[128,512]{1,0:T(8,128)(2,1)S(1)}, bf16[128,512]{1,0:T(8,128)(2,1)S(1)}, u32[]{:S(2)}, u32[]{:S(2)}) %collective-permute-start.3) | collective-permute-done | bytes 131104 | tf_op jit(solution)/shard_map/ppermute | solution.py:229
  21.9 2.7 %collective-permute-done.8.refs_7_ = bf16[144,512]{1,0:T(8,128)(2,1)S(1)} collective-permute-done((bf16[144,512]{1,0:T(8,128)(2,1)S(1)}, bf16[144,512]{1,0:T(8,128)(2,1)S(1)}, u32[]{:S(2)}, u32[]{:S(2)}) %collective-permute-start.8) | collective-permute-done | bytes 147488 | tf_op jit(solution)/shard_map/ppermute | solution.py:19
  24.5 1.7 %collective-permute-start.9 = (bf16[4,128,512]{2,1,0:T(8,128)(2,1)S(1)}, bf16[4,128,512]{2,1,0:T(8,128)(2,1)S(1)}, u32[]{:S(2)}, u32[]{:S(2)}) collective-permute-start(bf16[4,128,512]{2,1,0:T(8,128)(2,1)S(1)} %pad_maximum_fusion.refs_8_), channel_id=1, source_target_pairs={{0,4},{4,0},{1,5},{5,1},{2,6},{6,2},{3,7},{7,3},{8,12},{12,8},{9,1... | collective-permute-start | bytes 1572872 | tf_op jit(solution)/shard_map/ppermute | solution.py:19
  26.7 1.7 %convolution_convert_fusion.1 = bf16[16,64,352]{2,1,0:T(8,128)(2,1)S(1)} fusion(bf16[16,64,512]{2,1,0:T(8,128)(2,1)S(1)} %get-tuple-element.75.placed, bf16[16,512,352]{1,2,0:T(8,128)(2,1)S(1)} %bitcast.53), kind=kOutput, calls=%fused_computation.1 | convolution fusion | flops 369459200 | bytes 7536640 | tf_op jit(solution)/shard_map/esd,ehd->esh/dot_general | solution.py:247
  28.6 1.7 %convolution_convert_fusion.2 = bf16[16,64,352]{2,1,0:T(8,128)(2,1)S(1)} fusion(bf16[16,64,512]{2,1,0:T(8,128)(2,1)S(1)} %get-tuple-element.75.placed, bf16[16,512,352]{1,2,0:T(8,128)(2,1)S(1)} %bitcast.56), kind=kOutput, calls=%fused_computation.2 | convolution fusion | flops 369459200 | bytes 7536640 | tf_op jit(solution)/shard_map/esd,ehd->esh/dot_general | solution.py:247
  32.0 1.8 %collective-permute-start.15 = (bf16[2,16,16,352]{3,2,1,0:T(8,128)(2,1)S(1)}, bf16[2,16,16,352]{3,2,1,0:T(8,128)(2,1)S(1)}, u32[]{:S(2)}, u32[]{:S(2)}) collective-permute-start(bf16[2,16,16,352]{3,2,1,0:T(8,128)(2,1)S(1)} %pad_maximum_fusion.2.refs_6_), channel_id=1, source_target_pairs={{0,16},{8,24},{16,0},{24,8},{1,17},{9,25},{17,1},{25,9},{2,18},{10... | collective-permute-start | bytes 1081352 | tf_op jit(solution)/shard_map/ppermute | solution.py:19
  33.8 4.2 %collective-permute-done.9.refs_4_ = bf16[4,128,512]{2,1,0:T(8,128)(2,1)S(1)} collective-permute-done((bf16[4,128,512]{2,1,0:T(8,128)(2,1)S(1)}, bf16[4,128,512]{2,1,0:T(8,128)(2,1)S(1)}, u32[]{:S(2)}, u32[]{:S(2)}) %collective-permute-start.9) | collective-permute-done | bytes 524320 | tf_op jit(solution)/shard_map/ppermute | solution.py:19
  39.4 1.7 %convolution_convert_fusion = bf16[16,64,352]{2,1,0:T(8,128)(2,1)S(1)} fusion(bf16[16,64,512]{2,1,0:T(8,128)(2,1)S(1)} %shard_map.86, bf16[16,512,352]{1,2,0:T(8,128)(2,1)S(1)} %bitcast.64), kind=kOutput, calls=%fused_computation | convolution fusion | flops 369459200 | bytes 7536640 | tf_op jit(solution)/shard_map/esd,ehd->esh/dot_general | solution.py:247
  43.5 1.7 %collective-permute-start.16 = (bf16[16,16,352]{2,1,0:T(8,128)(2,1)S(1)}, bf16[16,16,352]{2,1,0:T(8,128)(2,1)S(1)}, u32[]{:S(2)}, u32[]{:S(2)}) collective-permute-start(bf16[16,16,352]{2,1,0:T(8,128)(2,1)S(1)} %add_convert_fusion), channel_id=1, source_target_pairs={{0,16},{8,24},{16,0},{24,8},{1,17},{9,25},{17,1},{25,9},{2,18},{10... | collective-permute-start | bytes 540680 | tf_op jit(solution)/shard_map/ppermute | solution.py:19
  45.3 4.7 %collective-permute-done.16 = bf16[16,16,352]{2,1,0:T(8,128)(2,1)S(1)} collective-permute-done((bf16[16,16,352]{2,1,0:T(8,128)(2,1)S(1)}, bf16[16,16,352]{2,1,0:T(8,128)(2,1)S(1)}, u32[]{:S(2)}, u32[]{:S(2)}) %collective-permute-start.16) | collective-permute-done | bytes 180256 | tf_op jit(solution)/shard_map/ppermute | solution.py:19
  50.7 1.7 %collective-permute-start.19 = (bf16[7,16,704]{2,1,0:T(8,128)(2,1)S(1)}, bf16[7,16,704]{2,1,0:T(8,128)(2,1)S(1)}, u32[]{:S(2)}, u32[]{:S(2)}) collective-permute-start(bf16[7,16,704]{2,1,0:T(8,128)(2,1)S(1)} %fusion.10), channel_id=1, source_target_pairs={{0,16},{8,24},{16,0},{24,8},{1,17},{9,25},{17,1},{25,9},{2,18},{10... | collective-permute-start | bytes 473096 | tf_op jit(solution)/shard_map/ppermute | solution.py:19
  53.0 2.5 %shard_map.87 = (bf16[128,512]{1,0:T(8,128)(2,1)S(1)}, bf16[128,512]{1,0:T(8,128)(2,1)S(1)}, bf16[128,512]{1,0:T(8,128)(2,1)S(1)}, bf16[128,512]{1,0:T(8,128)(2,1)S(1)}, bf16[16,704,512]{2,1,0:T(8,128)(2,1)S(1)}) custom-call(s32[4,8,256]{2,1,0:T(8,128)S(1)} %get-tuple-element.59.refs_5_.refs_0_.refs_1_, ...), custom_call_target="tpu_custom_call" | custom-call | flops 1476395008 | bytes 11534336 | tf_op jit(solution)/shard_map/pallas_call | solution.py:148
  55.4 2.5 %collective-permute-done.19.refs_0_ = bf16[7,16,704]{2,1,0:T(8,128)(2,1)S(1)} collective-permute-done((bf16[7,16,704]{2,1,0:T(8,128)(2,1)S(1)}, bf16[7,16,704]{2,1,0:T(8,128)(2,1)S(1)}, u32[]{:S(2)}, u32[]{:S(2)}) %collective-permute-start.19) | collective-permute-done | bytes 157728 | tf_op jit(solution)/shard_map/ppermute | solution.py:19
  65.3 1.7 %collective-permute-start.24 = (bf16[128,512]{1,0:T(8,128)(2,1)S(1)}, bf16[128,512]{1,0:T(8,128)(2,1)S(1)}, u32[]{:S(2)}, u32[]{:S(2)}) collective-permute-start(bf16[128,512]{1,0:T(8,128)(2,1)S(1)} %get-tuple-element.67), channel_id=1, source_target_pairs={{0,16},{1,24},{2,18},{3,26},{4,20},{5,28},{6,22},{7,30},{8,17},{9,... | collective-permute-start | bytes 393224 | tf_op jit(solution)/shard_map/ppermute | solution.py:296
  68.0 1.9 %collective-permute-start.26 = (bf16[128,512]{1,0:T(8,128)(2,1)S(1)}, bf16[128,512]{1,0:T(8,128)(2,1)S(1)}, u32[]{:S(2)}, u32[]{:S(2)}) collective-permute-start(bf16[128,512]{1,0:T(8,128)(2,1)S(1)} %get-tuple-element.69), channel_id=1, source_target_pairs={{0,24},{1,16},{2,26},{3,18},{4,28},{5,20},{6,30},{7,22},{8,25},{9,... | collective-permute-start | bytes 393224 | tf_op jit(solution)/shard_map/ppermute | solution.py:296
  71.2 2.0 %collective-permute-start.31 = (bf16[128,512]{1,0:T(8,128)(2,1)S(1)}, bf16[128,512]{1,0:T(8,128)(2,1)S(1)}, u32[]{:S(2)}, u32[]{:S(2)}) collective-permute-start(bf16[128,512]{1,0:T(8,128)(2,1)S(1)} %broadcast_select_fusion), channel_id=1, source_target_pairs={{0,1},{1,0},{2,3},{3,2},{4,5},{5,4},{6,7},{7,6},{8,9},{9,8},{10,11... | collective-permute-start | bytes 393224 | tf_op jit(solution)/shard_map/ppermute | solution.py:19
  73.2 5.7 %shard_map.90 = (bf16[16,352,512]{2,1,0:T(8,128)(2,1)}, bf16[16,352,512]{2,1,0:T(8,128)(2,1)}) custom-call(bf16[16,64,512]{2,1,0:T(8,128)(2,1)S(1)} %get-tuple-element.75.placed, bf16[16,16,704]{2,1,0:T(8,128)(2,1)S(1)} %pad_maximum_fusion.1.refs_1_.h0, bf16[16,16,704]{2,1,0:T(8,128)(2,1)S(1)} %collective-permute-done.20.refs_2_.h1, ...), custom_call_target="tpu_custom_call" | custom-call | flops 2952790016 | bytes 11534336 | tf_op jit(solution)/shard_map/pallas_call | solution.py:179
  79.5 2.7 %collective-permute-start.32 = (bf16[128,512]{1,0:T(8,128)(2,1)S(1)}, bf16[128,512]{1,0:T(8,128)(2,1)S(1)}, u32[]{:S(2)}, u32[]{:S(2)}) collective-permute-start(bf16[128,512]{1,0:T(8,128)(2,1)S(1)} %select_convert_fusion), channel_id=1, source_target_pairs={{0,2},{1,3},{2,0},{3,1},{4,6},{5,7},{6,4},{7,5},{8,10},{9,11},{10,... | collective-permute-start | bytes 393224 | tf_op jit(solution)/shard_map/ppermute | solution.py:19
  82.2 7.0 %collective-permute-done.32 = bf16[128,512]{1,0:T(8,128)(2,1)S(1)} collective-permute-done((bf16[128,512]{1,0:T(8,128)(2,1)S(1)}, bf16[128,512]{1,0:T(8,128)(2,1)S(1)}, u32[]{:S(2)}, u32[]{:S(2)}) %collective-permute-start.32) | collective-permute-done | bytes 131104 | tf_op jit(solution)/shard_map/ppermute | solution.py:19
  (89 shorter events, 26.7 us)
Async XLA Ops:
  3.3 7.7 %collective-permute-start = (bf16[144,512]{1,0:T(8,128)(2,1)S(1)}, bf16[144,512]{1,0:T(8,128)(2,1)S(1)}, u32[]{:S(2)}, u32[]{:S(2)}) collective-permute-start(bf16[144,512]{1,0:T(8,128)(2,1)S(1)} %get-tuple-element.102), channel_id=1, source_target_pairs={{0,16},{4,20},{8,24},{12,28},{16,0},{20,4},{24,8},{28,12},{1,17},{... | collective-permute-start | bytes 442376 | tf_op jit(solution)/shard_map/ppermute | solution.py:229
  6.4 6.3 %collective-permute-start.1 = (bf16[144,512]{1,0:T(8,128)(2,1)S(1)}, bf16[144,512]{1,0:T(8,128)(2,1)S(1)}, u32[]{:S(2)}, u32[]{:S(2)}) collective-permute-start(bf16[144,512]{1,0:T(8,128)(2,1)S(1)} %get-tuple-element.101), channel_id=1, source_target_pairs={{0,24},{4,28},{8,16},{12,20},{16,8},{20,12},{24,0},{28,4},{1,25},{... | collective-permute-start | bytes 442376 | tf_op jit(solution)/shard_map/ppermute | solution.py:229
  6.4 8.8 %collective-permute-start.5 = (bf16[144,512]{1,0:T(8,128)(2,1)S(1)}, bf16[144,512]{1,0:T(8,128)(2,1)S(1)}, u32[]{:S(2)}, u32[]{:S(2)}) collective-permute-start(bf16[144,512]{1,0:T(8,128)(2,1)S(1)} %get-tuple-element.103.refs_0_), channel_id=1, source_target_pairs={{0,4},{4,0},{8,12},{12,8},{16,20},{20,16},{24,28},{28,24},{1,5},{5... | collective-permute-start | bytes 442376 | tf_op jit(solution)/shard_map/ppermute | solution.py:229
  7.9 7.3 %collective-permute-start.6 = (bf16[144,512]{1,0:T(8,128)(2,1)S(1)}, bf16[144,512]{1,0:T(8,128)(2,1)S(1)}, u32[]{:S(2)}, u32[]{:S(2)}) collective-permute-start(bf16[144,512]{1,0:T(8,128)(2,1)S(1)} %get-tuple-element.104), channel_id=1, source_target_pairs={{0,12},{4,8},{8,4},{12,0},{16,28},{20,24},{24,20},{28,16},{1,13},{... | collective-permute-start | bytes 442376 | tf_op jit(solution)/shard_map/ppermute | solution.py:229
  12.6 6.0 %collective-permute-start.4 = (bf16[128,512]{1,0:T(8,128)(2,1)S(1)}, bf16[128,512]{1,0:T(8,128)(2,1)S(1)}, u32[]{:S(2)}, u32[]{:S(2)}) collective-permute-start(bf16[128,512]{1,0:T(8,128)(2,1)S(1)} %get-tuple-element.49), channel_id=1, source_target_pairs={{0,24},{4,28},{8,16},{12,20},{16,8},{20,12},{24,0},{28,4},{1,25},{... | collective-permute-start | bytes 393224 | tf_op jit(solution)/shard_map/ppermute | solution.py:229
  14.8 6.9 %collective-permute-start.3 = (bf16[128,512]{1,0:T(8,128)(2,1)S(1)}, bf16[128,512]{1,0:T(8,128)(2,1)S(1)}, u32[]{:S(2)}, u32[]{:S(2)}) collective-permute-start(bf16[128,512]{1,0:T(8,128)(2,1)S(1)} %get-tuple-element.48), channel_id=1, source_target_pairs={{0,16},{4,20},{8,24},{12,28},{16,0},{20,4},{24,8},{28,12},{1,17},{... | collective-permute-start | bytes 393224 | tf_op jit(solution)/shard_map/ppermute | solution.py:229
  15.1 6.6 %collective-permute-start.2 = (bf16[128,512]{1,0:T(8,128)(2,1)S(1)}, bf16[128,512]{1,0:T(8,128)(2,1)S(1)}, u32[]{:S(2)}, u32[]{:S(2)}) collective-permute-start(bf16[128,512]{1,0:T(8,128)(2,1)S(1)} %get-tuple-element.47), channel_id=1, source_target_pairs={{0,8},{4,12},{8,0},{12,4},{16,24},{20,28},{24,16},{28,20},{1,9},{5... | collective-permute-start | bytes 393224 | tf_op jit(solution)/shard_map/ppermute | solution.py:229
  15.1 6.7 %collective-permute-start.7 = (bf16[144,512]{1,0:T(8,128)(2,1)S(1)}, bf16[144,512]{1,0:T(8,128)(2,1)S(1)}, u32[]{:S(2)}, u32[]{:S(2)}) collective-permute-start(bf16[144,512]{1,0:T(8,128)(2,1)S(1)} %collective-permute-done.refs_2_), channel_id=1, source_target_pairs={{0,4},{4,0},{1,5},{5,1},{2,6},{6,2},{3,7},{7,3},{8,12},{12,8},{9,1... | collective-permute-start | bytes 442376 | tf_op jit(solution)/shard_map/ppermute | solution.py:19
  17.1 7.4 %collective-permute-start.8 = (bf16[144,512]{1,0:T(8,128)(2,1)S(1)}, bf16[144,512]{1,0:T(8,128)(2,1)S(1)}, u32[]{:S(2)}, u32[]{:S(2)}) collective-permute-start(bf16[144,512]{1,0:T(8,128)(2,1)S(1)} %collective-permute-done.1.refs_3_), channel_id=1, source_target_pairs={{0,4},{4,0},{1,5},{5,1},{2,6},{6,2},{3,7},{7,3},{8,12},{12,8},{9,1... | collective-permute-start | bytes 442376 | tf_op jit(solution)/shard_map/ppermute | solution.py:19
  18.7 7.6 %collective-permute-start.10 = (bf16[144,512]{1,0:T(8,128)(2,1)S(1)}, bf16[144,512]{1,0:T(8,128)(2,1)S(1)}, u32[]{:S(2)}, u32[]{:S(2)}) collective-permute-start(bf16[144,512]{1,0:T(8,128)(2,1)S(1)} %get-tuple-element.104), channel_id=1, source_target_pairs={{0,8},{4,12},{8,0},{12,4},{16,24},{20,28},{24,16},{28,20},{1,9},{5... | collective-permute-start | bytes 442376 | tf_op jit(solution)/shard_map/ppermute | solution.py:229
  24.5 13.5 %collective-permute-start.9 = (bf16[4,128,512]{2,1,0:T(8,128)(2,1)S(1)}, bf16[4,128,512]{2,1,0:T(8,128)(2,1)S(1)}, u32[]{:S(2)}, u32[]{:S(2)}) collective-permute-start(bf16[4,128,512]{2,1,0:T(8,128)(2,1)S(1)} %pad_maximum_fusion.refs_8_), channel_id=1, source_target_pairs={{0,4},{4,0},{1,5},{5,1},{2,6},{6,2},{3,7},{7,3},{8,12},{12,8},{9,1... | collective-permute-start | bytes 1572872 | tf_op jit(solution)/shard_map/ppermute | solution.py:19
  32.0 11.5 %collective-permute-start.15 = (bf16[2,16,16,352]{3,2,1,0:T(8,128)(2,1)S(1)}, bf16[2,16,16,352]{3,2,1,0:T(8,128)(2,1)S(1)}, u32[]{:S(2)}, u32[]{:S(2)}) collective-permute-start(bf16[2,16,16,352]{3,2,1,0:T(8,128)(2,1)S(1)} %pad_maximum_fusion.2.refs_6_), channel_id=1, source_target_pairs={{0,16},{8,24},{16,0},{24,8},{1,17},{9,25},{17,1},{25,9},{2,18},{10... | collective-permute-start | bytes 1081352 | tf_op jit(solution)/shard_map/ppermute | solution.py:19
  41.2 4.0 %collective-permute-start.17 = (bf16[16,16,352]{2,1,0:T(8,128)(2,1)S(1)}, bf16[16,16,352]{2,1,0:T(8,128)(2,1)S(1)}, u32[]{:S(2)}, u32[]{:S(2)}) collective-permute-start(bf16[16,16,352]{2,1,0:T(8,128)(2,1)S(1)} %get-tuple-element.87), channel_id=1, source_target_pairs={{0,8},{8,0},{16,24},{24,16},{1,9},{9,1},{17,25},{25,17},{2,10},{10... | collective-permute-start | bytes 540680 | tf_op jit(solution)/shard_map/ppermute | solution.py:19
  41.7 3.6 %collective-permute-start.18 = (bf16[16,16,352]{2,1,0:T(8,128)(2,1)S(1)}, bf16[16,16,352]{2,1,0:T(8,128)(2,1)S(1)}, u32[]{:S(2)}, u32[]{:S(2)}) collective-permute-start(bf16[16,16,352]{2,1,0:T(8,128)(2,1)S(1)} %get-tuple-element.89), channel_id=1, source_target_pairs={{0,8},{8,0},{16,24},{24,16},{1,9},{9,1},{17,25},{25,17},{2,10},{10... | collective-permute-start | bytes 540680 | tf_op jit(solution)/shard_map/ppermute | solution.py:19
  43.5 6.4 %collective-permute-start.16 = (bf16[16,16,352]{2,1,0:T(8,128)(2,1)S(1)}, bf16[16,16,352]{2,1,0:T(8,128)(2,1)S(1)}, u32[]{:S(2)}, u32[]{:S(2)}) collective-permute-start(bf16[16,16,352]{2,1,0:T(8,128)(2,1)S(1)} %add_convert_fusion), channel_id=1, source_target_pairs={{0,16},{8,24},{16,0},{24,8},{1,17},{9,25},{17,1},{25,9},{2,18},{10... | collective-permute-start | bytes 540680 | tf_op jit(solution)/shard_map/ppermute | solution.py:19
  50.7 7.2 %collective-permute-start.19 = (bf16[7,16,704]{2,1,0:T(8,128)(2,1)S(1)}, bf16[7,16,704]{2,1,0:T(8,128)(2,1)S(1)}, u32[]{:S(2)}, u32[]{:S(2)}) collective-permute-start(bf16[7,16,704]{2,1,0:T(8,128)(2,1)S(1)} %fusion.10), channel_id=1, source_target_pairs={{0,16},{8,24},{16,0},{24,8},{1,17},{9,25},{17,1},{25,9},{2,18},{10... | collective-permute-start | bytes 473096 | tf_op jit(solution)/shard_map/ppermute | solution.py:19
  52.6 9.7 %collective-permute-start.22 = (bf16[9,16,704]{2,1,0:T(8,128)(2,1)S(1)}, bf16[9,16,704]{2,1,0:T(8,128)(2,1)S(1)}, u32[]{:S(2)}, u32[]{:S(2)}) collective-permute-start(bf16[9,16,704]{2,1,0:T(8,128)(2,1)S(1)} %fusion.7), channel_id=1, source_target_pairs={{0,16},{8,24},{16,0},{24,8},{1,17},{9,25},{17,1},{25,9},{2,18},{10... | collective-permute-start | bytes 608264 | tf_op jit(solution)/shard_map/ppermute | solution.py:19
  62.3 8.8 %collective-permute-start.30 = (bf16[2,128,512]{2,1,0:T(8,128)(2,1)S(1)}, bf16[2,128,512]{2,1,0:T(8,128)(2,1)S(1)}, u32[]{:S(2)}, u32[]{:S(2)}) collective-permute-start(bf16[2,128,512]{2,1,0:T(8,128)(2,1)S(1)} %pad_maximum_fusion.5), channel_id=1, source_target_pairs={{0,4},{4,0},{1,5},{5,1},{2,6},{6,2},{3,7},{7,3},{8,12},{12,8},{9,1... | collective-permute-start | bytes 786440 | tf_op jit(solution)/shard_map/ppermute | solution.py:19
  65.3 13.7 %collective-permute-start.24 = (bf16[128,512]{1,0:T(8,128)(2,1)S(1)}, bf16[128,512]{1,0:T(8,128)(2,1)S(1)}, u32[]{:S(2)}, u32[]{:S(2)}) collective-permute-start(bf16[128,512]{1,0:T(8,128)(2,1)S(1)} %get-tuple-element.67), channel_id=1, source_target_pairs={{0,16},{1,24},{2,18},{3,26},{4,20},{5,28},{6,22},{7,30},{8,17},{9,... | collective-permute-start | bytes 393224 | tf_op jit(solution)/shard_map/ppermute | solution.py:296
  67.0 11.9 %collective-permute-start.25 = (bf16[128,512]{1,0:T(8,128)(2,1)S(1)}, bf16[128,512]{1,0:T(8,128)(2,1)S(1)}, u32[]{:S(2)}, u32[]{:S(2)}) collective-permute-start(bf16[128,512]{1,0:T(8,128)(2,1)S(1)} %get-tuple-element.68), channel_id=1, source_target_pairs={{0,20},{1,28},{2,22},{3,30},{4,16},{5,24},{6,18},{7,26},{8,21},{9,... | collective-permute-start | bytes 393224 | tf_op jit(solution)/shard_map/ppermute | solution.py:296
  68.0 11.3 %collective-permute-start.26 = (bf16[128,512]{1,0:T(8,128)(2,1)S(1)}, bf16[128,512]{1,0:T(8,128)(2,1)S(1)}, u32[]{:S(2)}, u32[]{:S(2)}) collective-permute-start(bf16[128,512]{1,0:T(8,128)(2,1)S(1)} %get-tuple-element.69), channel_id=1, source_target_pairs={{0,24},{1,16},{2,26},{3,18},{4,28},{5,20},{6,30},{7,22},{8,25},{9,... | collective-permute-start | bytes 393224 | tf_op jit(solution)/shard_map/ppermute | solution.py:296
  69.9 9.4 %collective-permute-start.27 = (bf16[128,512]{1,0:T(8,128)(2,1)S(1)}, bf16[128,512]{1,0:T(8,128)(2,1)S(1)}, u32[]{:S(2)}, u32[]{:S(2)}) collective-permute-start(bf16[128,512]{1,0:T(8,128)(2,1)S(1)} %get-tuple-element.70), channel_id=1, source_target_pairs={{0,28},{1,20},{2,30},{3,22},{4,24},{5,16},{6,26},{7,18},{8,29},{9,... | collective-permute-start | bytes 393224 | tf_op jit(solution)/shard_map/ppermute | solution.py:296
  71.2 8.2 %collective-permute-start.31 = (bf16[128,512]{1,0:T(8,128)(2,1)S(1)}, bf16[128,512]{1,0:T(8,128)(2,1)S(1)}, u32[]{:S(2)}, u32[]{:S(2)}) collective-permute-start(bf16[128,512]{1,0:T(8,128)(2,1)S(1)} %broadcast_select_fusion), channel_id=1, source_target_pairs={{0,1},{1,0},{2,3},{3,2},{4,5},{5,4},{6,7},{7,6},{8,9},{9,8},{10,11... | collective-permute-start | bytes 393224 | tf_op jit(solution)/shard_map/ppermute | solution.py:19
  79.5 9.6 %collective-permute-start.32 = (bf16[128,512]{1,0:T(8,128)(2,1)S(1)}, bf16[128,512]{1,0:T(8,128)(2,1)S(1)}, u32[]{:S(2)}, u32[]{:S(2)}) collective-permute-start(bf16[128,512]{1,0:T(8,128)(2,1)S(1)} %select_convert_fusion), channel_id=1, source_target_pairs={{0,2},{1,3},{2,0},{3,1},{4,6},{5,7},{6,4},{7,5},{8,10},{9,11},{10,... | collective-permute-start | bytes 393224 | tf_op jit(solution)/shard_map/ppermute | solution.py:19
  (15 other events, 51.1 us)

commit v6 on v5

--- a/solution.py
+++ b/solution.py
@@ -212,7 +212,8 @@
     ids_row = expert_ids.reshape(1, rows)
     order = jnp.arange(rows, dtype=jnp.int32)
     earlier = (expert_ids == ids_row) & (order[:, None] < order[None, :])
-    goal = ids_row * CAP + jnp.sum(earlier.astype(jnp.int32), axis=0, keepdims=True)
+    own_line = order[:, None] == order[None, :]
+    goal = jnp.sum(jnp.where(own_line, expert_ids * CAP, earlier.astype(jnp.int32)), axis=0, keepdims=True)
     meta = jnp.pad(goal.astype(BF16), ((0, META - 1), (0, width - rows)))
 
     def columns(values, rel):

time: 90.1 us -> 90.2 us (level)
  no operation moved by 1% of the time
where the time goes in v6:
time: 90.2 us; the launch traced here: 90 us
  waiting for transfers between devices  34.5 us (38%)
  starting transfers between devices  30.9 us (34%)
  Pallas kernels  11.6 us (13%)
  matrix products  4.98 us (6%)
  other arithmetic  3.77 us (4%)
  local copies, waits for them, and re-layouts  3.39 us (4%)
  between operations  0.96 us (1%)
    ppermute x21, waiting for transfers between devices, swap(): return lax.ppermute(value, axis, [(i, i ^ bit) for i in range(count)])  27.1 us
    ppermute x21, starting transfers between devices, swap(): return lax.ppermute(value, axis, [(i, i ^ bit) for i in range(count)])  17.7 us
    ppermute x8, starting transfers between devices, to_owner(): return lax.ppermute(value, ('dp', 'expert'), pairs)  8.11 us
    ppermute x8, waiting for transfers between devices, to_owner(): return lax.ppermute(value, ('dp', 'expert'), pairs)  7.02 us
    pallas_call x1, Pallas kernels, weight_grads(): pl.pallas_call(weight_kernel, grid=(local_experts // per_step,), out_shap...  5.75 us
    ppermute x4, starting transfers between devices, to_keeper(): return lax.ppermute(value, ('dp', 'expert', 'tensor'), pairs)  5.04 us
    dot_general x3, matrix products, project(): jnp.einsum('esd,ehd->esh', values, weight, preferred_element_type=F32)  4.98 us
    pallas_call x3, Pallas kernels, back(): pl.pallas_call(functools.partial(back_kernel, low, first, last), out_shap...  4.93 us
  transfers between devices with their start and end apart: 33, of which 17 were waited for; matrix products, arithmetic and copies ran while one was open for 8% of the time, Pallas kernels for 13%

profile of v6, /device:TPU:0, one launch (start us, length us, event | category | flops | bytes accessed | tf_op | source)
XLA Modules:
  0.0 90.0 jit_solution(4097090057250473787)
XLA Ops:
  3.4 3.0 %collective-permute-start = (bf16[144,512]{1,0:T(8,128)(2,1)S(1)}, bf16[144,512]{1,0:T(8,128)(2,1)S(1)}, u32[]{:S(2)}, u32[]{:S(2)}) collective-permute-start(bf16[144,512]{1,0:T(8,128)(2,1)S(1)} %get-tuple-element.102), channel_id=1, source_target_pairs={{0,16},{4,20},{8,24},{12,28},{16,0},{20,4},{24,8},{28,12},{1,17},{... | collective-permute-start | bytes 442376 | tf_op jit(solution)/shard_map/ppermute | solution.py:230
  9.3 1.8 %collective-permute-done.refs_2_ = bf16[144,512]{1,0:T(8,128)(2,1)S(1)} collective-permute-done((bf16[144,512]{1,0:T(8,128)(2,1)S(1)}, bf16[144,512]{1,0:T(8,128)(2,1)S(1)}, u32[]{:S(2)}, u32[]{:S(2)}) %collective-permute-start) | collective-permute-done | bytes 147488 | tf_op jit(solution)/shard_map/ppermute | solution.py:230
  11.1 1.6 %collective-permute-done.1.refs_3_ = bf16[144,512]{1,0:T(8,128)(2,1)S(1)} collective-permute-done((bf16[144,512]{1,0:T(8,128)(2,1)S(1)}, bf16[144,512]{1,0:T(8,128)(2,1)S(1)}, u32[]{:S(2)}, u32[]{:S(2)}) %collective-permute-start.1) | collective-permute-done | bytes 147488 | tf_op jit(solution)/shard_map/ppermute | solution.py:230
  12.7 2.2 %collective-permute-start.4 = (bf16[128,512]{1,0:T(8,128)(2,1)S(1)}, bf16[128,512]{1,0:T(8,128)(2,1)S(1)}, u32[]{:S(2)}, u32[]{:S(2)}) collective-permute-start(bf16[128,512]{1,0:T(8,128)(2,1)S(1)} %get-tuple-element.49), channel_id=1, source_target_pairs={{0,24},{4,28},{8,16},{12,20},{16,8},{20,12},{24,0},{28,4},{1,25},{... | collective-permute-start | bytes 393224 | tf_op jit(solution)/shard_map/ppermute | solution.py:230
  15.2 2.0 %collective-permute-start.7 = (bf16[144,512]{1,0:T(8,128)(2,1)S(1)}, bf16[144,512]{1,0:T(8,128)(2,1)S(1)}, u32[]{:S(2)}, u32[]{:S(2)}) collective-permute-start(bf16[144,512]{1,0:T(8,128)(2,1)S(1)} %collective-permute-done.refs_2_), channel_id=1, source_target_pairs={{0,4},{4,0},{1,5},{5,1},{2,6},{6,2},{3,7},{7,3},{8,12},{12,8},{9,1... | collective-permute-start | bytes 442376 | tf_op jit(solution)/shard_map/ppermute | solution.py:19
  19.6 2.2 %collective-permute-done.3.refs_2_ = bf16[128,512]{1,0:T(8,128)(2,1)S(1)} collective-permute-done((bf16[128,512]{1,0:T(8,128)(2,1)S(1)}, bf16[128,512]{1,0:T(8,128)(2,1)S(1)}, u32[]{:S(2)}, u32[]{:S(2)}) %collective-permute-start.3) | collective-permute-done | bytes 131104 | tf_op jit(solution)/shard_map/ppermute | solution.py:230
  21.9 2.7 %collective-permute-done.8.refs_7_ = bf16[144,512]{1,0:T(8,128)(2,1)S(1)} collective-permute-done((bf16[144,512]{1,0:T(8,128)(2,1)S(1)}, bf16[144,512]{1,0:T(8,128)(2,1)S(1)}, u32[]{:S(2)}, u32[]{:S(2)}) %collective-permute-start.8) | collective-permute-done | bytes 147488 | tf_op jit(solution)/shard_map/ppermute | solution.py:19
  24.6 1.7 %collective-permute-start.9 = (bf16[4,128,512]{2,1,0:T(8,128)(2,1)S(1)}, bf16[4,128,512]{2,1,0:T(8,128)(2,1)S(1)}, u32[]{:S(2)}, u32[]{:S(2)}) collective-permute-start(bf16[4,128,512]{2,1,0:T(8,128)(2,1)S(1)} %pad_maximum_fusion.refs_8_), channel_id=1, source_target_pairs={{0,4},{4,0},{1,5},{5,1},{2,6},{6,2},{3,7},{7,3},{8,12},{12,8},{9,1... | collective-permute-start | bytes 1572872 | tf_op jit(solution)/shard_map/ppermute | solution.py:19
  26.8 1.7 %convolution_convert_fusion.1 = bf16[16,64,352]{2,1,0:T(8,128)(2,1)S(1)} fusion(bf16[16,64,512]{2,1,0:T(8,128)(2,1)S(1)} %get-tuple-element.75.placed, bf16[16,512,352]{1,2,0:T(8,128)(2,1)S(1)} %bitcast.51), kind=kOutput, calls=%fused_computation.1 | convolution fusion | flops 369459200 | bytes 7536640 | tf_op jit(solution)/shard_map/esd,ehd->esh/dot_general | solution.py:248
  28.6 1.7 %convolution_convert_fusion.2 = bf16[16,64,352]{2,1,0:T(8,128)(2,1)S(1)} fusion(bf16[16,64,512]{2,1,0:T(8,128)(2,1)S(1)} %get-tuple-element.75.placed, bf16[16,512,352]{1,2,0:T(8,128)(2,1)S(1)} %bitcast.54), kind=kOutput, calls=%fused_computation.2 | convolution fusion | flops 369459200 | bytes 7536640 | tf_op jit(solution)/shard_map/esd,ehd->esh/dot_general | solution.py:248
  32.1 1.8 %collective-permute-start.15 = (bf16[2,16,16,352]{3,2,1,0:T(8,128)(2,1)S(1)}, bf16[2,16,16,352]{3,2,1,0:T(8,128)(2,1)S(1)}, u32[]{:S(2)}, u32[]{:S(2)}) collective-permute-start(bf16[2,16,16,352]{3,2,1,0:T(8,128)(2,1)S(1)} %pad_maximum_fusion.2.refs_6_), channel_id=1, source_target_pairs={{0,16},{8,24},{16,0},{24,8},{1,17},{9,25},{17,1},{25,9},{2,18},{10... | collective-permute-start | bytes 1081352 | tf_op jit(solution)/shard_map/ppermute | solution.py:19
  33.8 4.2 %collective-permute-done.9.refs_4_ = bf16[4,128,512]{2,1,0:T(8,128)(2,1)S(1)} collective-permute-done((bf16[4,128,512]{2,1,0:T(8,128)(2,1)S(1)}, bf16[4,128,512]{2,1,0:T(8,128)(2,1)S(1)}, u32[]{:S(2)}, u32[]{:S(2)}) %collective-permute-start.9) | collective-permute-done | bytes 524320 | tf_op jit(solution)/shard_map/ppermute | solution.py:19
  39.5 1.7 %convolution_convert_fusion = bf16[16,64,352]{2,1,0:T(8,128)(2,1)S(1)} fusion(bf16[16,64,512]{2,1,0:T(8,128)(2,1)S(1)} %shard_map.86, bf16[16,512,352]{1,2,0:T(8,128)(2,1)S(1)} %bitcast.62), kind=kOutput, calls=%fused_computation | convolution fusion | flops 369459200 | bytes 7536640 | tf_op jit(solution)/shard_map/esd,ehd->esh/dot_general | solution.py:248
  43.6 1.8 %collective-permute-start.16 = (bf16[16,16,352]{2,1,0:T(8,128)(2,1)S(1)}, bf16[16,16,352]{2,1,0:T(8,128)(2,1)S(1)}, u32[]{:S(2)}, u32[]{:S(2)}) collective-permute-start(bf16[16,16,352]{2,1,0:T(8,128)(2,1)S(1)} %add_convert_fusion), channel_id=1, source_target_pairs={{0,16},{8,24},{16,0},{24,8},{1,17},{9,25},{17,1},{25,9},{2,18},{10... | collective-permute-start | bytes 540680 | tf_op jit(solution)/shard_map/ppermute | solution.py:19
  45.4 4.7 %collective-permute-done.16 = bf16[16,16,352]{2,1,0:T(8,128)(2,1)S(1)} collective-permute-done((bf16[16,16,352]{2,1,0:T(8,128)(2,1)S(1)}, bf16[16,16,352]{2,1,0:T(8,128)(2,1)S(1)}, u32[]{:S(2)}, u32[]{:S(2)}) %collective-permute-start.16) | collective-permute-done | bytes 180256 | tf_op jit(solution)/shard_map/ppermute | solution.py:19
  50.7 1.8 %collective-permute-start.19 = (bf16[7,16,704]{2,1,0:T(8,128)(2,1)S(1)}, bf16[7,16,704]{2,1,0:T(8,128)(2,1)S(1)}, u32[]{:S(2)}, u32[]{:S(2)}) collective-permute-start(bf16[7,16,704]{2,1,0:T(8,128)(2,1)S(1)} %fusion.10), channel_id=1, source_target_pairs={{0,16},{8,24},{16,0},{24,8},{1,17},{9,25},{17,1},{25,9},{2,18},{10... | collective-permute-start | bytes 473096 | tf_op jit(solution)/shard_map/ppermute | solution.py:19
  53.0 2.5 %shard_map.87 = (bf16[128,512]{1,0:T(8,128)(2,1)S(1)}, bf16[128,512]{1,0:T(8,128)(2,1)S(1)}, bf16[128,512]{1,0:T(8,128)(2,1)S(1)}, bf16[128,512]{1,0:T(8,128)(2,1)S(1)}, bf16[16,704,512]{2,1,0:T(8,128)(2,1)S(1)}) custom-call(s32[4,8,256]{2,1,0:T(8,128)S(1)} %get-tuple-element.59.refs_5_.refs_0_.refs_1_, ...), custom_call_target="tpu_custom_call" | custom-call | flops 1476395008 | bytes 11534336 | tf_op jit(solution)/shard_map/pallas_call | solution.py:148
  55.5 2.5 %collective-permute-done.19.refs_0_ = bf16[7,16,704]{2,1,0:T(8,128)(2,1)S(1)} collective-permute-done((bf16[7,16,704]{2,1,0:T(8,128)(2,1)S(1)}, bf16[7,16,704]{2,1,0:T(8,128)(2,1)S(1)}, u32[]{:S(2)}, u32[]{:S(2)}) %collective-permute-start.19) | collective-permute-done | bytes 157728 | tf_op jit(solution)/shard_map/ppermute | solution.py:19
  65.3 1.8 %collective-permute-start.24 = (bf16[128,512]{1,0:T(8,128)(2,1)S(1)}, bf16[128,512]{1,0:T(8,128)(2,1)S(1)}, u32[]{:S(2)}, u32[]{:S(2)}) collective-permute-start(bf16[128,512]{1,0:T(8,128)(2,1)S(1)} %get-tuple-element.67), channel_id=1, source_target_pairs={{0,16},{1,24},{2,18},{3,26},{4,20},{5,28},{6,22},{7,30},{8,17},{9,... | collective-permute-start | bytes 393224 | tf_op jit(solution)/shard_map/ppermute | solution.py:297
  68.1 1.9 %collective-permute-start.26 = (bf16[128,512]{1,0:T(8,128)(2,1)S(1)}, bf16[128,512]{1,0:T(8,128)(2,1)S(1)}, u32[]{:S(2)}, u32[]{:S(2)}) collective-permute-start(bf16[128,512]{1,0:T(8,128)(2,1)S(1)} %get-tuple-element.69), channel_id=1, source_target_pairs={{0,24},{1,16},{2,26},{3,18},{4,28},{5,20},{6,30},{7,22},{8,25},{9,... | collective-permute-start | bytes 393224 | tf_op jit(solution)/shard_map/ppermute | solution.py:297
  71.2 2.0 %collective-permute-start.31 = (bf16[128,512]{1,0:T(8,128)(2,1)S(1)}, bf16[128,512]{1,0:T(8,128)(2,1)S(1)}, u32[]{:S(2)}, u32[]{:S(2)}) collective-permute-start(bf16[128,512]{1,0:T(8,128)(2,1)S(1)} %broadcast_select_fusion), channel_id=1, source_target_pairs={{0,1},{1,0},{2,3},{3,2},{4,5},{5,4},{6,7},{7,6},{8,9},{9,8},{10,11... | collective-permute-start | bytes 393224 | tf_op jit(solution)/shard_map/ppermute | solution.py:19
  73.3 5.7 %shard_map.90 = (bf16[16,352,512]{2,1,0:T(8,128)(2,1)}, bf16[16,352,512]{2,1,0:T(8,128)(2,1)}) custom-call(bf16[16,64,512]{2,1,0:T(8,128)(2,1)S(1)} %get-tuple-element.75.placed, bf16[16,16,704]{2,1,0:T(8,128)(2,1)S(1)} %pad_maximum_fusion.1.refs_1_.h0, bf16[16,16,704]{2,1,0:T(8,128)(2,1)S(1)} %collective-permute-done.20.refs_2_.h1, ...), custom_call_target="tpu_custom_call" | custom-call | flops 2952790016 | bytes 11534336 | tf_op jit(solution)/shard_map/pallas_call | solution.py:179
  79.6 2.6 %collective-permute-start.32 = (bf16[128,512]{1,0:T(8,128)(2,1)S(1)}, bf16[128,512]{1,0:T(8,128)(2,1)S(1)}, u32[]{:S(2)}, u32[]{:S(2)}) collective-permute-start(bf16[128,512]{1,0:T(8,128)(2,1)S(1)} %select_convert_fusion), channel_id=1, source_target_pairs={{0,2},{1,3},{2,0},{3,1},{4,6},{5,7},{6,4},{7,5},{8,10},{9,11},{10,... | collective-permute-start | bytes 393224 | tf_op jit(solution)/shard_map/ppermute | solution.py:19
  82.2 7.0 %collective-permute-done.32 = bf16[128,512]{1,0:T(8,128)(2,1)S(1)} collective-permute-done((bf16[128,512]{1,0:T(8,128)(2,1)S(1)}, bf16[128,512]{1,0:T(8,128)(2,1)S(1)}, u32[]{:S(2)}, u32[]{:S(2)}) %collective-permute-start.32) | collective-permute-done | bytes 131104 | tf_op jit(solution)/shard_map/ppermute | solution.py:19
  (90 shorter events, 26.7 us)
Async XLA Ops:
  3.4 7.7 %collective-permute-start = (bf16[144,512]{1,0:T(8,128)(2,1)S(1)}, bf16[144,512]{1,0:T(8,128)(2,1)S(1)}, u32[]{:S(2)}, u32[]{:S(2)}) collective-permute-start(bf16[144,512]{1,0:T(8,128)(2,1)S(1)} %get-tuple-element.102), channel_id=1, source_target_pairs={{0,16},{4,20},{8,24},{12,28},{16,0},{20,4},{24,8},{28,12},{1,17},{... | collective-permute-start | bytes 442376 | tf_op jit(solution)/shard_map/ppermute | solution.py:230
  6.4 6.3 %collective-permute-start.1 = (bf16[144,512]{1,0:T(8,128)(2,1)S(1)}, bf16[144,512]{1,0:T(8,128)(2,1)S(1)}, u32[]{:S(2)}, u32[]{:S(2)}) collective-permute-start(bf16[144,512]{1,0:T(8,128)(2,1)S(1)} %get-tuple-element.101), channel_id=1, source_target_pairs={{0,24},{4,28},{8,16},{12,20},{16,8},{20,12},{24,0},{28,4},{1,25},{... | collective-permute-start | bytes 442376 | tf_op jit(solution)/shard_map/ppermute | solution.py:230
  6.4 8.8 %collective-permute-start.5 = (bf16[144,512]{1,0:T(8,128)(2,1)S(1)}, bf16[144,512]{1,0:T(8,128)(2,1)S(1)}, u32[]{:S(2)}, u32[]{:S(2)}) collective-permute-start(bf16[144,512]{1,0:T(8,128)(2,1)S(1)} %get-tuple-element.103.refs_0_), channel_id=1, source_target_pairs={{0,4},{4,0},{8,12},{12,8},{16,20},{20,16},{24,28},{28,24},{1,5},{5... | collective-permute-start | bytes 442376 | tf_op jit(solution)/shard_map/ppermute | solution.py:230
  7.9 7.3 %collective-permute-start.6 = (bf16[144,512]{1,0:T(8,128)(2,1)S(1)}, bf16[144,512]{1,0:T(8,128)(2,1)S(1)}, u32[]{:S(2)}, u32[]{:S(2)}) collective-permute-start(bf16[144,512]{1,0:T(8,128)(2,1)S(1)} %get-tuple-element.104), channel_id=1, source_target_pairs={{0,12},{4,8},{8,4},{12,0},{16,28},{20,24},{24,20},{28,16},{1,13},{... | collective-permute-start | bytes 442376 | tf_op jit(solution)/shard_map/ppermute | solution.py:230
  12.7 6.0 %collective-permute-start.4 = (bf16[128,512]{1,0:T(8,128)(2,1)S(1)}, bf16[128,512]{1,0:T(8,128)(2,1)S(1)}, u32[]{:S(2)}, u32[]{:S(2)}) collective-permute-start(bf16[128,512]{1,0:T(8,128)(2,1)S(1)} %get-tuple-element.49), channel_id=1, source_target_pairs={{0,24},{4,28},{8,16},{12,20},{16,8},{20,12},{24,0},{28,4},{1,25},{... | collective-permute-start | bytes 393224 | tf_op jit(solution)/shard_map/ppermute | solution.py:230
  14.9 6.9 %collective-permute-start.3 = (bf16[128,512]{1,0:T(8,128)(2,1)S(1)}, bf16[128,512]{1,0:T(8,128)(2,1)S(1)}, u32[]{:S(2)}, u32[]{:S(2)}) collective-permute-start(bf16[128,512]{1,0:T(8,128)(2,1)S(1)} %get-tuple-element.48), channel_id=1, source_target_pairs={{0,16},{4,20},{8,24},{12,28},{16,0},{20,4},{24,8},{28,12},{1,17},{... | collective-permute-start | bytes 393224 | tf_op jit(solution)/shard_map/ppermute | solution.py:230
  15.2 6.6 %collective-permute-start.2 = (bf16[128,512]{1,0:T(8,128)(2,1)S(1)}, bf16[128,512]{1,0:T(8,128)(2,1)S(1)}, u32[]{:S(2)}, u32[]{:S(2)}) collective-permute-start(bf16[128,512]{1,0:T(8,128)(2,1)S(1)} %get-tuple-element.47), channel_id=1, source_target_pairs={{0,8},{4,12},{8,0},{12,4},{16,24},{20,28},{24,16},{28,20},{1,9},{5... | collective-permute-start | bytes 393224 | tf_op jit(solution)/shard_map/ppermute | solution.py:230
  15.2 6.7 %collective-permute-start.7 = (bf16[144,512]{1,0:T(8,128)(2,1)S(1)}, bf16[144,512]{1,0:T(8,128)(2,1)S(1)}, u32[]{:S(2)}, u32[]{:S(2)}) collective-permute-start(bf16[144,512]{1,0:T(8,128)(2,1)S(1)} %collective-permute-done.refs_2_), channel_id=1, source_target_pairs={{0,4},{4,0},{1,5},{5,1},{2,6},{6,2},{3,7},{7,3},{8,12},{12,8},{9,1... | collective-permute-start | bytes 442376 | tf_op jit(solution)/shard_map/ppermute | solution.py:19
  17.2 7.4 %collective-permute-start.8 = (bf16[144,512]{1,0:T(8,128)(2,1)S(1)}, bf16[144,512]{1,0:T(8,128)(2,1)S(1)}, u32[]{:S(2)}, u32[]{:S(2)}) collective-permute-start(bf16[144,512]{1,0:T(8,128)(2,1)S(1)} %collective-permute-done.1.refs_3_), channel_id=1, source_target_pairs={{0,4},{4,0},{1,5},{5,1},{2,6},{6,2},{3,7},{7,3},{8,12},{12,8},{9,1... | collective-permute-start | bytes 442376 | tf_op jit(solution)/shard_map/ppermute | solution.py:19
  18.7 7.6 %collective-permute-start.10 = (bf16[144,512]{1,0:T(8,128)(2,1)S(1)}, bf16[144,512]{1,0:T(8,128)(2,1)S(1)}, u32[]{:S(2)}, u32[]{:S(2)}) collective-permute-start(bf16[144,512]{1,0:T(8,128)(2,1)S(1)} %get-tuple-element.104), channel_id=1, source_target_pairs={{0,8},{4,12},{8,0},{12,4},{16,24},{20,28},{24,16},{28,20},{1,9},{5... | collective-permute-start | bytes 442376 | tf_op jit(solution)/shard_map/ppermute | solution.py:230
  24.6 13.5 %collective-permute-start.9 = (bf16[4,128,512]{2,1,0:T(8,128)(2,1)S(1)}, bf16[4,128,512]{2,1,0:T(8,128)(2,1)S(1)}, u32[]{:S(2)}, u32[]{:S(2)}) collective-permute-start(bf16[4,128,512]{2,1,0:T(8,128)(2,1)S(1)} %pad_maximum_fusion.refs_8_), channel_id=1, source_target_pairs={{0,4},{4,0},{1,5},{5,1},{2,6},{6,2},{3,7},{7,3},{8,12},{12,8},{9,1... | collective-permute-start | bytes 1572872 | tf_op jit(solution)/shard_map/ppermute | solution.py:19
  32.1 11.5 %collective-permute-start.15 = (bf16[2,16,16,352]{3,2,1,0:T(8,128)(2,1)S(1)}, bf16[2,16,16,352]{3,2,1,0:T(8,128)(2,1)S(1)}, u32[]{:S(2)}, u32[]{:S(2)}) collective-permute-start(bf16[2,16,16,352]{3,2,1,0:T(8,128)(2,1)S(1)} %pad_maximum_fusion.2.refs_6_), channel_id=1, source_target_pairs={{0,16},{8,24},{16,0},{24,8},{1,17},{9,25},{17,1},{25,9},{2,18},{10... | collective-permute-start | bytes 1081352 | tf_op jit(solution)/shard_map/ppermute | solution.py:19
  41.3 4.1 %collective-permute-start.17 = (bf16[16,16,352]{2,1,0:T(8,128)(2,1)S(1)}, bf16[16,16,352]{2,1,0:T(8,128)(2,1)S(1)}, u32[]{:S(2)}, u32[]{:S(2)}) collective-permute-start(bf16[16,16,352]{2,1,0:T(8,128)(2,1)S(1)} %get-tuple-element.87), channel_id=1, source_target_pairs={{0,8},{8,0},{16,24},{24,16},{1,9},{9,1},{17,25},{25,17},{2,10},{10... | collective-permute-start | bytes 540680 | tf_op jit(solution)/shard_map/ppermute | solution.py:19
  41.8 3.6 %collective-permute-start.18 = (bf16[16,16,352]{2,1,0:T(8,128)(2,1)S(1)}, bf16[16,16,352]{2,1,0:T(8,128)(2,1)S(1)}, u32[]{:S(2)}, u32[]{:S(2)}) collective-permute-start(bf16[16,16,352]{2,1,0:T(8,128)(2,1)S(1)} %get-tuple-element.89), channel_id=1, source_target_pairs={{0,8},{8,0},{16,24},{24,16},{1,9},{9,1},{17,25},{25,17},{2,10},{10... | collective-permute-start | bytes 540680 | tf_op jit(solution)/shard_map/ppermute | solution.py:19
  43.6 6.4 %collective-permute-start.16 = (bf16[16,16,352]{2,1,0:T(8,128)(2,1)S(1)}, bf16[16,16,352]{2,1,0:T(8,128)(2,1)S(1)}, u32[]{:S(2)}, u32[]{:S(2)}) collective-permute-start(bf16[16,16,352]{2,1,0:T(8,128)(2,1)S(1)} %add_convert_fusion), channel_id=1, source_target_pairs={{0,16},{8,24},{16,0},{24,8},{1,17},{9,25},{17,1},{25,9},{2,18},{10... | collective-permute-start | bytes 540680 | tf_op jit(solution)/shard_map/ppermute | solution.py:19
  50.7 7.2 %collective-permute-start.19 = (bf16[7,16,704]{2,1,0:T(8,128)(2,1)S(1)}, bf16[7,16,704]{2,1,0:T(8,128)(2,1)S(1)}, u32[]{:S(2)}, u32[]{:S(2)}) collective-permute-start(bf16[7,16,704]{2,1,0:T(8,128)(2,1)S(1)} %fusion.10), channel_id=1, source_target_pairs={{0,16},{8,24},{16,0},{24,8},{1,17},{9,25},{17,1},{25,9},{2,18},{10... | collective-permute-start | bytes 473096 | tf_op jit(solution)/shard_map/ppermute | solution.py:19
  52.6 9.7 %collective-permute-start.22 = (bf16[9,16,704]{2,1,0:T(8,128)(2,1)S(1)}, bf16[9,16,704]{2,1,0:T(8,128)(2,1)S(1)}, u32[]{:S(2)}, u32[]{:S(2)}) collective-permute-start(bf16[9,16,704]{2,1,0:T(8,128)(2,1)S(1)} %fusion.7), channel_id=1, source_target_pairs={{0,16},{8,24},{16,0},{24,8},{1,17},{9,25},{17,1},{25,9},{2,18},{10... | collective-permute-start | bytes 608264 | tf_op jit(solution)/shard_map/ppermute | solution.py:19
  62.4 8.8 %collective-permute-start.30 = (bf16[2,128,512]{2,1,0:T(8,128)(2,1)S(1)}, bf16[2,128,512]{2,1,0:T(8,128)(2,1)S(1)}, u32[]{:S(2)}, u32[]{:S(2)}) collective-permute-start(bf16[2,128,512]{2,1,0:T(8,128)(2,1)S(1)} %pad_maximum_fusion.5), channel_id=1, source_target_pairs={{0,4},{4,0},{1,5},{5,1},{2,6},{6,2},{3,7},{7,3},{8,12},{12,8},{9,1... | collective-permute-start | bytes 786440 | tf_op jit(solution)/shard_map/ppermute | solution.py:19
  65.3 13.7 %collective-permute-start.24 = (bf16[128,512]{1,0:T(8,128)(2,1)S(1)}, bf16[128,512]{1,0:T(8,128)(2,1)S(1)}, u32[]{:S(2)}, u32[]{:S(2)}) collective-permute-start(bf16[128,512]{1,0:T(8,128)(2,1)S(1)} %get-tuple-element.67), channel_id=1, source_target_pairs={{0,16},{1,24},{2,18},{3,26},{4,20},{5,28},{6,22},{7,30},{8,17},{9,... | collective-permute-start | bytes 393224 | tf_op jit(solution)/shard_map/ppermute | solution.py:297
  67.1 11.9 %collective-permute-start.25 = (bf16[128,512]{1,0:T(8,128)(2,1)S(1)}, bf16[128,512]{1,0:T(8,128)(2,1)S(1)}, u32[]{:S(2)}, u32[]{:S(2)}) collective-permute-start(bf16[128,512]{1,0:T(8,128)(2,1)S(1)} %get-tuple-element.68), channel_id=1, source_target_pairs={{0,20},{1,28},{2,22},{3,30},{4,16},{5,24},{6,18},{7,26},{8,21},{9,... | collective-permute-start | bytes 393224 | tf_op jit(solution)/shard_map/ppermute | solution.py:297
  68.1 11.3 %collective-permute-start.26 = (bf16[128,512]{1,0:T(8,128)(2,1)S(1)}, bf16[128,512]{1,0:T(8,128)(2,1)S(1)}, u32[]{:S(2)}, u32[]{:S(2)}) collective-permute-start(bf16[128,512]{1,0:T(8,128)(2,1)S(1)} %get-tuple-element.69), channel_id=1, source_target_pairs={{0,24},{1,16},{2,26},{3,18},{4,28},{5,20},{6,30},{7,22},{8,25},{9,... | collective-permute-start | bytes 393224 | tf_op jit(solution)/shard_map/ppermute | solution.py:297
  70.0 9.4 %collective-permute-start.27 = (bf16[128,512]{1,0:T(8,128)(2,1)S(1)}, bf16[128,512]{1,0:T(8,128)(2,1)S(1)}, u32[]{:S(2)}, u32[]{:S(2)}) collective-permute-start(bf16[128,512]{1,0:T(8,128)(2,1)S(1)} %get-tuple-element.70), channel_id=1, source_target_pairs={{0,28},{1,20},{2,30},{3,22},{4,24},{5,16},{6,26},{7,18},{8,29},{9,... | collective-permute-start | bytes 393224 | tf_op jit(solution)/shard_map/ppermute | solution.py:297
  71.2 8.2 %collective-permute-start.31 = (bf16[128,512]{1,0:T(8,128)(2,1)S(1)}, bf16[128,512]{1,0:T(8,128)(2,1)S(1)}, u32[]{:S(2)}, u32[]{:S(2)}) collective-permute-start(bf16[128,512]{1,0:T(8,128)(2,1)S(1)} %broadcast_select_fusion), channel_id=1, source_target_pairs={{0,1},{1,0},{2,3},{3,2},{4,5},{5,4},{6,7},{7,6},{8,9},{9,8},{10,11... | collective-permute-start | bytes 393224 | tf_op jit(solution)/shard_map/ppermute | solution.py:19
  79.6 9.6 %collective-permute-start.32 = (bf16[128,512]{1,0:T(8,128)(2,1)S(1)}, bf16[128,512]{1,0:T(8,128)(2,1)S(1)}, u32[]{:S(2)}, u32[]{:S(2)}) collective-permute-start(bf16[128,512]{1,0:T(8,128)(2,1)S(1)} %select_convert_fusion), channel_id=1, source_target_pairs={{0,2},{1,3},{2,0},{3,1},{4,6},{5,7},{6,4},{7,5},{8,10},{9,11},{10,... | collective-permute-start | bytes 393224 | tf_op jit(solution)/shard_map/ppermute | solution.py:19
  (15 other events, 51.2 us)

commit v7 on v5

--- a/solution.py
+++ b/solution.py
@@ -254,9 +254,8 @@
     placed, lines = place(own_tokens, near_tokens + far_tokens, None, rows, local_experts, [leaving_grads])
     gate_near, gate_far = near_and_far(project(placed, gate_weight))
     up_near, up_far = near_and_far(project(placed, up_weight))
-    far = jnp.stack([gate_far, up_far])
-    there = swap(far, "dp", n_dp, 2)
-    placed_grads = place(own_grads, [other_grads], lines, rows, local_experts, [far])
+    there = [swap(gate_far, "dp", n_dp, 2), swap(up_far, "dp", n_dp, 2)]
+    placed_grads = place(own_grads, [other_grads], lines, rows, local_experts, [gate_far, up_far])
     hidden_act = project(placed_grads, down_weight)
     beside, there = lax.optimization_barrier((swap(hidden_act[3], "dp", n_dp, 1), there))
     hidden_far = plus(hidden_act[2], beside).astype(BF16)

time: 90.1 us -> 90 us (level)
  waiting for transfers between devices: 34.5 us -> 33 us
  starting transfers between devices: 30.9 us -> 32.2 us
    ppermute x21 -> x22, starting transfers between devices: 17.7 us -> 19.1 us  [swap(): return lax.ppermute(value, axis, [(i, i ^ bit) for i in range(count)])]
    ppermute x21 -> x22, waiting for transfers between devices: 27.1 us -> 25.9 us  [swap(): return lax.ppermute(value, axis, [(i, i ^ bit) for i in range(count)])]
  transfers between devices with their start and end apart: 33 -> 34, of which waited for: 17 -> 15; matrix products, arithmetic and copies ran while one was open for 8% -> 8% of each run, Pallas kernels for 13% -> 13%
where the time goes in v7:
time: 90 us; the launch traced here: 89.8 us
  waiting for transfers between devices  33 us (37%)
  starting transfers between devices  32.2 us (36%)
  Pallas kernels  11.6 us (13%)
  matrix products  4.98 us (6%)
  other arithmetic  3.66 us (4%)
  local copies, waits for them, and re-layouts  3.38 us (4%)
  between operations  0.95 us (1%)
    ppermute x22, waiting for transfers between devices, swap(): return lax.ppermute(value, axis, [(i, i ^ bit) for i in range(count)])  25.9 us
    ppermute x22, starting transfers between devices, swap(): return lax.ppermute(value, axis, [(i, i ^ bit) for i in range(count)])  19.1 us
    ppermute x8, starting transfers between devices, to_owner(): return lax.ppermute(value, ('dp', 'expert'), pairs)  8.11 us
    ppermute x8, waiting for transfers between devices, to_owner(): return lax.ppermute(value, ('dp', 'expert'), pairs)  7.02 us
    pallas_call x1, Pallas kernels, weight_grads(): pl.pallas_call(weight_kernel, grid=(local_experts // per_step,), out_shap...  5.75 us
    ppermute x4, starting transfers between devices, to_keeper(): return lax.ppermute(value, ('dp', 'expert', 'tensor'), pairs)  5.02 us
    dot_general x3, matrix products, project(): jnp.einsum('esd,ehd->esh', values, weight, preferred_element_type=F32)  4.98 us
    pallas_call x3, Pallas kernels, back(): pl.pallas_call(functools.partial(back_kernel, low, first, last), out_shap...  4.94 us
  transfers between devices with their start and end apart: 34, of which 15 were waited for; matrix products, arithmetic and copies ran while one was open for 8% of the time, Pallas kernels for 13%

profile of v7, /device:TPU:0, one launch (start us, length us, event | category | flops | bytes accessed | tf_op | source)
XLA Modules:
  0.0 89.8 jit_solution(14222238734091429241)
XLA Ops:
  3.3 3.0 %collective-permute-start = (bf16[144,512]{1,0:T(8,128)(2,1)S(1)}, bf16[144,512]{1,0:T(8,128)(2,1)S(1)}, u32[]{:S(2)}, u32[]{:S(2)}) collective-permute-start(bf16[144,512]{1,0:T(8,128)(2,1)S(1)} %get-tuple-element.104), channel_id=1, source_target_pairs={{0,16},{4,20},{8,24},{12,28},{16,0},{20,4},{24,8},{28,12},{1,17},{... | collective-permute-start | bytes 442376 | tf_op jit(solution)/shard_map/ppermute | solution.py:229
  9.2 1.8 %collective-permute-done.refs_2_ = bf16[144,512]{1,0:T(8,128)(2,1)S(1)} collective-permute-done((bf16[144,512]{1,0:T(8,128)(2,1)S(1)}, bf16[144,512]{1,0:T(8,128)(2,1)S(1)}, u32[]{:S(2)}, u32[]{:S(2)}) %collective-permute-start) | collective-permute-done | bytes 147488 | tf_op jit(solution)/shard_map/ppermute | solution.py:229
  11.0 1.6 %collective-permute-done.1.refs_3_ = bf16[144,512]{1,0:T(8,128)(2,1)S(1)} collective-permute-done((bf16[144,512]{1,0:T(8,128)(2,1)S(1)}, bf16[144,512]{1,0:T(8,128)(2,1)S(1)}, u32[]{:S(2)}, u32[]{:S(2)}) %collective-permute-start.1) | collective-permute-done | bytes 147488 | tf_op jit(solution)/shard_map/ppermute | solution.py:229
  12.6 2.2 %collective-permute-start.4 = (bf16[128,512]{1,0:T(8,128)(2,1)S(1)}, bf16[128,512]{1,0:T(8,128)(2,1)S(1)}, u32[]{:S(2)}, u32[]{:S(2)}) collective-permute-start(bf16[128,512]{1,0:T(8,128)(2,1)S(1)} %get-tuple-element.50), channel_id=1, source_target_pairs={{0,24},{4,28},{8,16},{12,20},{16,8},{20,12},{24,0},{28,4},{1,25},{... | collective-permute-start | bytes 393224 | tf_op jit(solution)/shard_map/ppermute | solution.py:229
  15.1 2.0 %collective-permute-start.7 = (bf16[144,512]{1,0:T(8,128)(2,1)S(1)}, bf16[144,512]{1,0:T(8,128)(2,1)S(1)}, u32[]{:S(2)}, u32[]{:S(2)}) collective-permute-start(bf16[144,512]{1,0:T(8,128)(2,1)S(1)} %collective-permute-done.refs_2_), channel_id=1, source_target_pairs={{0,4},{4,0},{1,5},{5,1},{2,6},{6,2},{3,7},{7,3},{8,12},{12,8},{9,1... | collective-permute-start | bytes 442376 | tf_op jit(solution)/shard_map/ppermute | solution.py:19
  19.5 2.2 %collective-permute-done.3.refs_2_ = bf16[128,512]{1,0:T(8,128)(2,1)S(1)} collective-permute-done((bf16[128,512]{1,0:T(8,128)(2,1)S(1)}, bf16[128,512]{1,0:T(8,128)(2,1)S(1)}, u32[]{:S(2)}, u32[]{:S(2)}) %collective-permute-start.3) | collective-permute-done | bytes 131104 | tf_op jit(solution)/shard_map/ppermute | solution.py:229
  21.9 2.7 %collective-permute-done.8.refs_7_ = bf16[144,512]{1,0:T(8,128)(2,1)S(1)} collective-permute-done((bf16[144,512]{1,0:T(8,128)(2,1)S(1)}, bf16[144,512]{1,0:T(8,128)(2,1)S(1)}, u32[]{:S(2)}, u32[]{:S(2)}) %collective-permute-start.8) | collective-permute-done | bytes 147488 | tf_op jit(solution)/shard_map/ppermute | solution.py:19
  24.5 1.7 %collective-permute-start.9 = (bf16[4,128,512]{2,1,0:T(8,128)(2,1)S(1)}, bf16[4,128,512]{2,1,0:T(8,128)(2,1)S(1)}, u32[]{:S(2)}, u32[]{:S(2)}) collective-permute-start(bf16[4,128,512]{2,1,0:T(8,128)(2,1)S(1)} %pad_maximum_fusion.refs_8_), channel_id=1, source_target_pairs={{0,4},{4,0},{1,5},{5,1},{2,6},{6,2},{3,7},{7,3},{8,12},{12,8},{9,1... | collective-permute-start | bytes 1572872 | tf_op jit(solution)/shard_map/ppermute | solution.py:19
  26.7 1.7 %convolution_convert_fusion.2 = bf16[16,64,352]{2,1,0:T(8,128)(2,1)S(1)} fusion(bf16[16,64,512]{2,1,0:T(8,128)(2,1)S(1)} %get-tuple-element.77.placed, bf16[16,512,352]{1,2,0:T(8,128)(2,1)S(1)} %bitcast.45), kind=kOutput, calls=%fused_computation.2 | convolution fusion | flops 369459200 | bytes 7536640 | tf_op jit(solution)/shard_map/esd,ehd->esh/dot_general | solution.py:247
  28.6 1.7 %convolution_convert_fusion.1 = bf16[16,64,352]{2,1,0:T(8,128)(2,1)S(1)} fusion(bf16[16,64,512]{2,1,0:T(8,128)(2,1)S(1)} %get-tuple-element.77.placed, bf16[16,512,352]{1,2,0:T(8,128)(2,1)S(1)} %bitcast.42), kind=kOutput, calls=%fused_computation.1 | convolution fusion | flops 369459200 | bytes 7536640 | tf_op jit(solution)/shard_map/esd,ehd->esh/dot_general | solution.py:247
  30.9 1.7 %collective-permute-start.15 = (bf16[16,16,352]{2,1,0:T(8,128)(2,1)S(1)}, bf16[16,16,352]{2,1,0:T(8,128)(2,1)S(1)}, u32[]{:S(2)}, u32[]{:S(2)}) collective-permute-start(bf16[16,16,352]{2,1,0:T(8,128)(2,1)S(1)} %add_convert_fusion.2.refs_6_), channel_id=1, source_target_pairs={{0,16},{8,24},{16,0},{24,8},{1,17},{9,25},{17,1},{25,9},{2,18},{10... | collective-permute-start | bytes 540680 | tf_op jit(solution)/shard_map/ppermute | solution.py:19
  33.7 4.3 %collective-permute-done.9.refs_4_ = bf16[4,128,512]{2,1,0:T(8,128)(2,1)S(1)} collective-permute-done((bf16[4,128,512]{2,1,0:T(8,128)(2,1)S(1)}, bf16[4,128,512]{2,1,0:T(8,128)(2,1)S(1)}, u32[]{:S(2)}, u32[]{:S(2)}) %collective-permute-start.9) | collective-permute-done | bytes 524320 | tf_op jit(solution)/shard_map/ppermute | solution.py:19
  39.4 1.7 %convolution_convert_fusion = bf16[16,64,352]{2,1,0:T(8,128)(2,1)S(1)} fusion(bf16[16,64,512]{2,1,0:T(8,128)(2,1)S(1)} %shard_map.86, bf16[16,512,352]{1,2,0:T(8,128)(2,1)S(1)} %bitcast.53), kind=kOutput, calls=%fused_computation | convolution fusion | flops 369459200 | bytes 7536640 | tf_op jit(solution)/shard_map/esd,ehd->esh/dot_general | solution.py:247
  42.7 1.6 %collective-permute-start.17 = (bf16[16,16,352]{2,1,0:T(8,128)(2,1)S(1)}, bf16[16,16,352]{2,1,0:T(8,128)(2,1)S(1)}, u32[]{:S(2)}, u32[]{:S(2)}) collective-permute-start(bf16[16,16,352]{2,1,0:T(8,128)(2,1)S(1)} %add_convert_fusion), channel_id=1, source_target_pairs={{0,16},{8,24},{16,0},{24,8},{1,17},{9,25},{17,1},{25,9},{2,18},{10... | collective-permute-start | bytes 540680 | tf_op jit(solution)/shard_map/ppermute | solution.py:19
  44.4 5.4 %collective-permute-done.17 = bf16[16,16,352]{2,1,0:T(8,128)(2,1)S(1)} collective-permute-done((bf16[16,16,352]{2,1,0:T(8,128)(2,1)S(1)}, bf16[16,16,352]{2,1,0:T(8,128)(2,1)S(1)}, u32[]{:S(2)}, u32[]{:S(2)}) %collective-permute-start.17) | collective-permute-done | bytes 180256 | tf_op jit(solution)/shard_map/ppermute | solution.py:19
  50.5 1.6 %collective-permute-start.20 = (bf16[7,16,704]{2,1,0:T(8,128)(2,1)S(1)}, bf16[7,16,704]{2,1,0:T(8,128)(2,1)S(1)}, u32[]{:S(2)}, u32[]{:S(2)}) collective-permute-start(bf16[7,16,704]{2,1,0:T(8,128)(2,1)S(1)} %fusion.4), channel_id=1, source_target_pairs={{0,16},{8,24},{16,0},{24,8},{1,17},{9,25},{17,1},{25,9},{2,18},{10... | collective-permute-start | bytes 473096 | tf_op jit(solution)/shard_map/ppermute | solution.py:19
  52.7 2.5 %shard_map.87 = (bf16[128,512]{1,0:T(8,128)(2,1)S(1)}, bf16[128,512]{1,0:T(8,128)(2,1)S(1)}, bf16[128,512]{1,0:T(8,128)(2,1)S(1)}, bf16[128,512]{1,0:T(8,128)(2,1)S(1)}, bf16[16,704,512]{2,1,0:T(8,128)(2,1)S(1)}) custom-call(s32[4,8,256]{2,1,0:T(8,128)S(1)} %get-tuple-element.60.refs_5_.refs_0_.refs_1_, ...), custom_call_target="tpu_custom_call" | custom-call | flops 1476395008 | bytes 11534336 | tf_op jit(solution)/shard_map/pallas_call | solution.py:148
  55.2 2.5 %collective-permute-done.20.refs_0_ = bf16[7,16,704]{2,1,0:T(8,128)(2,1)S(1)} collective-permute-done((bf16[7,16,704]{2,1,0:T(8,128)(2,1)S(1)}, bf16[7,16,704]{2,1,0:T(8,128)(2,1)S(1)}, u32[]{:S(2)}, u32[]{:S(2)}) %collective-permute-start.20) | collective-permute-done | bytes 157728 | tf_op jit(solution)/shard_map/ppermute | solution.py:19
  65.2 1.6 %collective-permute-start.25 = (bf16[128,512]{1,0:T(8,128)(2,1)S(1)}, bf16[128,512]{1,0:T(8,128)(2,1)S(1)}, u32[]{:S(2)}, u32[]{:S(2)}) collective-permute-start(bf16[128,512]{1,0:T(8,128)(2,1)S(1)} %get-tuple-element.69), channel_id=1, source_target_pairs={{0,16},{1,24},{2,18},{3,26},{4,20},{5,28},{6,22},{7,30},{8,17},{9,... | collective-permute-start | bytes 393224 | tf_op jit(solution)/shard_map/ppermute | solution.py:295
  68.0 1.9 %collective-permute-start.27 = (bf16[128,512]{1,0:T(8,128)(2,1)S(1)}, bf16[128,512]{1,0:T(8,128)(2,1)S(1)}, u32[]{:S(2)}, u32[]{:S(2)}) collective-permute-start(bf16[128,512]{1,0:T(8,128)(2,1)S(1)} %get-tuple-element.71), channel_id=1, source_target_pairs={{0,24},{1,16},{2,26},{3,18},{4,28},{5,20},{6,30},{7,22},{8,25},{9,... | collective-permute-start | bytes 393224 | tf_op jit(solution)/shard_map/ppermute | solution.py:295
  70.9 2.3 %collective-permute-start.32 = (bf16[128,512]{1,0:T(8,128)(2,1)S(1)}, bf16[128,512]{1,0:T(8,128)(2,1)S(1)}, u32[]{:S(2)}, u32[]{:S(2)}) collective-permute-start(bf16[128,512]{1,0:T(8,128)(2,1)S(1)} %broadcast_select_fusion), channel_id=1, source_target_pairs={{0,1},{1,0},{2,3},{3,2},{4,5},{5,4},{6,7},{7,6},{8,9},{9,8},{10,11... | collective-permute-start | bytes 393224 | tf_op jit(solution)/shard_map/ppermute | solution.py:19
  73.2 5.8 %shard_map.90 = (bf16[16,352,512]{2,1,0:T(8,128)(2,1)}, bf16[16,352,512]{2,1,0:T(8,128)(2,1)}) custom-call(bf16[16,64,512]{2,1,0:T(8,128)(2,1)S(1)} %get-tuple-element.77.placed, bf16[16,16,704]{2,1,0:T(8,128)(2,1)S(1)} %pad_maximum_fusion.1.refs_1_.h0, bf16[16,16,704]{2,1,0:T(8,128)(2,1)S(1)} %collective-permute-done.21.refs_2_.h1, ...), custom_call_target="tpu_custom_call" | custom-call | flops 2952790016 | bytes 11534336 | tf_op jit(solution)/shard_map/pallas_call | solution.py:179
  79.3 2.7 %collective-permute-start.33 = (bf16[128,512]{1,0:T(8,128)(2,1)S(1)}, bf16[128,512]{1,0:T(8,128)(2,1)S(1)}, u32[]{:S(2)}, u32[]{:S(2)}) collective-permute-start(bf16[128,512]{1,0:T(8,128)(2,1)S(1)} %select_convert_fusion), channel_id=1, source_target_pairs={{0,2},{1,3},{2,0},{3,1},{4,6},{5,7},{6,4},{7,5},{8,10},{9,11},{10,... | collective-permute-start | bytes 393224 | tf_op jit(solution)/shard_map/ppermute | solution.py:19
  81.9 7.0 %collective-permute-done.33 = bf16[128,512]{1,0:T(8,128)(2,1)S(1)} collective-permute-done((bf16[128,512]{1,0:T(8,128)(2,1)S(1)}, bf16[128,512]{1,0:T(8,128)(2,1)S(1)}, u32[]{:S(2)}, u32[]{:S(2)}) %collective-permute-start.33) | collective-permute-done | bytes 131104 | tf_op jit(solution)/shard_map/ppermute | solution.py:19
  (90 shorter events, 25.8 us)
Async XLA Ops:
  3.3 7.7 %collective-permute-start = (bf16[144,512]{1,0:T(8,128)(2,1)S(1)}, bf16[144,512]{1,0:T(8,128)(2,1)S(1)}, u32[]{:S(2)}, u32[]{:S(2)}) collective-permute-start(bf16[144,512]{1,0:T(8,128)(2,1)S(1)} %get-tuple-element.104), channel_id=1, source_target_pairs={{0,16},{4,20},{8,24},{12,28},{16,0},{20,4},{24,8},{28,12},{1,17},{... | collective-permute-start | bytes 442376 | tf_op jit(solution)/shard_map/ppermute | solution.py:229
  6.4 6.3 %collective-permute-start.1 = (bf16[144,512]{1,0:T(8,128)(2,1)S(1)}, bf16[144,512]{1,0:T(8,128)(2,1)S(1)}, u32[]{:S(2)}, u32[]{:S(2)}) collective-permute-start(bf16[144,512]{1,0:T(8,128)(2,1)S(1)} %get-tuple-element.103), channel_id=1, source_target_pairs={{0,24},{4,28},{8,16},{12,20},{16,8},{20,12},{24,0},{28,4},{1,25},{... | collective-permute-start | bytes 442376 | tf_op jit(solution)/shard_map/ppermute | solution.py:229
  6.4 8.8 %collective-permute-start.5 = (bf16[144,512]{1,0:T(8,128)(2,1)S(1)}, bf16[144,512]{1,0:T(8,128)(2,1)S(1)}, u32[]{:S(2)}, u32[]{:S(2)}) collective-permute-start(bf16[144,512]{1,0:T(8,128)(2,1)S(1)} %get-tuple-element.105.refs_0_), channel_id=1, source_target_pairs={{0,4},{4,0},{8,12},{12,8},{16,20},{20,16},{24,28},{28,24},{1,5},{5... | collective-permute-start | bytes 442376 | tf_op jit(solution)/shard_map/ppermute | solution.py:229
  7.9 7.3 %collective-permute-start.6 = (bf16[144,512]{1,0:T(8,128)(2,1)S(1)}, bf16[144,512]{1,0:T(8,128)(2,1)S(1)}, u32[]{:S(2)}, u32[]{:S(2)}) collective-permute-start(bf16[144,512]{1,0:T(8,128)(2,1)S(1)} %get-tuple-element.106), channel_id=1, source_target_pairs={{0,12},{4,8},{8,4},{12,0},{16,28},{20,24},{24,20},{28,16},{1,13},{... | collective-permute-start | bytes 442376 | tf_op jit(solution)/shard_map/ppermute | solution.py:229
  12.6 6.0 %collective-permute-start.4 = (bf16[128,512]{1,0:T(8,128)(2,1)S(1)}, bf16[128,512]{1,0:T(8,128)(2,1)S(1)}, u32[]{:S(2)}, u32[]{:S(2)}) collective-permute-start(bf16[128,512]{1,0:T(8,128)(2,1)S(1)} %get-tuple-element.50), channel_id=1, source_target_pairs={{0,24},{4,28},{8,16},{12,20},{16,8},{20,12},{24,0},{28,4},{1,25},{... | collective-permute-start | bytes 393224 | tf_op jit(solution)/shard_map/ppermute | solution.py:229
  14.8 6.9 %collective-permute-start.3 = (bf16[128,512]{1,0:T(8,128)(2,1)S(1)}, bf16[128,512]{1,0:T(8,128)(2,1)S(1)}, u32[]{:S(2)}, u32[]{:S(2)}) collective-permute-start(bf16[128,512]{1,0:T(8,128)(2,1)S(1)} %get-tuple-element.49), channel_id=1, source_target_pairs={{0,16},{4,20},{8,24},{12,28},{16,0},{20,4},{24,8},{28,12},{1,17},{... | collective-permute-start | bytes 393224 | tf_op jit(solution)/shard_map/ppermute | solution.py:229
  15.1 6.6 %collective-permute-start.2 = (bf16[128,512]{1,0:T(8,128)(2,1)S(1)}, bf16[128,512]{1,0:T(8,128)(2,1)S(1)}, u32[]{:S(2)}, u32[]{:S(2)}) collective-permute-start(bf16[128,512]{1,0:T(8,128)(2,1)S(1)} %get-tuple-element.48), channel_id=1, source_target_pairs={{0,8},{4,12},{8,0},{12,4},{16,24},{20,28},{24,16},{28,20},{1,9},{5... | collective-permute-start | bytes 393224 | tf_op jit(solution)/shard_map/ppermute | solution.py:229
  15.1 6.7 %collective-permute-start.7 = (bf16[144,512]{1,0:T(8,128)(2,1)S(1)}, bf16[144,512]{1,0:T(8,128)(2,1)S(1)}, u32[]{:S(2)}, u32[]{:S(2)}) collective-permute-start(bf16[144,512]{1,0:T(8,128)(2,1)S(1)} %collective-permute-done.refs_2_), channel_id=1, source_target_pairs={{0,4},{4,0},{1,5},{5,1},{2,6},{6,2},{3,7},{7,3},{8,12},{12,8},{9,1... | collective-permute-start | bytes 442376 | tf_op jit(solution)/shard_map/ppermute | solution.py:19
  17.1 7.4 %collective-permute-start.8 = (bf16[144,512]{1,0:T(8,128)(2,1)S(1)}, bf16[144,512]{1,0:T(8,128)(2,1)S(1)}, u32[]{:S(2)}, u32[]{:S(2)}) collective-permute-start(bf16[144,512]{1,0:T(8,128)(2,1)S(1)} %collective-permute-done.1.refs_3_), channel_id=1, source_target_pairs={{0,4},{4,0},{1,5},{5,1},{2,6},{6,2},{3,7},{7,3},{8,12},{12,8},{9,1... | collective-permute-start | bytes 442376 | tf_op jit(solution)/shard_map/ppermute | solution.py:19
  18.7 7.6 %collective-permute-start.10 = (bf16[144,512]{1,0:T(8,128)(2,1)S(1)}, bf16[144,512]{1,0:T(8,128)(2,1)S(1)}, u32[]{:S(2)}, u32[]{:S(2)}) collective-permute-start(bf16[144,512]{1,0:T(8,128)(2,1)S(1)} %get-tuple-element.106), channel_id=1, source_target_pairs={{0,8},{4,12},{8,0},{12,4},{16,24},{20,28},{24,16},{28,20},{1,9},{5... | collective-permute-start | bytes 442376 | tf_op jit(solution)/shard_map/ppermute | solution.py:229
  24.5 13.5 %collective-permute-start.9 = (bf16[4,128,512]{2,1,0:T(8,128)(2,1)S(1)}, bf16[4,128,512]{2,1,0:T(8,128)(2,1)S(1)}, u32[]{:S(2)}, u32[]{:S(2)}) collective-permute-start(bf16[4,128,512]{2,1,0:T(8,128)(2,1)S(1)} %pad_maximum_fusion.refs_8_), channel_id=1, source_target_pairs={{0,4},{4,0},{1,5},{5,1},{2,6},{6,2},{3,7},{7,3},{8,12},{12,8},{9,1... | collective-permute-start | bytes 1572872 | tf_op jit(solution)/shard_map/ppermute | solution.py:19
  30.9 10.9 %collective-permute-start.15 = (bf16[16,16,352]{2,1,0:T(8,128)(2,1)S(1)}, bf16[16,16,352]{2,1,0:T(8,128)(2,1)S(1)}, u32[]{:S(2)}, u32[]{:S(2)}) collective-permute-start(bf16[16,16,352]{2,1,0:T(8,128)(2,1)S(1)} %add_convert_fusion.2.refs_6_), channel_id=1, source_target_pairs={{0,16},{8,24},{16,0},{24,8},{1,17},{9,25},{17,1},{25,9},{2,18},{10... | collective-permute-start | bytes 540680 | tf_op jit(solution)/shard_map/ppermute | solution.py:19
  32.7 9.6 %collective-permute-start.16 = (bf16[16,16,352]{2,1,0:T(8,128)(2,1)S(1)}, bf16[16,16,352]{2,1,0:T(8,128)(2,1)S(1)}, u32[]{:S(2)}, u32[]{:S(2)}) collective-permute-start(bf16[16,16,352]{2,1,0:T(8,128)(2,1)S(1)} %add_convert_fusion.1.refs_7_), channel_id=1, source_target_pairs={{0,16},{8,24},{16,0},{24,8},{1,17},{9,25},{17,1},{25,9},{2,18},{10... | collective-permute-start | bytes 540680 | tf_op jit(solution)/shard_map/ppermute | solution.py:19
  41.2 3.1 %collective-permute-start.18 = (bf16[16,16,352]{2,1,0:T(8,128)(2,1)S(1)}, bf16[16,16,352]{2,1,0:T(8,128)(2,1)S(1)}, u32[]{:S(2)}, u32[]{:S(2)}) collective-permute-start(bf16[16,16,352]{2,1,0:T(8,128)(2,1)S(1)} %get-tuple-element.89), channel_id=1, source_target_pairs={{0,8},{8,0},{16,24},{24,16},{1,9},{9,1},{17,25},{25,17},{2,10},{10... | collective-permute-start | bytes 540680 | tf_op jit(solution)/shard_map/ppermute | solution.py:19
  42.7 7.0 %collective-permute-start.17 = (bf16[16,16,352]{2,1,0:T(8,128)(2,1)S(1)}, bf16[16,16,352]{2,1,0:T(8,128)(2,1)S(1)}, u32[]{:S(2)}, u32[]{:S(2)}) collective-permute-start(bf16[16,16,352]{2,1,0:T(8,128)(2,1)S(1)} %add_convert_fusion), channel_id=1, source_target_pairs={{0,16},{8,24},{16,0},{24,8},{1,17},{9,25},{17,1},{25,9},{2,18},{10... | collective-permute-start | bytes 540680 | tf_op jit(solution)/shard_map/ppermute | solution.py:19
  50.5 7.2 %collective-permute-start.20 = (bf16[7,16,704]{2,1,0:T(8,128)(2,1)S(1)}, bf16[7,16,704]{2,1,0:T(8,128)(2,1)S(1)}, u32[]{:S(2)}, u32[]{:S(2)}) collective-permute-start(bf16[7,16,704]{2,1,0:T(8,128)(2,1)S(1)} %fusion.4), channel_id=1, source_target_pairs={{0,16},{8,24},{16,0},{24,8},{1,17},{9,25},{17,1},{25,9},{2,18},{10... | collective-permute-start | bytes 473096 | tf_op jit(solution)/shard_map/ppermute | solution.py:19
  52.2 9.8 %collective-permute-start.23 = (bf16[9,16,704]{2,1,0:T(8,128)(2,1)S(1)}, bf16[9,16,704]{2,1,0:T(8,128)(2,1)S(1)}, u32[]{:S(2)}, u32[]{:S(2)}) collective-permute-start(bf16[9,16,704]{2,1,0:T(8,128)(2,1)S(1)} %fusion.3), channel_id=1, source_target_pairs={{0,16},{8,24},{16,0},{24,8},{1,17},{9,25},{17,1},{25,9},{2,18},{10... | collective-permute-start | bytes 608264 | tf_op jit(solution)/shard_map/ppermute | solution.py:19
  62.1 8.8 %collective-permute-start.31 = (bf16[2,128,512]{2,1,0:T(8,128)(2,1)S(1)}, bf16[2,128,512]{2,1,0:T(8,128)(2,1)S(1)}, u32[]{:S(2)}, u32[]{:S(2)}) collective-permute-start(bf16[2,128,512]{2,1,0:T(8,128)(2,1)S(1)} %pad_maximum_fusion.4), channel_id=1, source_target_pairs={{0,4},{4,0},{1,5},{5,1},{2,6},{6,2},{3,7},{7,3},{8,12},{12,8},{9,1... | collective-permute-start | bytes 786440 | tf_op jit(solution)/shard_map/ppermute | solution.py:19
  65.2 13.8 %collective-permute-start.25 = (bf16[128,512]{1,0:T(8,128)(2,1)S(1)}, bf16[128,512]{1,0:T(8,128)(2,1)S(1)}, u32[]{:S(2)}, u32[]{:S(2)}) collective-permute-start(bf16[128,512]{1,0:T(8,128)(2,1)S(1)} %get-tuple-element.69), channel_id=1, source_target_pairs={{0,16},{1,24},{2,18},{3,26},{4,20},{5,28},{6,22},{7,30},{8,17},{9,... | collective-permute-start | bytes 393224 | tf_op jit(solution)/shard_map/ppermute | solution.py:295
  66.8 12.2 %collective-permute-start.26 = (bf16[128,512]{1,0:T(8,128)(2,1)S(1)}, bf16[128,512]{1,0:T(8,128)(2,1)S(1)}, u32[]{:S(2)}, u32[]{:S(2)}) collective-permute-start(bf16[128,512]{1,0:T(8,128)(2,1)S(1)} %get-tuple-element.70), channel_id=1, source_target_pairs={{0,20},{1,28},{2,22},{3,30},{4,16},{5,24},{6,18},{7,26},{8,21},{9,... | collective-permute-start | bytes 393224 | tf_op jit(solution)/shard_map/ppermute | solution.py:295
  68.0 11.1 %collective-permute-start.27 = (bf16[128,512]{1,0:T(8,128)(2,1)S(1)}, bf16[128,512]{1,0:T(8,128)(2,1)S(1)}, u32[]{:S(2)}, u32[]{:S(2)}) collective-permute-start(bf16[128,512]{1,0:T(8,128)(2,1)S(1)} %get-tuple-element.71), channel_id=1, source_target_pairs={{0,24},{1,16},{2,26},{3,18},{4,28},{5,20},{6,30},{7,22},{8,25},{9,... | collective-permute-start | bytes 393224 | tf_op jit(solution)/shard_map/ppermute | solution.py:295
  69.9 9.2 %collective-permute-start.28 = (bf16[128,512]{1,0:T(8,128)(2,1)S(1)}, bf16[128,512]{1,0:T(8,128)(2,1)S(1)}, u32[]{:S(2)}, u32[]{:S(2)}) collective-permute-start(bf16[128,512]{1,0:T(8,128)(2,1)S(1)} %get-tuple-element.72), channel_id=1, source_target_pairs={{0,28},{1,20},{2,30},{3,22},{4,24},{5,16},{6,26},{7,18},{8,29},{9,... | collective-permute-start | bytes 393224 | tf_op jit(solution)/shard_map/ppermute | solution.py:295
  70.9 8.2 %collective-permute-start.32 = (bf16[128,512]{1,0:T(8,128)(2,1)S(1)}, bf16[128,512]{1,0:T(8,128)(2,1)S(1)}, u32[]{:S(2)}, u32[]{:S(2)}) collective-permute-start(bf16[128,512]{1,0:T(8,128)(2,1)S(1)} %broadcast_select_fusion), channel_id=1, source_target_pairs={{0,1},{1,0},{2,3},{3,2},{4,5},{5,4},{6,7},{7,6},{8,9},{9,8},{10,11... | collective-permute-start | bytes 393224 | tf_op jit(solution)/shard_map/ppermute | solution.py:19
  79.3 9.7 %collective-permute-start.33 = (bf16[128,512]{1,0:T(8,128)(2,1)S(1)}, bf16[128,512]{1,0:T(8,128)(2,1)S(1)}, u32[]{:S(2)}, u32[]{:S(2)}) collective-permute-start(bf16[128,512]{1,0:T(8,128)(2,1)S(1)} %select_convert_fusion), channel_id=1, source_target_pairs={{0,2},{1,3},{2,0},{3,1},{4,6},{5,7},{6,4},{7,5},{8,10},{9,11},{10,... | collective-permute-start | bytes 393224 | tf_op jit(solution)/shard_map/ppermute | solution.py:19
  (16 other events, 53.5 us)

commit v8 on v7

--- a/solution.py
+++ b/solution.py
@@ -236,7 +236,6 @@
     far_tokens = [swap(c, "expert", n_x, 1) for c in far_tokens]
     own_grads = [to_owner(c, rel, 0) for rel, c in enumerate(grads)]
     leaving_grads = jnp.stack(own_grads)
-    far_tokens, leaving_grads = lax.optimization_barrier((far_tokens, leaving_grads))
     other_grads = swap(leaving_grads, "expert", n_x, 1)
     gate_weight, up_weight, down_weight = (
         jnp.swapaxes(weight, 1, 2) for weight in (gate_weight, up_weight, down_weight)

time: 90 us -> 88.3 us (0.981)
  waiting for transfers between devices: 33 us -> 30.4 us
  starting transfers between devices: 32.2 us -> 33.2 us
    ppermute x22, waiting for transfers between devices: 25.9 us -> 24.1 us  [swap(): return lax.ppermute(value, axis, [(i, i ^ bit) for i in range(count)])]
    ppermute x22, starting transfers between devices: 19.1 us -> 20.4 us  [swap(): return lax.ppermute(value, axis, [(i, i ^ bit) for i in range(count)])]
where the time goes in v8:
time: 88.3 us; the launch traced here: 88.1 us
  starting transfers between devices  33.2 us (38%)
  waiting for transfers between devices  30.4 us (34%)
  Pallas kernels  11.6 us (13%)
  matrix products  4.98 us (6%)
  other arithmetic  3.66 us (4%)
  local copies, waits for them, and re-layouts  3.38 us (4%)
  between operations  0.97 us (1%)
    ppermute x22, waiting for transfers between devices, swap(): return lax.ppermute(value, axis, [(i, i ^ bit) for i in range(count)])  24.1 us
    ppermute x22, starting transfers between devices, swap(): return lax.ppermute(value, axis, [(i, i ^ bit) for i in range(count)])  20.4 us
    ppermute x8, starting transfers between devices, to_owner(): return lax.ppermute(value, ('dp', 'expert'), pairs)  7.78 us
    ppermute x8, waiting for transfers between devices, to_owner(): return lax.ppermute(value, ('dp', 'expert'), pairs)  6.24 us
    pallas_call x1, Pallas kernels, weight_grads(): pl.pallas_call(weight_kernel, grid=(local_experts // per_step,), out_shap...  5.75 us
    ppermute x4, starting transfers between devices, to_keeper(): return lax.ppermute(value, ('dp', 'expert', 'tensor'), pairs)  5.02 us
    dot_general x3, matrix products, project(): jnp.einsum('esd,ehd->esh', values, weight, preferred_element_type=F32)  4.98 us
    pallas_call x3, Pallas kernels, back(): pl.pallas_call(functools.partial(back_kernel, low, first, last), out_shap...  4.94 us
  transfers between devices with their start and end apart: 34, of which 15 were waited for; matrix products, arithmetic and copies ran while one was open for 8% of the time, Pallas kernels for 13%

profile of v8, /device:TPU:0, one launch (start us, length us, event | category | flops | bytes accessed | tf_op | source)
XLA Modules:
  0.0 88.1 jit_solution(17895465079324468233)
XLA Ops:
  3.3 3.0 %collective-permute-start = (bf16[144,512]{1,0:T(8,128)(2,1)S(1)}, bf16[144,512]{1,0:T(8,128)(2,1)S(1)}, u32[]{:S(2)}, u32[]{:S(2)}) collective-permute-start(bf16[144,512]{1,0:T(8,128)(2,1)S(1)} %get-tuple-element.98), channel_id=1, source_target_pairs={{0,16},{4,20},{8,24},{12,28},{16,0},{20,4},{24,8},{28,12},{1,17},{... | collective-permute-start | bytes 442376 | tf_op jit(solution)/shard_map/ppermute | solution.py:229
  9.2 1.8 %collective-permute-done.refs_2_ = bf16[144,512]{1,0:T(8,128)(2,1)S(1)} collective-permute-done((bf16[144,512]{1,0:T(8,128)(2,1)S(1)}, bf16[144,512]{1,0:T(8,128)(2,1)S(1)}, u32[]{:S(2)}, u32[]{:S(2)}) %collective-permute-start) | collective-permute-done | bytes 147488 | tf_op jit(solution)/shard_map/ppermute | solution.py:229
  11.0 1.6 %collective-permute-done.1.refs_3_ = bf16[144,512]{1,0:T(8,128)(2,1)S(1)} collective-permute-done((bf16[144,512]{1,0:T(8,128)(2,1)S(1)}, bf16[144,512]{1,0:T(8,128)(2,1)S(1)}, u32[]{:S(2)}, u32[]{:S(2)}) %collective-permute-start.1) | collective-permute-done | bytes 147488 | tf_op jit(solution)/shard_map/ppermute | solution.py:229
  12.6 2.2 %collective-permute-start.4 = (bf16[128,512]{1,0:T(8,128)(2,1)S(1)}, bf16[128,512]{1,0:T(8,128)(2,1)S(1)}, u32[]{:S(2)}, u32[]{:S(2)}) collective-permute-start(bf16[128,512]{1,0:T(8,128)(2,1)S(1)} %get-tuple-element.47), channel_id=1, source_target_pairs={{0,24},{4,28},{8,16},{12,20},{16,8},{20,12},{24,0},{28,4},{1,25},{... | collective-permute-start | bytes 393224 | tf_op jit(solution)/shard_map/ppermute | solution.py:229
  15.6 1.7 %collective-permute-start.9 = (bf16[144,512]{1,0:T(8,128)(2,1)S(1)}, bf16[144,512]{1,0:T(8,128)(2,1)S(1)}, u32[]{:S(2)}, u32[]{:S(2)}) collective-permute-start(bf16[144,512]{1,0:T(8,128)(2,1)S(1)} %collective-permute-done.refs_2_), channel_id=1, source_target_pairs={{0,4},{4,0},{1,5},{5,1},{2,6},{6,2},{3,7},{7,3},{8,12},{12,8},{9,1... | collective-permute-start | bytes 442376 | tf_op jit(solution)/shard_map/ppermute | solution.py:19
  18.7 1.5 %collective-permute-start.10 = (bf16[144,512]{1,0:T(8,128)(2,1)S(1)}, bf16[144,512]{1,0:T(8,128)(2,1)S(1)}, u32[]{:S(2)}, u32[]{:S(2)}) collective-permute-start(bf16[144,512]{1,0:T(8,128)(2,1)S(1)} %collective-permute-done.1.refs_3_), channel_id=1, source_target_pairs={{0,4},{4,0},{1,5},{5,1},{2,6},{6,2},{3,7},{7,3},{8,12},{12,8},{9,1... | collective-permute-start | bytes 442376 | tf_op jit(solution)/shard_map/ppermute | solution.py:19
  20.2 1.5 %collective-permute-done.3.refs_2_ = bf16[128,512]{1,0:T(8,128)(2,1)S(1)} collective-permute-done((bf16[128,512]{1,0:T(8,128)(2,1)S(1)}, bf16[128,512]{1,0:T(8,128)(2,1)S(1)}, u32[]{:S(2)}, u32[]{:S(2)}) %collective-permute-start.3) | collective-permute-done | bytes 131104 | tf_op jit(solution)/shard_map/ppermute | solution.py:229
  21.8 1.6 %collective-permute-start.5 = (bf16[4,128,512]{2,1,0:T(8,128)(2,1)S(1)}, bf16[4,128,512]{2,1,0:T(8,128)(2,1)S(1)}, u32[]{:S(2)}, u32[]{:S(2)}) collective-permute-start(bf16[4,128,512]{2,1,0:T(8,128)(2,1)S(1)} %pad_maximum_fusion.refs_8_), channel_id=1, source_target_pairs={{0,4},{4,0},{1,5},{5,1},{2,6},{6,2},{3,7},{7,3},{8,12},{12,8},{9,1... | collective-permute-start | bytes 1572872 | tf_op jit(solution)/shard_map/ppermute | solution.py:19
  23.4 2.0 %collective-permute-done.10.refs_7_ = bf16[144,512]{1,0:T(8,128)(2,1)S(1)} collective-permute-done((bf16[144,512]{1,0:T(8,128)(2,1)S(1)}, bf16[144,512]{1,0:T(8,128)(2,1)S(1)}, u32[]{:S(2)}, u32[]{:S(2)}) %collective-permute-start.10) | collective-permute-done | bytes 147488 | tf_op jit(solution)/shard_map/ppermute | solution.py:19
  25.9 1.7 %convolution_convert_fusion.2 = bf16[16,64,352]{2,1,0:T(8,128)(2,1)S(1)} fusion(bf16[16,64,512]{2,1,0:T(8,128)(2,1)S(1)} %get-tuple-element.71.placed, bf16[16,512,352]{1,2,0:T(8,128)(2,1)S(1)} %bitcast.45), kind=kOutput, calls=%fused_computation.2 | convolution fusion | flops 369459200 | bytes 7536640 | tf_op jit(solution)/shard_map/esd,ehd->esh/dot_general | solution.py:246
  27.7 1.7 %convolution_convert_fusion.1 = bf16[16,64,352]{2,1,0:T(8,128)(2,1)S(1)} fusion(bf16[16,64,512]{2,1,0:T(8,128)(2,1)S(1)} %get-tuple-element.71.placed, bf16[16,512,352]{1,2,0:T(8,128)(2,1)S(1)} %bitcast.42), kind=kOutput, calls=%fused_computation.1 | convolution fusion | flops 369459200 | bytes 7536640 | tf_op jit(solution)/shard_map/esd,ehd->esh/dot_general | solution.py:246
  32.3 4.2 %collective-permute-done.5.refs_4_ = bf16[4,128,512]{2,1,0:T(8,128)(2,1)S(1)} collective-permute-done((bf16[4,128,512]{2,1,0:T(8,128)(2,1)S(1)}, bf16[4,128,512]{2,1,0:T(8,128)(2,1)S(1)}, u32[]{:S(2)}, u32[]{:S(2)}) %collective-permute-start.5) | collective-permute-done | bytes 524320 | tf_op jit(solution)/shard_map/ppermute | solution.py:19
  37.9 1.7 %convolution_convert_fusion = bf16[16,64,352]{2,1,0:T(8,128)(2,1)S(1)} fusion(bf16[16,64,512]{2,1,0:T(8,128)(2,1)S(1)} %shard_map.86, bf16[16,512,352]{1,2,0:T(8,128)(2,1)S(1)} %bitcast.53), kind=kOutput, calls=%fused_computation | convolution fusion | flops 369459200 | bytes 7536640 | tf_op jit(solution)/shard_map/esd,ehd->esh/dot_general | solution.py:246
  42.5 5.7 %collective-permute-done.17 = bf16[16,16,352]{2,1,0:T(8,128)(2,1)S(1)} collective-permute-done((bf16[16,16,352]{2,1,0:T(8,128)(2,1)S(1)}, bf16[16,16,352]{2,1,0:T(8,128)(2,1)S(1)}, u32[]{:S(2)}, u32[]{:S(2)}) %collective-permute-start.17) | collective-permute-done | bytes 180256 | tf_op jit(solution)/shard_map/ppermute | solution.py:19
  51.2 2.5 %shard_map.87 = (bf16[128,512]{1,0:T(8,128)(2,1)S(1)}, bf16[128,512]{1,0:T(8,128)(2,1)S(1)}, bf16[128,512]{1,0:T(8,128)(2,1)S(1)}, bf16[128,512]{1,0:T(8,128)(2,1)S(1)}, bf16[16,704,512]{2,1,0:T(8,128)(2,1)S(1)}) custom-call(s32[4,8,256]{2,1,0:T(8,128)S(1)} %get-tuple-element.54.refs_5_.refs_0_.refs_1_, ...), custom_call_target="tpu_custom_call" | custom-call | flops 1476395008 | bytes 11534336 | tf_op jit(solution)/shard_map/pallas_call | solution.py:148
  53.7 2.5 %collective-permute-done.20.refs_0_ = bf16[7,16,704]{2,1,0:T(8,128)(2,1)S(1)} collective-permute-done((bf16[7,16,704]{2,1,0:T(8,128)(2,1)S(1)}, bf16[7,16,704]{2,1,0:T(8,128)(2,1)S(1)}, u32[]{:S(2)}, u32[]{:S(2)}) %collective-permute-start.20) | collective-permute-done | bytes 157728 | tf_op jit(solution)/shard_map/ppermute | solution.py:19
  59.0 1.5 %collective-permute-done.23.refs_2_ = bf16[9,16,704]{2,1,0:T(8,128)(2,1)S(1)} collective-permute-done((bf16[9,16,704]{2,1,0:T(8,128)(2,1)S(1)}, bf16[9,16,704]{2,1,0:T(8,128)(2,1)S(1)}, u32[]{:S(2)}, u32[]{:S(2)}) %collective-permute-start.23) | collective-permute-done | bytes 202784 | tf_op jit(solution)/shard_map/ppermute | solution.py:19
  60.5 1.7 %collective-permute-start.31 = (bf16[2,128,512]{2,1,0:T(8,128)(2,1)S(1)}, bf16[2,128,512]{2,1,0:T(8,128)(2,1)S(1)}, u32[]{:S(2)}, u32[]{:S(2)}) collective-permute-start(bf16[2,128,512]{2,1,0:T(8,128)(2,1)S(1)} %pad_maximum_fusion.4), channel_id=1, source_target_pairs={{0,4},{4,0},{1,5},{5,1},{2,6},{6,2},{3,7},{7,3},{8,12},{12,8},{9,1... | collective-permute-start | bytes 786440 | tf_op jit(solution)/shard_map/ppermute | solution.py:19
  62.3 1.5 %shard_map.89 = (bf16[128,512]{1,0:T(8,128)(2,1)S(1)}, bf16[128,512]{1,0:T(8,128)(2,1)S(1)}, bf16[128,512]{1,0:T(8,128)(2,1)S(1)}, bf16[128,512]{1,0:T(8,128)(2,1)S(1)}) custom-call(bf16[2,112,512]{2,1,0:T(8,128)(2,1)S(1)} %shard_map.88.refs_0_, s32[4,8,256]{2,1,0:T(8,128)S(1)} %get-tuple-element.54.refs_5_.refs_0_.refs_1_, ...), custom_call_target="tpu_custom_call" | custom-call | flops 830472192 | bytes 6488064 | tf_op jit(solution)/shard_map/pallas_call | solution.py:148
  64.9 1.8 %collective-permute-start.26 = (bf16[128,512]{1,0:T(8,128)(2,1)S(1)}, bf16[128,512]{1,0:T(8,128)(2,1)S(1)}, u32[]{:S(2)}, u32[]{:S(2)}) collective-permute-start(bf16[128,512]{1,0:T(8,128)(2,1)S(1)} %get-tuple-element.64), channel_id=1, source_target_pairs={{0,20},{1,28},{2,22},{3,30},{4,16},{5,24},{6,18},{7,26},{8,21},{9,... | collective-permute-start | bytes 393224 | tf_op jit(solution)/shard_map/ppermute | solution.py:294
  69.4 3.6 %collective-permute-start.32 = (bf16[128,512]{1,0:T(8,128)(2,1)S(1)}, bf16[128,512]{1,0:T(8,128)(2,1)S(1)}, u32[]{:S(2)}, u32[]{:S(2)}) collective-permute-start(bf16[128,512]{1,0:T(8,128)(2,1)S(1)} %broadcast_select_fusion), channel_id=1, source_target_pairs={{0,1},{1,0},{2,3},{3,2},{4,5},{5,4},{6,7},{7,6},{8,9},{9,8},{10,11... | collective-permute-start | bytes 393224 | tf_op jit(solution)/shard_map/ppermute | solution.py:19
  73.0 5.8 %shard_map.90 = (bf16[16,352,512]{2,1,0:T(8,128)(2,1)}, bf16[16,352,512]{2,1,0:T(8,128)(2,1)}) custom-call(bf16[16,64,512]{2,1,0:T(8,128)(2,1)S(1)} %get-tuple-element.71.placed, bf16[16,16,704]{2,1,0:T(8,128)(2,1)S(1)} %pad_maximum_fusion.1.refs_1_.h0, bf16[16,16,704]{2,1,0:T(8,128)(2,1)S(1)} %collective-permute-done.21.refs_2_.h1, ...), custom_call_target="tpu_custom_call" | custom-call | flops 2952790016 | bytes 11534336 | tf_op jit(solution)/shard_map/pallas_call | solution.py:179
  78.9 2.7 %collective-permute-start.33 = (bf16[128,512]{1,0:T(8,128)(2,1)S(1)}, bf16[128,512]{1,0:T(8,128)(2,1)S(1)}, u32[]{:S(2)}, u32[]{:S(2)}) collective-permute-start(bf16[128,512]{1,0:T(8,128)(2,1)S(1)} %select_convert_fusion), channel_id=1, source_target_pairs={{0,2},{1,3},{2,0},{3,1},{4,6},{5,7},{6,4},{7,5},{8,10},{9,11},{10,... | collective-permute-start | bytes 393224 | tf_op jit(solution)/shard_map/ppermute | solution.py:19
  81.6 5.7 %collective-permute-done.33 = bf16[128,512]{1,0:T(8,128)(2,1)S(1)} collective-permute-done((bf16[128,512]{1,0:T(8,128)(2,1)S(1)}, bf16[128,512]{1,0:T(8,128)(2,1)S(1)}, u32[]{:S(2)}, u32[]{:S(2)}) %collective-permute-start.33) | collective-permute-done | bytes 131104 | tf_op jit(solution)/shard_map/ppermute | solution.py:19
  (90 shorter events, 26.2 us)
Async XLA Ops:
  3.3 7.7 %collective-permute-start = (bf16[144,512]{1,0:T(8,128)(2,1)S(1)}, bf16[144,512]{1,0:T(8,128)(2,1)S(1)}, u32[]{:S(2)}, u32[]{:S(2)}) collective-permute-start(bf16[144,512]{1,0:T(8,128)(2,1)S(1)} %get-tuple-element.98), channel_id=1, source_target_pairs={{0,16},{4,20},{8,24},{12,28},{16,0},{20,4},{24,8},{28,12},{1,17},{... | collective-permute-start | bytes 442376 | tf_op jit(solution)/shard_map/ppermute | solution.py:229
  6.4 6.3 %collective-permute-start.1 = (bf16[144,512]{1,0:T(8,128)(2,1)S(1)}, bf16[144,512]{1,0:T(8,128)(2,1)S(1)}, u32[]{:S(2)}, u32[]{:S(2)}) collective-permute-start(bf16[144,512]{1,0:T(8,128)(2,1)S(1)} %get-tuple-element.97), channel_id=1, source_target_pairs={{0,24},{4,28},{8,16},{12,20},{16,8},{20,12},{24,0},{28,4},{1,25},{... | collective-permute-start | bytes 442376 | tf_op jit(solution)/shard_map/ppermute | solution.py:229
  6.4 8.8 %collective-permute-start.7 = (bf16[144,512]{1,0:T(8,128)(2,1)S(1)}, bf16[144,512]{1,0:T(8,128)(2,1)S(1)}, u32[]{:S(2)}, u32[]{:S(2)}) collective-permute-start(bf16[144,512]{1,0:T(8,128)(2,1)S(1)} %get-tuple-element.99.refs_0_), channel_id=1, source_target_pairs={{0,4},{4,0},{8,12},{12,8},{16,20},{20,16},{24,28},{28,24},{1,5},{5... | collective-permute-start | bytes 442376 | tf_op jit(solution)/shard_map/ppermute | solution.py:229
  7.9 7.8 %collective-permute-start.8 = (bf16[144,512]{1,0:T(8,128)(2,1)S(1)}, bf16[144,512]{1,0:T(8,128)(2,1)S(1)}, u32[]{:S(2)}, u32[]{:S(2)}) collective-permute-start(bf16[144,512]{1,0:T(8,128)(2,1)S(1)} %get-tuple-element.100), channel_id=1, source_target_pairs={{0,12},{4,8},{8,4},{12,0},{16,28},{20,24},{24,20},{28,16},{1,13},{... | collective-permute-start | bytes 442376 | tf_op jit(solution)/shard_map/ppermute | solution.py:229
  12.6 6.0 %collective-permute-start.4 = (bf16[128,512]{1,0:T(8,128)(2,1)S(1)}, bf16[128,512]{1,0:T(8,128)(2,1)S(1)}, u32[]{:S(2)}, u32[]{:S(2)}) collective-permute-start(bf16[128,512]{1,0:T(8,128)(2,1)S(1)} %get-tuple-element.47), channel_id=1, source_target_pairs={{0,24},{4,28},{8,16},{12,20},{16,8},{20,12},{24,0},{28,4},{1,25},{... | collective-permute-start | bytes 393224 | tf_op jit(solution)/shard_map/ppermute | solution.py:229
  14.8 6.9 %collective-permute-start.3 = (bf16[128,512]{1,0:T(8,128)(2,1)S(1)}, bf16[128,512]{1,0:T(8,128)(2,1)S(1)}, u32[]{:S(2)}, u32[]{:S(2)}) collective-permute-start(bf16[128,512]{1,0:T(8,128)(2,1)S(1)} %get-tuple-element.46), channel_id=1, source_target_pairs={{0,16},{4,20},{8,24},{12,28},{16,0},{20,4},{24,8},{28,12},{1,17},{... | collective-permute-start | bytes 393224 | tf_op jit(solution)/shard_map/ppermute | solution.py:229
  15.1 6.6 %collective-permute-start.2 = (bf16[128,512]{1,0:T(8,128)(2,1)S(1)}, bf16[128,512]{1,0:T(8,128)(2,1)S(1)}, u32[]{:S(2)}, u32[]{:S(2)}) collective-permute-start(bf16[128,512]{1,0:T(8,128)(2,1)S(1)} %get-tuple-element.45), channel_id=1, source_target_pairs={{0,8},{4,12},{8,0},{12,4},{16,24},{20,28},{24,16},{28,20},{1,9},{5... | collective-permute-start | bytes 393224 | tf_op jit(solution)/shard_map/ppermute | solution.py:229
  15.1 8.2 %collective-permute-start.6 = (bf16[144,512]{1,0:T(8,128)(2,1)S(1)}, bf16[144,512]{1,0:T(8,128)(2,1)S(1)}, u32[]{:S(2)}, u32[]{:S(2)}) collective-permute-start(bf16[144,512]{1,0:T(8,128)(2,1)S(1)} %get-tuple-element.100), channel_id=1, source_target_pairs={{0,8},{4,12},{8,0},{12,4},{16,24},{20,28},{24,16},{28,20},{1,9},{5... | collective-permute-start | bytes 442376 | tf_op jit(solution)/shard_map/ppermute | solution.py:229
  15.6 7.7 %collective-permute-start.9 = (bf16[144,512]{1,0:T(8,128)(2,1)S(1)}, bf16[144,512]{1,0:T(8,128)(2,1)S(1)}, u32[]{:S(2)}, u32[]{:S(2)}) collective-permute-start(bf16[144,512]{1,0:T(8,128)(2,1)S(1)} %collective-permute-done.refs_2_), channel_id=1, source_target_pairs={{0,4},{4,0},{1,5},{5,1},{2,6},{6,2},{3,7},{7,3},{8,12},{12,8},{9,1... | collective-permute-start | bytes 442376 | tf_op jit(solution)/shard_map/ppermute | solution.py:19
  18.7 6.7 %collective-permute-start.10 = (bf16[144,512]{1,0:T(8,128)(2,1)S(1)}, bf16[144,512]{1,0:T(8,128)(2,1)S(1)}, u32[]{:S(2)}, u32[]{:S(2)}) collective-permute-start(bf16[144,512]{1,0:T(8,128)(2,1)S(1)} %collective-permute-done.1.refs_3_), channel_id=1, source_target_pairs={{0,4},{4,0},{1,5},{5,1},{2,6},{6,2},{3,7},{7,3},{8,12},{12,8},{9,1... | collective-permute-start | bytes 442376 | tf_op jit(solution)/shard_map/ppermute | solution.py:19
  21.8 14.7 %collective-permute-start.5 = (bf16[4,128,512]{2,1,0:T(8,128)(2,1)S(1)}, bf16[4,128,512]{2,1,0:T(8,128)(2,1)S(1)}, u32[]{:S(2)}, u32[]{:S(2)}) collective-permute-start(bf16[4,128,512]{2,1,0:T(8,128)(2,1)S(1)} %pad_maximum_fusion.refs_8_), channel_id=1, source_target_pairs={{0,4},{4,0},{1,5},{5,1},{2,6},{6,2},{3,7},{7,3},{8,12},{12,8},{9,1... | collective-permute-start | bytes 1572872 | tf_op jit(solution)/shard_map/ppermute | solution.py:19
  30.0 10.3 %collective-permute-start.15 = (bf16[16,16,352]{2,1,0:T(8,128)(2,1)S(1)}, bf16[16,16,352]{2,1,0:T(8,128)(2,1)S(1)}, u32[]{:S(2)}, u32[]{:S(2)}) collective-permute-start(bf16[16,16,352]{2,1,0:T(8,128)(2,1)S(1)} %add_convert_fusion.2.refs_6_), channel_id=1, source_target_pairs={{0,16},{8,24},{16,0},{24,8},{1,17},{9,25},{17,1},{25,9},{2,18},{10... | collective-permute-start | bytes 540680 | tf_op jit(solution)/shard_map/ppermute | solution.py:19
  31.1 10.1 %collective-permute-start.16 = (bf16[16,16,352]{2,1,0:T(8,128)(2,1)S(1)}, bf16[16,16,352]{2,1,0:T(8,128)(2,1)S(1)}, u32[]{:S(2)}, u32[]{:S(2)}) collective-permute-start(bf16[16,16,352]{2,1,0:T(8,128)(2,1)S(1)} %add_convert_fusion.1.refs_7_), channel_id=1, source_target_pairs={{0,16},{8,24},{16,0},{24,8},{1,17},{9,25},{17,1},{25,9},{2,18},{10... | collective-permute-start | bytes 540680 | tf_op jit(solution)/shard_map/ppermute | solution.py:19
  39.7 2.8 %collective-permute-start.18 = (bf16[16,16,352]{2,1,0:T(8,128)(2,1)S(1)}, bf16[16,16,352]{2,1,0:T(8,128)(2,1)S(1)}, u32[]{:S(2)}, u32[]{:S(2)}) collective-permute-start(bf16[16,16,352]{2,1,0:T(8,128)(2,1)S(1)} %get-tuple-element.83), channel_id=1, source_target_pairs={{0,8},{8,0},{16,24},{24,16},{1,9},{9,1},{17,25},{25,17},{2,10},{10... | collective-permute-start | bytes 540680 | tf_op jit(solution)/shard_map/ppermute | solution.py:19
  41.2 7.0 %collective-permute-start.17 = (bf16[16,16,352]{2,1,0:T(8,128)(2,1)S(1)}, bf16[16,16,352]{2,1,0:T(8,128)(2,1)S(1)}, u32[]{:S(2)}, u32[]{:S(2)}) collective-permute-start(bf16[16,16,352]{2,1,0:T(8,128)(2,1)S(1)} %add_convert_fusion), channel_id=1, source_target_pairs={{0,16},{8,24},{16,0},{24,8},{1,17},{9,25},{17,1},{25,9},{2,18},{10... | collective-permute-start | bytes 540680 | tf_op jit(solution)/shard_map/ppermute | solution.py:19
  48.9 7.2 %collective-permute-start.20 = (bf16[7,16,704]{2,1,0:T(8,128)(2,1)S(1)}, bf16[7,16,704]{2,1,0:T(8,128)(2,1)S(1)}, u32[]{:S(2)}, u32[]{:S(2)}) collective-permute-start(bf16[7,16,704]{2,1,0:T(8,128)(2,1)S(1)} %fusion.4), channel_id=1, source_target_pairs={{0,16},{8,24},{16,0},{24,8},{1,17},{9,25},{17,1},{25,9},{2,18},{10... | collective-permute-start | bytes 473096 | tf_op jit(solution)/shard_map/ppermute | solution.py:19
  50.3 10.2 %collective-permute-start.23 = (bf16[9,16,704]{2,1,0:T(8,128)(2,1)S(1)}, bf16[9,16,704]{2,1,0:T(8,128)(2,1)S(1)}, u32[]{:S(2)}, u32[]{:S(2)}) collective-permute-start(bf16[9,16,704]{2,1,0:T(8,128)(2,1)S(1)} %fusion.3), channel_id=1, source_target_pairs={{0,16},{8,24},{16,0},{24,8},{1,17},{9,25},{17,1},{25,9},{2,18},{10... | collective-permute-start | bytes 608264 | tf_op jit(solution)/shard_map/ppermute | solution.py:19
  60.5 8.8 %collective-permute-start.31 = (bf16[2,128,512]{2,1,0:T(8,128)(2,1)S(1)}, bf16[2,128,512]{2,1,0:T(8,128)(2,1)S(1)}, u32[]{:S(2)}, u32[]{:S(2)}) collective-permute-start(bf16[2,128,512]{2,1,0:T(8,128)(2,1)S(1)} %pad_maximum_fusion.4), channel_id=1, source_target_pairs={{0,4},{4,0},{1,5},{5,1},{2,6},{6,2},{3,7},{7,3},{8,12},{12,8},{9,1... | collective-permute-start | bytes 786440 | tf_op jit(solution)/shard_map/ppermute | solution.py:19
  63.8 14.9 %collective-permute-start.25 = (bf16[128,512]{1,0:T(8,128)(2,1)S(1)}, bf16[128,512]{1,0:T(8,128)(2,1)S(1)}, u32[]{:S(2)}, u32[]{:S(2)}) collective-permute-start(bf16[128,512]{1,0:T(8,128)(2,1)S(1)} %get-tuple-element.63), channel_id=1, source_target_pairs={{0,16},{1,24},{2,18},{3,26},{4,20},{5,28},{6,22},{7,30},{8,17},{9,... | collective-permute-start | bytes 393224 | tf_op jit(solution)/shard_map/ppermute | solution.py:294
  64.9 13.8 %collective-permute-start.26 = (bf16[128,512]{1,0:T(8,128)(2,1)S(1)}, bf16[128,512]{1,0:T(8,128)(2,1)S(1)}, u32[]{:S(2)}, u32[]{:S(2)}) collective-permute-start(bf16[128,512]{1,0:T(8,128)(2,1)S(1)} %get-tuple-element.64), channel_id=1, source_target_pairs={{0,20},{1,28},{2,22},{3,30},{4,16},{5,24},{6,18},{7,26},{8,21},{9,... | collective-permute-start | bytes 393224 | tf_op jit(solution)/shard_map/ppermute | solution.py:294
  66.7 12.1 %collective-permute-start.27 = (bf16[128,512]{1,0:T(8,128)(2,1)S(1)}, bf16[128,512]{1,0:T(8,128)(2,1)S(1)}, u32[]{:S(2)}, u32[]{:S(2)}) collective-permute-start(bf16[128,512]{1,0:T(8,128)(2,1)S(1)} %get-tuple-element.65), channel_id=1, source_target_pairs={{0,24},{1,16},{2,26},{3,18},{4,28},{5,20},{6,30},{7,22},{8,25},{9,... | collective-permute-start | bytes 393224 | tf_op jit(solution)/shard_map/ppermute | solution.py:294
  68.1 10.7 %collective-permute-start.28 = (bf16[128,512]{1,0:T(8,128)(2,1)S(1)}, bf16[128,512]{1,0:T(8,128)(2,1)S(1)}, u32[]{:S(2)}, u32[]{:S(2)}) collective-permute-start(bf16[128,512]{1,0:T(8,128)(2,1)S(1)} %get-tuple-element.66), channel_id=1, source_target_pairs={{0,28},{1,20},{2,30},{3,22},{4,24},{5,16},{6,26},{7,18},{8,29},{9,... | collective-permute-start | bytes 393224 | tf_op jit(solution)/shard_map/ppermute | solution.py:294
  69.4 9.3 %collective-permute-start.32 = (bf16[128,512]{1,0:T(8,128)(2,1)S(1)}, bf16[128,512]{1,0:T(8,128)(2,1)S(1)}, u32[]{:S(2)}, u32[]{:S(2)}) collective-permute-start(bf16[128,512]{1,0:T(8,128)(2,1)S(1)} %broadcast_select_fusion), channel_id=1, source_target_pairs={{0,1},{1,0},{2,3},{3,2},{4,5},{5,4},{6,7},{7,6},{8,9},{9,8},{10,11... | collective-permute-start | bytes 393224 | tf_op jit(solution)/shard_map/ppermute | solution.py:19
  78.9 8.3 %collective-permute-start.33 = (bf16[128,512]{1,0:T(8,128)(2,1)S(1)}, bf16[128,512]{1,0:T(8,128)(2,1)S(1)}, u32[]{:S(2)}, u32[]{:S(2)}) collective-permute-start(bf16[128,512]{1,0:T(8,128)(2,1)S(1)} %select_convert_fusion), channel_id=1, source_target_pairs={{0,2},{1,3},{2,0},{3,1},{4,6},{5,7},{6,4},{7,5},{8,10},{9,11},{10,... | collective-permute-start | bytes 393224 | tf_op jit(solution)/shard_map/ppermute | solution.py:19
  (16 other events, 48.1 us)

commit v9 on v8

--- a/solution.py
+++ b/solution.py
@@ -231,7 +231,7 @@
     own_tokens = [to_owner(c, rel, 0) for rel, c in enumerate(chunks)]
     near_tokens = [to_owner(c, rel, 1) for rel, c in enumerate(chunks[:2])]
     grads = [columns(cotangent, rel) for rel in range(n_dp)]
-    far_tokens, grads = lax.optimization_barrier((own_tokens[2:], grads))
+    far_tokens = own_tokens[2:]
     near_tokens, far_tokens = lax.optimization_barrier((near_tokens, far_tokens))
     far_tokens = [swap(c, "expert", n_x, 1) for c in far_tokens]
     own_grads = [to_owner(c, rel, 0) for rel, c in enumerate(grads)]

time: 88.3 us -> 88 us (level)
  waiting for transfers between devices: 30.4 us -> 28.9 us
  starting transfers between devices: 33.2 us -> 34.4 us
    ppermute x8, waiting for transfers between devices: 6.24 us -> 2.9 us  [to_owner(): return lax.ppermute(value, ('dp', 'expert'), pairs)]
    ppermute x22, waiting for transfers between devices: 24.1 us -> 25.4 us  [swap(): return lax.ppermute(value, axis, [(i, i ^ bit) for i in range(count)])]
    ppermute x8, starting transfers between devices: 7.78 us -> 8.82 us  [to_owner(): return lax.ppermute(value, ('dp', 'expert'), pairs)]
  transfers between devices with their start and end apart: 34 -> 34, of which waited for: 15 -> 16; matrix products, arithmetic and copies ran while one was open for 8% -> 8% of each run, Pallas kernels for 13% -> 13%
where the time goes in v9:
time: 88 us; the launch traced here: 87.8 us
  starting transfers between devices  34.4 us (39%)
  waiting for transfers between devices  28.9 us (33%)
  Pallas kernels  11.6 us (13%)
  matrix products  4.98 us (6%)
  other arithmetic  3.66 us (4%)
  local copies, waits for them, and re-layouts  3.38 us (4%)
  between operations  0.95 us (1%)
    ppermute x22, waiting for transfers between devices, swap(): return lax.ppermute(value, axis, [(i, i ^ bit) for i in range(count)])  25.4 us
    ppermute x22, starting transfers between devices, swap(): return lax.ppermute(value, axis, [(i, i ^ bit) for i in range(count)])  20.4 us
    ppermute x8, starting transfers between devices, to_owner(): return lax.ppermute(value, ('dp', 'expert'), pairs)  8.82 us
    pallas_call x1, Pallas kernels, weight_grads(): pl.pallas_call(weight_kernel, grid=(local_experts // per_step,), out_shap...  5.74 us
    ppermute x4, starting transfers between devices, to_keeper(): return lax.ppermute(value, ('dp', 'expert', 'tensor'), pairs)  5.18 us
    dot_general x3, matrix products, project(): jnp.einsum('esd,ehd->esh', values, weight, preferred_element_type=F32)  4.98 us
    pallas_call x3, Pallas kernels, back(): pl.pallas_call(functools.partial(back_kernel, low, first, last), out_shap...  4.94 us
    ppermute x8, waiting for transfers between devices, to_owner(): return lax.ppermute(value, ('dp', 'expert'), pairs)  2.9 us
  transfers between devices with their start and end apart: 34, of which 16 were waited for; matrix products, arithmetic and copies ran while one was open for 8% of the time, Pallas kernels for 13%

profile of v9, /device:TPU:0, one launch (start us, length us, event | category | flops | bytes accessed | tf_op | source)
XLA Modules:
  0.0 87.8 jit_solution(1237105581738739800)
XLA Ops:
  3.3 3.0 %collective-permute-start.5 = (bf16[144,512]{1,0:T(8,128)(2,1)S(1)}, bf16[144,512]{1,0:T(8,128)(2,1)S(1)}, u32[]{:S(2)}, u32[]{:S(2)}) collective-permute-start(bf16[144,512]{1,0:T(8,128)(2,1)S(1)} %get-tuple-element.88), channel_id=1, source_target_pairs={{0,16},{4,20},{8,24},{12,28},{16,0},{20,4},{24,8},{28,12},{1,17},{... | collective-permute-start | bytes 442376 | tf_op jit(solution)/shard_map/ppermute | solution.py:229
  11.0 2.1 %collective-permute-start.1 = (bf16[128,512]{1,0:T(8,128)(2,1)S(1)}, bf16[128,512]{1,0:T(8,128)(2,1)S(1)}, u32[]{:S(2)}, u32[]{:S(2)}) collective-permute-start(bf16[128,512]{1,0:T(8,128)(2,1)S(1)} %get-tuple-element.80), channel_id=1, source_target_pairs={{0,16},{4,20},{8,24},{12,28},{16,0},{20,4},{24,8},{28,12},{1,17},{... | collective-permute-start | bytes 393224 | tf_op jit(solution)/shard_map/ppermute | solution.py:229
  15.1 2.0 %collective-permute-start.9 = (bf16[144,512]{1,0:T(8,128)(2,1)S(1)}, bf16[144,512]{1,0:T(8,128)(2,1)S(1)}, u32[]{:S(2)}, u32[]{:S(2)}) collective-permute-start(bf16[144,512]{1,0:T(8,128)(2,1)S(1)} %collective-permute-done.5.refs_2_), channel_id=1, source_target_pairs={{0,4},{4,0},{1,5},{5,1},{2,6},{6,2},{3,7},{7,3},{8,12},{12,8},{9,1... | collective-permute-start | bytes 442376 | tf_op jit(solution)/shard_map/ppermute | solution.py:19
  19.1 1.8 %collective-permute-start.3 = (bf16[4,128,512]{2,1,0:T(8,128)(2,1)S(1)}, bf16[4,128,512]{2,1,0:T(8,128)(2,1)S(1)}, u32[]{:S(2)}, u32[]{:S(2)}) collective-permute-start(bf16[4,128,512]{2,1,0:T(8,128)(2,1)S(1)} %pad_maximum_fusion.refs_8_), channel_id=1, source_target_pairs={{0,4},{4,0},{1,5},{5,1},{2,6},{6,2},{3,7},{7,3},{8,12},{12,8},{9,1... | collective-permute-start | bytes 1572872 | tf_op jit(solution)/shard_map/ppermute | solution.py:19
  21.8 3.2 %collective-permute-done.10.refs_7_ = bf16[144,512]{1,0:T(8,128)(2,1)S(1)} collective-permute-done((bf16[144,512]{1,0:T(8,128)(2,1)S(1)}, bf16[144,512]{1,0:T(8,128)(2,1)S(1)}, u32[]{:S(2)}, u32[]{:S(2)}) %collective-permute-start.10) | collective-permute-done | bytes 147488 | tf_op jit(solution)/shard_map/ppermute | solution.py:19
  25.4 1.7 %convolution_convert_fusion.2 = bf16[16,64,352]{2,1,0:T(8,128)(2,1)S(1)} fusion(bf16[16,64,512]{2,1,0:T(8,128)(2,1)S(1)} %get-tuple-element.59.placed, bf16[16,512,352]{1,2,0:T(8,128)(2,1)S(1)} %bitcast.45), kind=kOutput, calls=%fused_computation.2 | convolution fusion | flops 369459200 | bytes 7536640 | tf_op jit(solution)/shard_map/esd,ehd->esh/dot_general | solution.py:246
  27.2 1.7 %convolution_convert_fusion.1 = bf16[16,64,352]{2,1,0:T(8,128)(2,1)S(1)} fusion(bf16[16,64,512]{2,1,0:T(8,128)(2,1)S(1)} %get-tuple-element.59.placed, bf16[16,512,352]{1,2,0:T(8,128)(2,1)S(1)} %bitcast.42), kind=kOutput, calls=%fused_computation.1 | convolution fusion | flops 369459200 | bytes 7536640 | tf_op jit(solution)/shard_map/esd,ehd->esh/dot_general | solution.py:246
  29.6 2.4 %collective-permute-start.15 = (bf16[16,16,352]{2,1,0:T(8,128)(2,1)S(1)}, bf16[16,16,352]{2,1,0:T(8,128)(2,1)S(1)}, u32[]{:S(2)}, u32[]{:S(2)}) collective-permute-start(bf16[16,16,352]{2,1,0:T(8,128)(2,1)S(1)} %add_convert_fusion.2.refs_6_), channel_id=1, source_target_pairs={{0,16},{8,24},{16,0},{24,8},{1,17},{9,25},{17,1},{25,9},{2,18},{10... | collective-permute-start | bytes 540680 | tf_op jit(solution)/shard_map/ppermute | solution.py:19
  33.0 2.6 %collective-permute-done.3.refs_4_ = bf16[4,128,512]{2,1,0:T(8,128)(2,1)S(1)} collective-permute-done((bf16[4,128,512]{2,1,0:T(8,128)(2,1)S(1)}, bf16[4,128,512]{2,1,0:T(8,128)(2,1)S(1)}, u32[]{:S(2)}, u32[]{:S(2)}) %collective-permute-start.3) | collective-permute-done | bytes 524320 | tf_op jit(solution)/shard_map/ppermute | solution.py:19
  37.1 1.7 %convolution_convert_fusion = bf16[16,64,352]{2,1,0:T(8,128)(2,1)S(1)} fusion(bf16[16,64,512]{2,1,0:T(8,128)(2,1)S(1)} %shard_map.86, bf16[16,512,352]{1,2,0:T(8,128)(2,1)S(1)} %bitcast.53), kind=kOutput, calls=%fused_computation | convolution fusion | flops 369459200 | bytes 7536640 | tf_op jit(solution)/shard_map/esd,ehd->esh/dot_general | solution.py:246
  41.3 1.8 %collective-permute-start.17 = (bf16[16,16,352]{2,1,0:T(8,128)(2,1)S(1)}, bf16[16,16,352]{2,1,0:T(8,128)(2,1)S(1)}, u32[]{:S(2)}, u32[]{:S(2)}) collective-permute-start(bf16[16,16,352]{2,1,0:T(8,128)(2,1)S(1)} %add_convert_fusion), channel_id=1, source_target_pairs={{0,16},{8,24},{16,0},{24,8},{1,17},{9,25},{17,1},{25,9},{2,18},{10... | collective-permute-start | bytes 540680 | tf_op jit(solution)/shard_map/ppermute | solution.py:19
  43.1 4.6 %collective-permute-done.17 = bf16[16,16,352]{2,1,0:T(8,128)(2,1)S(1)} collective-permute-done((bf16[16,16,352]{2,1,0:T(8,128)(2,1)S(1)}, bf16[16,16,352]{2,1,0:T(8,128)(2,1)S(1)}, u32[]{:S(2)}, u32[]{:S(2)}) %collective-permute-start.17) | collective-permute-done | bytes 180256 | tf_op jit(solution)/shard_map/ppermute | solution.py:19
  48.4 1.7 %collective-permute-start.20 = (bf16[7,16,704]{2,1,0:T(8,128)(2,1)S(1)}, bf16[7,16,704]{2,1,0:T(8,128)(2,1)S(1)}, u32[]{:S(2)}, u32[]{:S(2)}) collective-permute-start(bf16[7,16,704]{2,1,0:T(8,128)(2,1)S(1)} %fusion.4), channel_id=1, source_target_pairs={{0,16},{8,24},{16,0},{24,8},{1,17},{9,25},{17,1},{25,9},{2,18},{10... | collective-permute-start | bytes 473096 | tf_op jit(solution)/shard_map/ppermute | solution.py:19
  50.7 2.5 %shard_map.87 = (bf16[128,512]{1,0:T(8,128)(2,1)S(1)}, bf16[128,512]{1,0:T(8,128)(2,1)S(1)}, bf16[128,512]{1,0:T(8,128)(2,1)S(1)}, bf16[128,512]{1,0:T(8,128)(2,1)S(1)}, bf16[16,704,512]{2,1,0:T(8,128)(2,1)S(1)}) custom-call(s32[4,8,256]{2,1,0:T(8,128)S(1)} %get-tuple-element.42.refs_5_.refs_0_.refs_1_, ...), custom_call_target="tpu_custom_call" | custom-call | flops 1476395008 | bytes 11534336 | tf_op jit(solution)/shard_map/pallas_call | solution.py:148
  53.2 2.5 %collective-permute-done.20.refs_0_ = bf16[7,16,704]{2,1,0:T(8,128)(2,1)S(1)} collective-permute-done((bf16[7,16,704]{2,1,0:T(8,128)(2,1)S(1)}, bf16[7,16,704]{2,1,0:T(8,128)(2,1)S(1)}, u32[]{:S(2)}, u32[]{:S(2)}) %collective-permute-start.20) | collective-permute-done | bytes 157728 | tf_op jit(solution)/shard_map/ppermute | solution.py:19
  58.5 1.5 %collective-permute-done.23.refs_2_ = bf16[9,16,704]{2,1,0:T(8,128)(2,1)S(1)} collective-permute-done((bf16[9,16,704]{2,1,0:T(8,128)(2,1)S(1)}, bf16[9,16,704]{2,1,0:T(8,128)(2,1)S(1)}, u32[]{:S(2)}, u32[]{:S(2)}) %collective-permute-start.23) | collective-permute-done | bytes 202784 | tf_op jit(solution)/shard_map/ppermute | solution.py:19
  60.0 1.5 %collective-permute-start.31 = (bf16[2,128,512]{2,1,0:T(8,128)(2,1)S(1)}, bf16[2,128,512]{2,1,0:T(8,128)(2,1)S(1)}, u32[]{:S(2)}, u32[]{:S(2)}) collective-permute-start(bf16[2,128,512]{2,1,0:T(8,128)(2,1)S(1)} %pad_maximum_fusion.4), channel_id=1, source_target_pairs={{0,4},{4,0},{1,5},{5,1},{2,6},{6,2},{3,7},{7,3},{8,12},{12,8},{9,1... | collective-permute-start | bytes 786440 | tf_op jit(solution)/shard_map/ppermute | solution.py:19
  61.6 1.5 %shard_map.89 = (bf16[128,512]{1,0:T(8,128)(2,1)S(1)}, bf16[128,512]{1,0:T(8,128)(2,1)S(1)}, bf16[128,512]{1,0:T(8,128)(2,1)S(1)}, bf16[128,512]{1,0:T(8,128)(2,1)S(1)}) custom-call(bf16[2,112,512]{2,1,0:T(8,128)(2,1)S(1)} %shard_map.88.refs_0_, s32[4,8,256]{2,1,0:T(8,128)S(1)} %get-tuple-element.42.refs_5_.refs_0_.refs_1_, ...), custom_call_target="tpu_custom_call" | custom-call | flops 830472192 | bytes 6488064 | tf_op jit(solution)/shard_map/pallas_call | solution.py:148
  63.1 1.8 %collective-permute-start.25 = (bf16[128,512]{1,0:T(8,128)(2,1)S(1)}, bf16[128,512]{1,0:T(8,128)(2,1)S(1)}, u32[]{:S(2)}, u32[]{:S(2)}) collective-permute-start(bf16[128,512]{1,0:T(8,128)(2,1)S(1)} %get-tuple-element.51), channel_id=1, source_target_pairs={{0,16},{1,24},{2,18},{3,26},{4,20},{5,28},{6,22},{7,30},{8,17},{9,... | collective-permute-start | bytes 393224 | tf_op jit(solution)/shard_map/ppermute | solution.py:294
  66.0 2.1 %collective-permute-start.27 = (bf16[128,512]{1,0:T(8,128)(2,1)S(1)}, bf16[128,512]{1,0:T(8,128)(2,1)S(1)}, u32[]{:S(2)}, u32[]{:S(2)}) collective-permute-start(bf16[128,512]{1,0:T(8,128)(2,1)S(1)} %get-tuple-element.53), channel_id=1, source_target_pairs={{0,24},{1,16},{2,26},{3,18},{4,28},{5,20},{6,30},{7,22},{8,25},{9,... | collective-permute-start | bytes 393224 | tf_op jit(solution)/shard_map/ppermute | solution.py:294
  68.9 2.0 %collective-permute-start.32 = (bf16[128,512]{1,0:T(8,128)(2,1)S(1)}, bf16[128,512]{1,0:T(8,128)(2,1)S(1)}, u32[]{:S(2)}, u32[]{:S(2)}) collective-permute-start(bf16[128,512]{1,0:T(8,128)(2,1)S(1)} %broadcast_select_fusion), channel_id=1, source_target_pairs={{0,1},{1,0},{2,3},{3,2},{4,5},{5,4},{6,7},{7,6},{8,9},{9,8},{10,11... | collective-permute-start | bytes 393224 | tf_op jit(solution)/shard_map/ppermute | solution.py:19
  70.9 5.7 %shard_map.90 = (bf16[16,352,512]{2,1,0:T(8,128)(2,1)}, bf16[16,352,512]{2,1,0:T(8,128)(2,1)}) custom-call(bf16[16,64,512]{2,1,0:T(8,128)(2,1)S(1)} %get-tuple-element.59.placed, bf16[16,16,704]{2,1,0:T(8,128)(2,1)S(1)} %pad_maximum_fusion.1.refs_1_.h0, bf16[16,16,704]{2,1,0:T(8,128)(2,1)S(1)} %collective-permute-done.21.refs_2_.h1, ...), custom_call_target="tpu_custom_call" | custom-call | flops 2952790016 | bytes 11534336 | tf_op jit(solution)/shard_map/pallas_call | solution.py:179
  77.4 2.7 %collective-permute-start.33 = (bf16[128,512]{1,0:T(8,128)(2,1)S(1)}, bf16[128,512]{1,0:T(8,128)(2,1)S(1)}, u32[]{:S(2)}, u32[]{:S(2)}) collective-permute-start(bf16[128,512]{1,0:T(8,128)(2,1)S(1)} %select_convert_fusion), channel_id=1, source_target_pairs={{0,2},{1,3},{2,0},{3,1},{4,6},{5,7},{6,4},{7,5},{8,10},{9,11},{10,... | collective-permute-start | bytes 393224 | tf_op jit(solution)/shard_map/ppermute | solution.py:19
  80.1 6.9 %collective-permute-done.33 = bf16[128,512]{1,0:T(8,128)(2,1)S(1)} collective-permute-done((bf16[128,512]{1,0:T(8,128)(2,1)S(1)}, bf16[128,512]{1,0:T(8,128)(2,1)S(1)}, u32[]{:S(2)}, u32[]{:S(2)}) %collective-permute-start.33) | collective-permute-done | bytes 131104 | tf_op jit(solution)/shard_map/ppermute | solution.py:19
  (90 shorter events, 26.0 us)
Async XLA Ops:
  3.3 7.7 %collective-permute-start.5 = (bf16[144,512]{1,0:T(8,128)(2,1)S(1)}, bf16[144,512]{1,0:T(8,128)(2,1)S(1)}, u32[]{:S(2)}, u32[]{:S(2)}) collective-permute-start(bf16[144,512]{1,0:T(8,128)(2,1)S(1)} %get-tuple-element.88), channel_id=1, source_target_pairs={{0,16},{4,20},{8,24},{12,28},{16,0},{20,4},{24,8},{28,12},{1,17},{... | collective-permute-start | bytes 442376 | tf_op jit(solution)/shard_map/ppermute | solution.py:229
  6.4 7.3 %collective-permute-start.6 = (bf16[144,512]{1,0:T(8,128)(2,1)S(1)}, bf16[144,512]{1,0:T(8,128)(2,1)S(1)}, u32[]{:S(2)}, u32[]{:S(2)}) collective-permute-start(bf16[144,512]{1,0:T(8,128)(2,1)S(1)} %get-tuple-element.85), channel_id=1, source_target_pairs={{0,24},{4,28},{8,16},{12,20},{16,8},{20,12},{24,0},{28,4},{1,25},{... | collective-permute-start | bytes 442376 | tf_op jit(solution)/shard_map/ppermute | solution.py:229
  6.4 8.0 %collective-permute-start.7 = (bf16[144,512]{1,0:T(8,128)(2,1)S(1)}, bf16[144,512]{1,0:T(8,128)(2,1)S(1)}, u32[]{:S(2)}, u32[]{:S(2)}) collective-permute-start(bf16[144,512]{1,0:T(8,128)(2,1)S(1)} %get-tuple-element.86.refs_0_), channel_id=1, source_target_pairs={{0,4},{4,0},{8,12},{12,8},{16,20},{20,16},{24,28},{28,24},{1,5},{5... | collective-permute-start | bytes 442376 | tf_op jit(solution)/shard_map/ppermute | solution.py:229
  7.9 7.2 %collective-permute-start.8 = (bf16[144,512]{1,0:T(8,128)(2,1)S(1)}, bf16[144,512]{1,0:T(8,128)(2,1)S(1)}, u32[]{:S(2)}, u32[]{:S(2)}) collective-permute-start(bf16[144,512]{1,0:T(8,128)(2,1)S(1)} %get-tuple-element.87), channel_id=1, source_target_pairs={{0,12},{4,8},{8,4},{12,0},{16,28},{20,24},{24,20},{28,16},{1,13},{... | collective-permute-start | bytes 442376 | tf_op jit(solution)/shard_map/ppermute | solution.py:229
  9.2 7.9 %collective-permute-start.2 = (bf16[128,512]{1,0:T(8,128)(2,1)S(1)}, bf16[128,512]{1,0:T(8,128)(2,1)S(1)}, u32[]{:S(2)}, u32[]{:S(2)}) collective-permute-start(bf16[128,512]{1,0:T(8,128)(2,1)S(1)} %get-tuple-element.79), channel_id=1, source_target_pairs={{0,24},{4,28},{8,16},{12,20},{16,8},{20,12},{24,0},{28,4},{1,25},{... | collective-permute-start | bytes 393224 | tf_op jit(solution)/shard_map/ppermute | solution.py:229
  11.0 7.9 %collective-permute-start.1 = (bf16[128,512]{1,0:T(8,128)(2,1)S(1)}, bf16[128,512]{1,0:T(8,128)(2,1)S(1)}, u32[]{:S(2)}, u32[]{:S(2)}) collective-permute-start(bf16[128,512]{1,0:T(8,128)(2,1)S(1)} %get-tuple-element.80), channel_id=1, source_target_pairs={{0,16},{4,20},{8,24},{12,28},{16,0},{20,4},{24,8},{28,12},{1,17},{... | collective-permute-start | bytes 393224 | tf_op jit(solution)/shard_map/ppermute | solution.py:229
  13.6 5.4 %collective-permute-start = (bf16[128,512]{1,0:T(8,128)(2,1)S(1)}, bf16[128,512]{1,0:T(8,128)(2,1)S(1)}, u32[]{:S(2)}, u32[]{:S(2)}) collective-permute-start(bf16[128,512]{1,0:T(8,128)(2,1)S(1)} %get-tuple-element.78), channel_id=1, source_target_pairs={{0,8},{4,12},{8,0},{12,4},{16,24},{20,28},{24,16},{28,20},{1,9},{5... | collective-permute-start | bytes 393224 | tf_op jit(solution)/shard_map/ppermute | solution.py:229
  14.3 6.6 %collective-permute-start.4 = (bf16[144,512]{1,0:T(8,128)(2,1)S(1)}, bf16[144,512]{1,0:T(8,128)(2,1)S(1)}, u32[]{:S(2)}, u32[]{:S(2)}) collective-permute-start(bf16[144,512]{1,0:T(8,128)(2,1)S(1)} %get-tuple-element.87), channel_id=1, source_target_pairs={{0,8},{4,12},{8,0},{12,4},{16,24},{20,28},{24,16},{28,20},{1,9},{5... | collective-permute-start | bytes 442376 | tf_op jit(solution)/shard_map/ppermute | solution.py:229
  15.1 6.7 %collective-permute-start.9 = (bf16[144,512]{1,0:T(8,128)(2,1)S(1)}, bf16[144,512]{1,0:T(8,128)(2,1)S(1)}, u32[]{:S(2)}, u32[]{:S(2)}) collective-permute-start(bf16[144,512]{1,0:T(8,128)(2,1)S(1)} %collective-permute-done.5.refs_2_), channel_id=1, source_target_pairs={{0,4},{4,0},{1,5},{5,1},{2,6},{6,2},{3,7},{7,3},{8,12},{12,8},{9,1... | collective-permute-start | bytes 442376 | tf_op jit(solution)/shard_map/ppermute | solution.py:19
  17.1 7.8 %collective-permute-start.10 = (bf16[144,512]{1,0:T(8,128)(2,1)S(1)}, bf16[144,512]{1,0:T(8,128)(2,1)S(1)}, u32[]{:S(2)}, u32[]{:S(2)}) collective-permute-start(bf16[144,512]{1,0:T(8,128)(2,1)S(1)} %collective-permute-done.6.refs_3_), channel_id=1, source_target_pairs={{0,4},{4,0},{1,5},{5,1},{2,6},{6,2},{3,7},{7,3},{8,12},{12,8},{9,1... | collective-permute-start | bytes 442376 | tf_op jit(solution)/shard_map/ppermute | solution.py:19
  19.1 16.6 %collective-permute-start.3 = (bf16[4,128,512]{2,1,0:T(8,128)(2,1)S(1)}, bf16[4,128,512]{2,1,0:T(8,128)(2,1)S(1)}, u32[]{:S(2)}, u32[]{:S(2)}) collective-permute-start(bf16[4,128,512]{2,1,0:T(8,128)(2,1)S(1)} %pad_maximum_fusion.refs_8_), channel_id=1, source_target_pairs={{0,4},{4,0},{1,5},{5,1},{2,6},{6,2},{3,7},{7,3},{8,12},{12,8},{9,1... | collective-permute-start | bytes 1572872 | tf_op jit(solution)/shard_map/ppermute | solution.py:19
  29.6 9.9 %collective-permute-start.15 = (bf16[16,16,352]{2,1,0:T(8,128)(2,1)S(1)}, bf16[16,16,352]{2,1,0:T(8,128)(2,1)S(1)}, u32[]{:S(2)}, u32[]{:S(2)}) collective-permute-start(bf16[16,16,352]{2,1,0:T(8,128)(2,1)S(1)} %add_convert_fusion.2.refs_6_), channel_id=1, source_target_pairs={{0,16},{8,24},{16,0},{24,8},{1,17},{9,25},{17,1},{25,9},{2,18},{10... | collective-permute-start | bytes 540680 | tf_op jit(solution)/shard_map/ppermute | solution.py:19
  32.0 9.3 %collective-permute-start.16 = (bf16[16,16,352]{2,1,0:T(8,128)(2,1)S(1)}, bf16[16,16,352]{2,1,0:T(8,128)(2,1)S(1)}, u32[]{:S(2)}, u32[]{:S(2)}) collective-permute-start(bf16[16,16,352]{2,1,0:T(8,128)(2,1)S(1)} %add_convert_fusion.1.refs_7_), channel_id=1, source_target_pairs={{0,16},{8,24},{16,0},{24,8},{1,17},{9,25},{17,1},{25,9},{2,18},{10... | collective-permute-start | bytes 540680 | tf_op jit(solution)/shard_map/ppermute | solution.py:19
  38.9 4.3 %collective-permute-start.18 = (bf16[16,16,352]{2,1,0:T(8,128)(2,1)S(1)}, bf16[16,16,352]{2,1,0:T(8,128)(2,1)S(1)}, u32[]{:S(2)}, u32[]{:S(2)}) collective-permute-start(bf16[16,16,352]{2,1,0:T(8,128)(2,1)S(1)} %get-tuple-element.71), channel_id=1, source_target_pairs={{0,8},{8,0},{16,24},{24,16},{1,9},{9,1},{17,25},{25,17},{2,10},{10... | collective-permute-start | bytes 540680 | tf_op jit(solution)/shard_map/ppermute | solution.py:19
  41.3 6.4 %collective-permute-start.17 = (bf16[16,16,352]{2,1,0:T(8,128)(2,1)S(1)}, bf16[16,16,352]{2,1,0:T(8,128)(2,1)S(1)}, u32[]{:S(2)}, u32[]{:S(2)}) collective-permute-start(bf16[16,16,352]{2,1,0:T(8,128)(2,1)S(1)} %add_convert_fusion), channel_id=1, source_target_pairs={{0,16},{8,24},{16,0},{24,8},{1,17},{9,25},{17,1},{25,9},{2,18},{10... | collective-permute-start | bytes 540680 | tf_op jit(solution)/shard_map/ppermute | solution.py:19
  48.4 7.2 %collective-permute-start.20 = (bf16[7,16,704]{2,1,0:T(8,128)(2,1)S(1)}, bf16[7,16,704]{2,1,0:T(8,128)(2,1)S(1)}, u32[]{:S(2)}, u32[]{:S(2)}) collective-permute-start(bf16[7,16,704]{2,1,0:T(8,128)(2,1)S(1)} %fusion.4), channel_id=1, source_target_pairs={{0,16},{8,24},{16,0},{24,8},{1,17},{9,25},{17,1},{25,9},{2,18},{10... | collective-permute-start | bytes 473096 | tf_op jit(solution)/shard_map/ppermute | solution.py:19
  50.3 9.7 %collective-permute-start.23 = (bf16[9,16,704]{2,1,0:T(8,128)(2,1)S(1)}, bf16[9,16,704]{2,1,0:T(8,128)(2,1)S(1)}, u32[]{:S(2)}, u32[]{:S(2)}) collective-permute-start(bf16[9,16,704]{2,1,0:T(8,128)(2,1)S(1)} %fusion.3), channel_id=1, source_target_pairs={{0,16},{8,24},{16,0},{24,8},{1,17},{9,25},{17,1},{25,9},{2,18},{10... | collective-permute-start | bytes 608264 | tf_op jit(solution)/shard_map/ppermute | solution.py:19
  60.0 8.8 %collective-permute-start.31 = (bf16[2,128,512]{2,1,0:T(8,128)(2,1)S(1)}, bf16[2,128,512]{2,1,0:T(8,128)(2,1)S(1)}, u32[]{:S(2)}, u32[]{:S(2)}) collective-permute-start(bf16[2,128,512]{2,1,0:T(8,128)(2,1)S(1)} %pad_maximum_fusion.4), channel_id=1, source_target_pairs={{0,4},{4,0},{1,5},{5,1},{2,6},{6,2},{3,7},{7,3},{8,12},{12,8},{9,1... | collective-permute-start | bytes 786440 | tf_op jit(solution)/shard_map/ppermute | solution.py:19
  63.1 13.5 %collective-permute-start.25 = (bf16[128,512]{1,0:T(8,128)(2,1)S(1)}, bf16[128,512]{1,0:T(8,128)(2,1)S(1)}, u32[]{:S(2)}, u32[]{:S(2)}) collective-permute-start(bf16[128,512]{1,0:T(8,128)(2,1)S(1)} %get-tuple-element.51), channel_id=1, source_target_pairs={{0,16},{1,24},{2,18},{3,26},{4,20},{5,28},{6,22},{7,30},{8,17},{9,... | collective-permute-start | bytes 393224 | tf_op jit(solution)/shard_map/ppermute | solution.py:294
  64.9 11.7 %collective-permute-start.26 = (bf16[128,512]{1,0:T(8,128)(2,1)S(1)}, bf16[128,512]{1,0:T(8,128)(2,1)S(1)}, u32[]{:S(2)}, u32[]{:S(2)}) collective-permute-start(bf16[128,512]{1,0:T(8,128)(2,1)S(1)} %get-tuple-element.52), channel_id=1, source_target_pairs={{0,20},{1,28},{2,22},{3,30},{4,16},{5,24},{6,18},{7,26},{8,21},{9,... | collective-permute-start | bytes 393224 | tf_op jit(solution)/shard_map/ppermute | solution.py:294
  66.0 11.3 %collective-permute-start.27 = (bf16[128,512]{1,0:T(8,128)(2,1)S(1)}, bf16[128,512]{1,0:T(8,128)(2,1)S(1)}, u32[]{:S(2)}, u32[]{:S(2)}) collective-permute-start(bf16[128,512]{1,0:T(8,128)(2,1)S(1)} %get-tuple-element.53), channel_id=1, source_target_pairs={{0,24},{1,16},{2,26},{3,18},{4,28},{5,20},{6,30},{7,22},{8,25},{9,... | collective-permute-start | bytes 393224 | tf_op jit(solution)/shard_map/ppermute | solution.py:294
  68.1 9.2 %collective-permute-start.28 = (bf16[128,512]{1,0:T(8,128)(2,1)S(1)}, bf16[128,512]{1,0:T(8,128)(2,1)S(1)}, u32[]{:S(2)}, u32[]{:S(2)}) collective-permute-start(bf16[128,512]{1,0:T(8,128)(2,1)S(1)} %get-tuple-element.54), channel_id=1, source_target_pairs={{0,28},{1,20},{2,30},{3,22},{4,24},{5,16},{6,26},{7,18},{8,29},{9,... | collective-permute-start | bytes 393224 | tf_op jit(solution)/shard_map/ppermute | solution.py:294
  68.9 8.4 %collective-permute-start.32 = (bf16[128,512]{1,0:T(8,128)(2,1)S(1)}, bf16[128,512]{1,0:T(8,128)(2,1)S(1)}, u32[]{:S(2)}, u32[]{:S(2)}) collective-permute-start(bf16[128,512]{1,0:T(8,128)(2,1)S(1)} %broadcast_select_fusion), channel_id=1, source_target_pairs={{0,1},{1,0},{2,3},{3,2},{4,5},{5,4},{6,7},{7,6},{8,9},{9,8},{10,11... | collective-permute-start | bytes 393224 | tf_op jit(solution)/shard_map/ppermute | solution.py:19
  77.4 9.6 %collective-permute-start.33 = (bf16[128,512]{1,0:T(8,128)(2,1)S(1)}, bf16[128,512]{1,0:T(8,128)(2,1)S(1)}, u32[]{:S(2)}, u32[]{:S(2)}) collective-permute-start(bf16[128,512]{1,0:T(8,128)(2,1)S(1)} %select_convert_fusion), channel_id=1, source_target_pairs={{0,2},{1,3},{2,0},{3,1},{4,6},{5,7},{6,4},{7,5},{8,10},{9,11},{10,... | collective-permute-start | bytes 393224 | tf_op jit(solution)/shard_map/ppermute | solution.py:19
  (16 other events, 61.8 us)
